TPU v7x, 256 devices: a whole 4x4x8 slice. The times are simulated.
256 devices in a mesh: occ: 32 (over x, z), vir: 8 (over y, core).
Axes of the slice: x: 4, y: 4, z: 8, core: 2. Of those that a mesh axis runs over, the one named last changes fastest.
Arguments:
- t2_amps: float32 [16384, 4096], P('occ', 'vir'), may hold values from -0.046875 to 0.046875
- lambda_amps: float32 [16384, 4096], P('occ', 'vir'), may hold values from -6 to 6
- live_pairs: int32 [32], P('occ'), may hold values from 64 to 512, as said below
- block_sizes: int32 [8], replicated, may hold values from 64 to 2560, as said below
Outputs:
- density: float32 [4096, 4096], P('occ', 'vir')
Inputs may be any that keep to these rules, and one draw needn't show every extreme that they name: Slots 0 to live_pairs[k] - 1 of block k are live; some block has all 512 live. `block_sizes`: the blocks tile the 4096 columns in order and sum to 4096; some block has exactly 64 columns and some exactly 2560.
All inputs are finite; a program needn't handle non-finite values.
Results may differ from a plain program's by a relative error of at most 0.00015.
Values sent between devices are 32-bit elements; how exact they have to be, the bound alone decides.
No kernel may reach another device: no remote copies, remote signals or barrier semaphores. Data moves between devices by JAX's collectives and lax.ppermute only.
A program may use at most 128 MiB of HBM per device.

v0:
```python
import jax
import jax.numpy as jnp
from jax import lax
from jax.sharding import PartitionSpec as P


def irrep_labels(index, sizes):
    ends = jnp.cumsum(sizes)
    return jnp.sum((index[:, None] >= ends[None, :]).astype(jnp.int32), axis=1)


def body(t2_amps, lambda_amps, live_pairs, block_sizes):
    rows = t2_amps.shape[0]
    cols = t2_amps.shape[1]
    step_rows = min(128, rows)
    own_count = live_pairs[0]
    places = jnp.arange(rows, dtype=jnp.int32)
    weights = (places < own_count).astype(jnp.float32)
    first_blk = jnp.zeros((), jnp.int32)
    last_blk = (own_count + step_rows - 1) // step_rows
    weighted_t = t2_amps * weights[:, None]
    full_lambda = lax.all_gather(lambda_amps, "vir", axis=1, tiled=True)
    total_cols = full_lambda.shape[1]
    occ_count = lax.axis_size("occ")
    out_rows = total_cols // occ_count
    col_start = lax.axis_index("vir") * cols
    count = full_lambda.shape[1]

    def add_block(blk_index, total):
        row_start = (blk_index * step_rows).astype(jnp.int32)
        lam_block = lax.dynamic_slice_in_dim(full_lambda, row_start, step_rows, 0)
        amp_block = lax.dynamic_slice_in_dim(weighted_t, row_start, step_rows, 0)
        return total + lax.dot_general(
            lam_block,
            amp_block,
            (((0,), (0,)), ((), ())),
            precision=lax.Precision.HIGHEST,
            preferred_element_type=jnp.float32,
        )

    summed = lax.psum_scatter(
        lax.fori_loop(first_blk, last_blk, add_block, jnp.zeros((count, cols), jnp.float32)),
        "occ",
        scatter_dimension=0,
        tiled=True,
    )
    row_index = lax.axis_index("occ") * out_rows + jnp.arange(out_rows, dtype=jnp.int32)
    col_index = col_start + jnp.arange(cols, dtype=jnp.int32)
    same = (
        irrep_labels(row_index, block_sizes)[:, None]
        == irrep_labels(col_index, block_sizes)[None, :]
    ).astype(jnp.float32)
    return summed * same


def solution(mesh):
    return jax.shard_map(
        body,
        mesh=mesh,
        in_specs=(P("occ", "vir"), P("occ", "vir"), P("occ"), P()),
        out_specs=P("occ", "vir"),
        check_vma=False,
    )
```

profile of v0, /device:TPU:1, one launch (start us, length us, event | category | flops | bytes accessed | tf_op | source)
XLA Modules:
  0.0 350.2 jit_solution(5379238242227870472)
XLA Ops:
  6.5 0.0 all-gather.2.cloned.1.call-start
  6.5 0.7 all-gather.2.cloned.1.call-update
  7.3 0.0 reduce-scatter.2.cloned.1.call-start
  8.0 1.4 broadcast_multiply_fusion
  9.3 56.4 %all-gather.2.cloned.1.call-done = f32[512,4096]{1,0:T(8,128)} async-done(((f32[512,512]{1,0:T(8,128)}), f32[512,4096]{1,0:T(8,128)}) %all-gather.2.cloned.1.call-update) | async-done | bytes 8388624 | tf_op jit(solution)/shard_map/all_gather | solution.py:22
  65.7 4.3 %broadcast_in_dim.2 = f32[4096,512]{1,0:T(8,128)} broadcast(f32[]{:T(128)} %constant.42.clone.1), dimensions={} | broadcast | bytes 8388612 | tf_op jit(solution)/shard_map/broadcast_in_dim | solution.py:42
  70.0 23.6 %while.10 = (s32[]{:T(128)}, f32[4096,512]{1,0:T(8,128)}, s32[]{:T(128)}, f32[512,4096]{1,0:T(8,128)}, f32[512,512]{1,0:T(8,128)S(1)}, /*index=5*/s32[]{:T(128)}, s32[]{:T(128)}, s32[]{:T(128)}, s32[]{:T(128)}) while((s32[]{:T(128)}, f32[4096,512]{1,0:T(8,128)}, s32[]{:T(128)}, f32[512,4096]{1,0:T(8,128)}, f32[512,512]{1,0:T(8,128)S(1)}, ...), condition=%wide.region_4.5_spmd, body=%wide.region_3.4_spmd.sunk | while | flops 3223322624 | bytes 19137676 | solution.py:42
  70.0 11.8 %convolution_add_fusion.2 = f32[4096,512]{1,0:T(8,128)} fusion(f32[4096,512]{1,0:T(8,128)} %get-tuple-element.86, f32[512,4096]{1,0:T(8,128)} %get-tuple-element.97, s32[]{:T(128)S(6)} %select_n.11, f32[512,512]{1,0:T(8,128)S(1)} %get-tuple-element.98), kind=kOutput, calls=%fused_computation.clone.1 | convolution fusion | flops 3223322624 | bytes 19137536 | tf_op jit(solution)/shard_map/while/body/dot_general | solution.py:33
  81.8 11.8 %convolution_add_fusion.2 = f32[4096,512]{1,0:T(8,128)} fusion(f32[4096,512]{1,0:T(8,128)} %get-tuple-element.86, f32[512,4096]{1,0:T(8,128)} %get-tuple-element.97, s32[]{:T(128)S(6)} %select_n.11, f32[512,512]{1,0:T(8,128)S(1)} %get-tuple-element.98), kind=kOutput, calls=%fused_computation.clone.1 | convolution fusion | flops 3223322624 | bytes 19137536 | tf_op jit(solution)/shard_map/while/body/dot_general | solution.py:33
  93.7 0.0 copy-start
  93.7 0.0 reduce-scatter.2.cloned.1.call-update
  93.7 0.6 copy-done
  94.3 0.2 reduce-window.8
  94.5 0.1 convert_reduce_fusion.1
  94.6 0.1 convert_reduce_fusion
  94.7 247.0 %reduce-scatter.2.cloned.1.call-done = f32[128,512]{1,0:T(8,128)} async-done(((f32[4096,512]{1,0:T(8,128)}), f32[128,512]{1,0:T(8,128)}) %reduce-scatter.2.cloned.1.call-update) | async-done | bytes 262160 | tf_op jit(solution)/shard_map/reduce_scatter | solution.py:41
  341.7 1.7 compare_select_fusion
  (3 shorter events, 0.0 us)
Async XLA Ops:
  6.5 59.2 %all-gather.2.cloned.1.call-start = ((), (), s32[]{:S(2)}) async-start(), calls=%async_computation.1 | async-start | bytes 9437184 | tf_op jit(solution)/shard_map/all_gather | solution.py:22
  7.3 334.4 %reduce-scatter.2.cloned.1.call-start = ((), (), s32[]{:S(2)}) async-start(), calls=%async_computation.2 | async-start | bytes 8650752 | tf_op jit(solution)/shard_map/reduce_scatter | solution.py:41
  93.7 0.7 copy-start
Sparse Core Ops, SparseCore 0:
  9.2 56.5 all-gather.1
  93.8 247.7 reduce-scatter.1
where the time goes:
time: 353 us; the launch traced here: 350 us
  waiting for transfers between devices  304 us (86%)
  matrix products  23.6 us (7%)
  between operations  14.1 us (4%)
  local copies, waits for them, and re-layouts  4.91 us (1%)
    reduce_scatter x1, waiting for transfers between devices, body(): lax.psum_scatter(lax.fori_loop(first_blk, last_blk, add_block, jnp.zeros(...  247 us
    all_gather x1, waiting for transfers between devices, body(): full_lambda = lax.all_gather(lambda_amps, 'vir', axis=1, tiled=True)  56.4 us
    dot_general x2, matrix products, add_block(): lax.dot_general(lam_block, amp_block, (((0,), (0,)), ((), ())), precision...  23.6 us
  transfers between devices with their start and end apart: 2, of which 2 were waited for; matrix products, arithmetic and copies ran while one was open for 0% of the time, Pallas kernels for 0%

commit v1 on v0

v1 whole, which is shorter than its diff:
```python
import functools
import jax
import jax.numpy as jnp
from jax import lax
from jax.experimental import pallas as pl
from jax.experimental.pallas import tpu as pltpu
from jax.sharding import Mesh, PartitionSpec as P

NX, NZ, NY, NC = 4, 8, 4, 2
V = 4096
K = 512
W = 512
SUB = 64
STREAMS = (("A", 32), ("A", 32))
ZORDER = (4, 3, -3, 2, -2, 1, -1, 0)


def ring(n, step):
    return [(i, (i + step) % n) for i in range(n)]


def shift(value, axis, n, step):
    return lax.ppermute(value, axis, ring(n, step))


def chunk_kernel(kind, rows, sub, scalars, b0, b1, b2, b3, thi, tlo, lims, out, stage):
    x, z, y, c = scalars[0], scalars[1], scalars[2], scalars[3]
    zz = scalars[4 + pl.program_id(0)]
    lam = jnp.concatenate([b0[0], b1[0], b2[0], b3[0]], axis=0)
    hi = lam.astype(jnp.bfloat16)
    lo = (lam - hi.astype(jnp.float32)).astype(jnp.bfloat16)
    dot = functools.partial(jnp.dot, preferred_element_type=jnp.float32)
    acc = dot(hi, thi[...]) + (dot(lo, thi[...]) + dot(hi, tlo[...]))
    first = lims[0:1, :]
    last = lims[1:2, :]
    place = lax.broadcasted_iota(jnp.int32, (rows, 1), 0)
    for rel in range(NY):
        xp = lax.rem(y + rel, NY)
        row = place + (xp * 1024 + zz * 128 + c * SUB + sub)
        part = acc[rel * rows:(rel + 1) * rows]
        part = jnp.where((row >= first) & (row < last), part, 0.0)
        if kind == "A":
            stage[xp] = part
        else:
            away = lax.rem(xp - x + NX, NX)
            spot = jnp.where(away == 2, 0, jnp.where(away == 0, 3, jnp.where(away == 1, 1, 2)))
            out[spot, 0] = part
    if kind == "A":
        out[0, 0] = stage[0] + stage[3]
        out[0, 1] = stage[1]
        out[0, 2] = stage[2]


def chunks(kind, rows, sub, scalars, blocks, thi, tlo, lims):
    lam_spec = pl.BlockSpec((1, rows, K), lambda k, s: (s[4 + k], 0, 0))
    whole = lambda shape: pl.BlockSpec(shape, lambda k, s: (0, 0))
    if kind == "A":
        shape, block = (NZ, 3, rows, 2 * W), (1, 3, rows, 2 * W)
        out_map = lambda k, s: (k, 0, 0, 0)
    else:
        shape, block = (NX, NZ, rows, 2 * W), (NX, 1, rows, 2 * W)
        out_map = lambda k, s: (0, k, 0, 0)
    return pl.pallas_call(
        functools.partial(chunk_kernel, kind, rows, sub),
        out_shape=jax.ShapeDtypeStruct(shape, jnp.float32),
        grid_spec=pltpu.PrefetchScalarGridSpec(
            num_scalar_prefetch=1,
            grid=(NZ,),
            in_specs=[lam_spec] * 4 + [whole((K, 2 * W))] * 2 + [whole((2, 2 * W))],
            out_specs=pl.BlockSpec(block, out_map),
            scratch_shapes=[pltpu.VMEM((NX, rows, 2 * W), jnp.float32)],
        ),
        compiler_params=pltpu.CompilerParams(vmem_limit_bytes=24 * 1024 * 1024),
        cost_estimate=pl.CostEstimate(
            flops=2 * 3 * NZ * 4 * rows * K * 2 * W,
            bytes_accessed=NZ * 4 * rows * K * 4 + 4 * K * 2 * W + NZ * 4 * rows * 2 * W * 4,
            transcendentals=0,
        ),
    )(scalars, *blocks, thi, tlo, lims)


def add_left(full, left):
    n = left.shape[-1]
    return jnp.concatenate([full[..., :n] + left, full[..., n:]], axis=-1)


def add_right(full, right):
    n = full.shape[-1] - right.shape[-1]
    return jnp.concatenate([full[..., :n], full[..., n:] + right], axis=-1)


def z_phase(part):
    half = part.shape[-1] // 2
    up = shift(part[0][..., :half], "z", NZ, 1)
    down = shift(part[0][..., half:], "z", NZ, -1)
    up = shift(add_left(part[1], up), "z", NZ, 1)
    down = shift(add_right(part[2], down), "z", NZ, -1)
    up = shift(part[3] + up, "z", NZ, 1)
    down = shift(part[4] + down, "z", NZ, -1)
    up = shift(part[5] + up, "z", NZ, 1)
    down = shift(part[6] + down, "z", NZ, -1)
    return part[7] + up + down


def stream_a(part, x):
    got = z_phase(part)
    slot = lambda d: lax.dynamic_index_in_dim(got, lax.rem(lax.rem(x + d, NX), 3), 0, keepdims=False)
    right = shift(slot(1), "x", NX, 1)
    left = shift(slot(3), "x", NX, 3)
    far = shift(slot(2), "x", NX, 2)
    return slot(0) + right + left + far


def stream_b(part):
    half = part.shape[-1] // 2
    up = shift(part[0][..., :half], "x", NX, 1)
    down = shift(part[0][..., half:], "x", NX, -1)
    up = shift(add_left(part[1], up), "x", NX, 1)
    down = shift(add_right(part[2], down), "x", NX, -1)
    return z_phase(part[3] + up + down)


def body(t2_amps, lambda_amps, live_pairs, block_sizes):
    x, z, y, c = (lax.axis_index(name).astype(jnp.int32) for name in "xzyc")
    swap = ring(NC, 1)
    order = [lax.rem(z + (d + NZ), NZ) for d in ZORDER]
    scalars = jnp.stack([x, z, y, c] + order).astype(jnp.int32)

    ends = jnp.cumsum(block_sizes)
    starts = ends - block_sizes
    cols = (y * 2 * W + jnp.arange(2 * W, dtype=jnp.int32))[None, :]
    inside = (cols >= starts[:, None]) & (cols < ends[:, None])
    lims = jnp.stack([
        jnp.sum(jnp.where(inside, starts[:, None], 0), axis=0),
        jnp.sum(jnp.where(inside, ends[:, None], 0), axis=0),
    ]).astype(jnp.int32)

    lam_rows = lambda_amps.T.reshape(4, NC, SUB, K)
    keep = lax.dynamic_index_in_dim(lam_rows, c, 1, keepdims=False)
    give = lax.dynamic_index_in_dim(lam_rows, 1 - c, 1, keepdims=False)
    both = lambda mine, other, axis: jnp.where(
        c == 0, jnp.concatenate([mine, other], axis), jnp.concatenate([other, mine], axis)
    )

    blocks = []
    sub = 0
    for kind, rows in STREAMS:
        mine = keep[:, sub:sub + rows]
        other = lax.ppermute(give[:, sub:sub + rows], "c", swap)
        own = both(mine, other, 0)
        blocks.append((
            own,
            shift(own, "y", NY, -1),
            shift(own, "y", NY, 2),
            shift(own, "y", NY, 1),
        ))
        sub += rows

    t2_pair = both(t2_amps, lax.ppermute(t2_amps, "c", swap), 1)
    live = jnp.arange(K, dtype=jnp.int32)[:, None] < live_pairs[0]
    t2_pair = jnp.where(live, t2_pair, 0.0)
    t2_top = lax.reduce_precision(t2_pair, 8, 7)
    thi = t2_top.astype(jnp.bfloat16)
    tlo = (t2_pair - t2_top).astype(jnp.bfloat16)

    done = []
    sub = 0
    for (kind, rows), block in zip(STREAMS, blocks):
        part = chunks(kind, rows, sub, scalars, block, thi, tlo, lims)
        got = stream_a(part, x) if kind == "A" else stream_b(part)
        row = (x * 1024 + z * 128 + c * SUB + sub + jnp.arange(rows, dtype=jnp.int32))[:, None]
        done.append(jnp.where((row >= lims[0:1]) & (row < lims[1:2]), got, 0.0))
        sub += rows

    rows_all = jnp.concatenate(done, axis=0).reshape(SUB, NC, W)
    mine = lax.dynamic_index_in_dim(rows_all, c, 1, keepdims=False)
    other = lax.ppermute(lax.dynamic_index_in_dim(rows_all, 1 - c, 1, keepdims=False), "c", swap)
    return both(mine, other, 0)


def solution(mesh):
    fine = Mesh(mesh.devices.reshape(NX, NZ, NY, NC), ("x", "z", "y", "c"))
    spec = P(("x", "z"), ("y", "c"))
    return jax.shard_map(
        body,
        mesh=fine,
        in_specs=(spec, spec, P(("x", "z")), P()),
        out_specs=spec,
        check_vma=False,
    )
```

time: 353 us -> 153 us (0.43)
  waiting for transfers between devices: 304 us -> 76.8 us
  starting transfers between devices: 0.04 us -> 43.7 us
  matrix products: 23.6 us -> 0 us
  between operations: 14.1 us -> 1.03 us
  Pallas kernels: 0 us -> 11.2 us
  other arithmetic: 3.46 us -> 9.65 us
  local copies, waits for them, and re-layouts: 4.91 us -> 9.98 us
    reduce_scatter x1 -> x0, waiting for transfers between devices: 247 us -> none  [body(): lax.psum_scatter(lax.fori_loop(first_blk, last_blk, add_block, jnp.zeros(...]
    ppermute x0 -> x32, waiting for transfers between devices: none -> 76.8 us  [the longest x28 75.8 us: shift(): return lax.ppermute(value, axis, ring(n, step))]
    all_gather x1 -> x0, waiting for transfers between devices: 56.4 us -> none  [body(): full_lambda = lax.all_gather(lambda_amps, 'vir', axis=1, tiled=True)]
    ppermute x0 -> x32, starting transfers between devices: none -> 43.7 us  [the longest x28 35.9 us: shift(): return lax.ppermute(value, axis, ring(n, step))]
    dot_general x2 -> x0, matrix products: 23.6 us -> none  [add_block(): lax.dot_general(lam_block, amp_block, (((0,), (0,)), ((), ())), precision...]
    pallas_call x0 -> x2, Pallas kernels: none -> 11.2 us  [chunks(): pl.pallas_call(functools.partial(chunk_kernel, kind, rows, sub), out_shap...]
    unnamed x2 -> x25, local copies, waits for them, and re-layouts: 0.62 us -> 8.22 us
    add x2 -> x12, other arithmetic: 0.01 us -> 5.22 us  [the longest x2 2.47 us: z_phase(): return part[7] + up + down]
  transfers between devices with their start and end apart: 2 -> 32, of which waited for: 2 -> 15; matrix products, arithmetic and copies ran while one was open for 0% -> 6% of each run, Pallas kernels for 0% -> 7%
where the time goes in v1:
time: 153 us; the launch traced here: 152 us
  waiting for transfers between devices  76.8 us (50%)
  starting transfers between devices  43.7 us (29%)
  Pallas kernels  11.2 us (7%)
  local copies, waits for them, and re-layouts  9.98 us (7%)
  other arithmetic  9.65 us (6%)
    ppermute x28, waiting for transfers between devices, shift(): return lax.ppermute(value, axis, ring(n, step))  75.8 us
    ppermute x28, starting transfers between devices, shift(): return lax.ppermute(value, axis, ring(n, step))  35.9 us
    pallas_call x2, Pallas kernels, chunks(): pl.pallas_call(functools.partial(chunk_kernel, kind, rows, sub), out_shap...  11.2 us
    unnamed x25, local copies, waits for them, and re-layouts  8.22 us
    ppermute x1, starting transfers between devices, body(): lax.ppermute(lax.dynamic_index_in_dim(rows_all, 1 - c, 1, keepdims=False)...  4.07 us
    ppermute x2, starting transfers between devices, body(): other = lax.ppermute(give[:, sub:sub + rows], 'c', swap)  3.75 us
  transfers between devices with their start and end apart: 32, of which 15 were waited for; matrix products, arithmetic and copies ran while one was open for 6% of the time, Pallas kernels for 7%

profile of v1, /device:TPU:1, one launch (start us, length us, event | category | flops | bytes accessed | tf_op | source)
XLA Modules:
  0.0 152.4 jit_solution(16604013062980177752)
XLA Ops:
  0.0 1.6 %copy.8 = f32[512,512]{0,1:T(8,128)S(1)} copy(f32[512,512]{1,0:T(8,128)} %param.5) | data formatting | bytes 2097152 | tf_op args[1]
  2.5 3.2 %collective-permute-start.16 = (f32[4,32,512]{2,1,0:T(8,128)S(1)}, f32[4,32,512]{2,1,0:T(8,128)S(1)}, u32[]{:S(2)}, u32[]{:S(2)}) collective-permute-start(f32[4,32,512]{2,1,0:T(8,128)S(1)} %get-tuple-element.24), channel_id=1, source_target_pairs={{0,1},{1,0},{2,3},{3,2},{4,5},{5,4},{6,7},{7,6},{8,9},{9,8},{10,11... | collective-permute-start | bytes 786440 | tf_op jit(solution)/shard_map/ppermute | solution.py:149
  10.7 2.1 %collective-permute-start.1 = (f32[8,32,512]{2,1,0:T(8,128)S(1)}, f32[8,32,512]{2,1,0:T(8,128)S(1)}, u32[]{:S(2)}, u32[]{:S(2)}) collective-permute-start(f32[8,32,512]{2,1,0:T(8,128)S(1)} %maximum_select_fusion.1.b0), channel_id=1, source_target_pairs={{0,6},{2,0},{4,2},{6,4},{1,7},{3,1},{5,3},{7,5},{8,14},{10,8},{12,... | collective-permute-start | bytes 1572872 | tf_op jit(solution)/shard_map/ppermute | solution.py:23
  12.7 1.4 collective-permute-start.2
  14.2 1.9 %fusion = (bf16[512,1024]{1,0:T(8,128)(2,1)S(1)}, bf16[512,1024]{1,0:T(8,128)(2,1)S(1)}) fusion(f32[512,512]{1,0:T(8,128)S(1)} %copy-done.9, f32[512,512]{1,0:T(8,128)} %collective-permute-done.4, pred[512]{0:T(512)(128)(4,1)S(1)} %iota_compare_fusion, pred[]{:T(512)S(6)} %eq.2), kind=kLoop, calls=%fused_computation.2 | loop fusion | flops 4194304 | bytes 4194817 | tf_op jit(solution)/shard_map/convert_element_type | solution.py:164
  16.1 4.5 %collective-permute-done.17.b1 = f32[8,32,512]{2,1,0:T(8,128)S(1)} collective-permute-done((f32[8,32,512]{2,1,0:T(8,128)S(1)}, f32[8,32,512]{2,1,0:T(8,128)S(1)}, u32[]{:S(2)}, u32[]{:S(2)}) %collective-permute-start.17) | collective-permute-done | bytes 524320 | tf_op jit(solution)/shard_map/ppermute | solution.py:23
  21.4 1.4 collective-permute-done.18.b2
  23.6 12.3 %collective-permute-done.19.b3 = f32[8,32,512]{2,1,0:T(8,128)S(1)} collective-permute-done((f32[8,32,512]{2,1,0:T(8,128)S(1)}, f32[8,32,512]{2,1,0:T(8,128)S(1)}, u32[]{:S(2)}, u32[]{:S(2)}) %collective-permute-start.19) | collective-permute-done | bytes 524320 | tf_op jit(solution)/shard_map/ppermute | solution.py:23
  40.9 5.6 %shard_map.47 = f32[8,3,32,1024]{3,2,1,0:T(8,128)S(1)} custom-call(s32[12]{0:T(128)S(1)} %stack.60.scalars, f32[8,32,512]{2,1,0:T(8,128)S(1)} %copy-done.2, f32[8,32,512]{2,1,0:T(8,128)S(1)} %copy-done.4, f32[8,32,512]{2,1,0:T(8,128)S(1)} %copy-done.6, f32[8,32,512]{2,1,0:T(8,128)S(1)} %copy-done.8, bf16[512,1024]{1,0:T(8,128)(2,1)S(1)} %get-tuple-element.18.thi, ...), custom_call_target="tpu_custom_call" | custom-call | flops 3221225472 | bytes 8388608 | tf_op jit(solution)/shard_map/pallas_call | solution.py:63
  46.7 5.6 %collective-permute-start.24 = (f32[3,32,512]{2,1,0:T(8,128)S(1)}, f32[3,32,512]{2,1,0:T(8,128)S(1)}, u32[]{:S(2)}, u32[]{:S(2)}) collective-permute-start(f32[3,32,512]{2,1,0:T(8,128)S(1)} %get-tuple-element.40), channel_id=1, source_target_pairs={{0,56},{8,0},{16,8},{24,16},{32,24},{40,32},{48,40},{56,48},{1,57}... | collective-permute-start | bytes 589832 | tf_op jit(solution)/shard_map/ppermute | solution.py:23
  52.4 5.0 %collective-permute-done.3.b3 = f32[8,32,512]{2,1,0:T(8,128)S(1)} collective-permute-done((f32[8,32,512]{2,1,0:T(8,128)S(1)}, f32[8,32,512]{2,1,0:T(8,128)S(1)}, u32[]{:S(2)}, u32[]{:S(2)}) %collective-permute-start.3) | collective-permute-done | bytes 524320 | tf_op jit(solution)/shard_map/ppermute | solution.py:23
  57.4 5.5 %shard_map.46 = f32[8,3,32,1024]{3,2,1,0:T(8,128)S(1)} custom-call(s32[12]{0:T(128)S(1)} %stack.60.scalars, f32[8,32,512]{2,1,0:T(8,128)S(1)} %maximum_select_fusion.1.b0, f32[8,32,512]{2,1,0:T(8,128)S(1)} %collective-permute-done.1.b1, f32[8,32,512]{2,1,0:T(8,128)S(1)} %collective-permute-done.2.b2, f32[8,32,512]{2,1,0:T(8,128)S(1)} %collective-permute-done.3.b3, ...), custom_call_target="tpu_custom_call" | custom-call | flops 3221225472 | bytes 8388608 | tf_op jit(solution)/shard_map/pallas_call | solution.py:63
  63.1 5.7 %collective-permute-start.9 = (f32[3,32,512]{2,1,0:T(8,128)S(1)}, f32[3,32,512]{2,1,0:T(8,128)S(1)}, u32[]{:S(2)}, u32[]{:S(2)}) collective-permute-start(f32[3,32,512]{2,1,0:T(8,128)S(1)} %get-tuple-element.31), channel_id=1, source_target_pairs={{0,56},{8,0},{16,8},{24,16},{32,24},{40,32},{48,40},{56,48},{1,57}... | collective-permute-start | bytes 589832 | tf_op jit(solution)/shard_map/ppermute | solution.py:23
  69.2 2.7 %collective-permute-start.25 = (f32[3,32,1024]{2,1,0:T(8,128)S(1)}, f32[3,32,1024]{2,1,0:T(8,128)S(1)}, u32[]{:S(2)}, u32[]{:S(2)}) collective-permute-start(f32[3,32,1024]{2,1,0:T(8,128)S(1)} %pad_maximum_fusion.3), channel_id=1, source_target_pairs={{0,56},{8,0},{16,8},{24,16},{32,24},{40,32},{48,40},{56,48},{1,57}... | collective-permute-start | bytes 1179656 | tf_op jit(solution)/shard_map/ppermute | solution.py:23
  72.0 3.6 %collective-permute-done.5 = f32[3,32,512]{2,1,0:T(8,128)S(1)} collective-permute-done((f32[3,32,512]{2,1,0:T(8,128)S(1)}, f32[3,32,512]{2,1,0:T(8,128)S(1)}, u32[]{:S(2)}, u32[]{:S(2)}) %collective-permute-start.5) | collective-permute-done | bytes 196640 | tf_op jit(solution)/shard_map/ppermute | solution.py:23
  75.8 8.3 %collective-permute-done.21 = f32[3,32,1024]{2,1,0:T(8,128)S(1)} collective-permute-done((f32[3,32,1024]{2,1,0:T(8,128)S(1)}, f32[3,32,1024]{2,1,0:T(8,128)S(1)}, u32[]{:S(2)}, u32[]{:S(2)}) %collective-permute-start.21) | collective-permute-done | bytes 393248 | tf_op jit(solution)/shard_map/ppermute | solution.py:23
  84.3 2.7 %collective-permute-start.10 = (f32[3,32,1024]{2,1,0:T(8,128)S(1)}, f32[3,32,1024]{2,1,0:T(8,128)S(1)}, u32[]{:S(2)}, u32[]{:S(2)}) collective-permute-start(f32[3,32,1024]{2,1,0:T(8,128)S(1)} %pad_maximum_fusion.1), channel_id=1, source_target_pairs={{0,56},{8,0},{16,8},{24,16},{32,24},{40,32},{48,40},{56,48},{1,57}... | collective-permute-start | bytes 1179656 | tf_op jit(solution)/shard_map/ppermute | solution.py:23
  87.0 5.5 %collective-permute-done.6 = f32[3,32,1024]{2,1,0:T(8,128)S(1)} collective-permute-done((f32[3,32,1024]{2,1,0:T(8,128)S(1)}, f32[3,32,1024]{2,1,0:T(8,128)S(1)}, u32[]{:S(2)}, u32[]{:S(2)}) %collective-permute-start.6) | collective-permute-done | bytes 393248 | tf_op jit(solution)/shard_map/ppermute | solution.py:23
  92.6 8.3 %collective-permute-done.22 = f32[3,32,1024]{2,1,0:T(8,128)S(1)} collective-permute-done((f32[3,32,1024]{2,1,0:T(8,128)S(1)}, f32[3,32,1024]{2,1,0:T(8,128)S(1)}, u32[]{:S(2)}, u32[]{:S(2)}) %collective-permute-start.22) | collective-permute-done | bytes 393248 | tf_op jit(solution)/shard_map/ppermute | solution.py:23
  101.1 8.2 %collective-permute-done.7 = f32[3,32,1024]{2,1,0:T(8,128)S(1)} collective-permute-done((f32[3,32,1024]{2,1,0:T(8,128)S(1)}, f32[3,32,1024]{2,1,0:T(8,128)S(1)}, u32[]{:S(2)}, u32[]{:S(2)}) %collective-permute-start.7) | collective-permute-done | bytes 393248 | tf_op jit(solution)/shard_map/ppermute | solution.py:23
  110.2 1.5 collective-permute-start.23
  113.9 5.3 %collective-permute-done.11 = f32[3,32,1024]{2,1,0:T(8,128)S(1)} collective-permute-done((f32[3,32,1024]{2,1,0:T(8,128)S(1)}, f32[3,32,1024]{2,1,0:T(8,128)S(1)}, u32[]{:S(2)}, u32[]{:S(2)}) %collective-permute-start.11) | collective-permute-done | bytes 393248 | tf_op jit(solution)/shard_map/ppermute | solution.py:23
  120.0 1.4 collective-permute-start.12
  121.4 6.2 %collective-permute-done.27 = f32[3,32,1024]{2,1,0:T(8,128)} collective-permute-done((f32[3,32,1024]{2,1,0:T(8,128)}, f32[3,32,1024]{2,1,0:T(8,128)}, u32[]{:S(2)}, u32[]{:S(2)}) %collective-permute-start.27) | collective-permute-done | bytes 393248 | tf_op jit(solution)/shard_map/ppermute | solution.py:23
  130.1 1.5 collective-permute-start.29
  131.6 1.5 %collective-permute-start.30 = (f32[32,1024]{1,0:T(8,128)S(1)}, f32[32,1024]{1,0:T(8,128)S(1)}, u32[]{:S(2)}, u32[]{:S(2)}) collective-permute-start(f32[32,1024]{1,0:T(8,128)S(1)} %get-tuple-element.35), channel_id=1, source_target_pairs={{0,128},{64,192},{128,0},{192,64},{1,129},{65,193},{129,1},{193,65... | collective-permute-start | bytes 393224 | tf_op jit(solution)/shard_map/ppermute | solution.py:23
  133.1 2.9 %collective-permute-done.12 = f32[3,32,1024]{2,1,0:T(8,128)} collective-permute-done((f32[3,32,1024]{2,1,0:T(8,128)}, f32[3,32,1024]{2,1,0:T(8,128)}, u32[]{:S(2)}, u32[]{:S(2)}) %collective-permute-start.12) | collective-permute-done | bytes 393248 | tf_op jit(solution)/shard_map/ppermute | solution.py:23
  138.6 1.5 collective-permute-start.14
  140.1 1.5 %collective-permute-start.15 = (f32[32,1024]{1,0:T(8,128)S(1)}, f32[32,1024]{1,0:T(8,128)S(1)}, u32[]{:S(2)}, u32[]{:S(2)}) collective-permute-start(f32[32,1024]{1,0:T(8,128)S(1)} %get-tuple-element.26), channel_id=1, source_target_pairs={{0,128},{64,192},{128,0},{192,64},{1,129},{65,193},{129,1},{193,65... | collective-permute-start | bytes 393224 | tf_op jit(solution)/shard_map/ppermute | solution.py:23
  141.6 2.2 %collective-permute-done.13 = f32[32,1024]{1,0:T(8,128)S(1)} collective-permute-done((f32[32,1024]{1,0:T(8,128)S(1)}, f32[32,1024]{1,0:T(8,128)S(1)}, u32[]{:S(2)}, u32[]{:S(2)}) %collective-permute-start.13) | collective-permute-done | bytes 131104 | tf_op jit(solution)/shard_map/ppermute | solution.py:23
  143.9 2.1 %collective-permute-done.15 = f32[32,1024]{1,0:T(8,128)S(1)} collective-permute-done((f32[32,1024]{1,0:T(8,128)S(1)}, f32[32,1024]{1,0:T(8,128)S(1)}, u32[]{:S(2)}, u32[]{:S(2)}) %collective-permute-start.15) | collective-permute-done | bytes 131104 | tf_op jit(solution)/shard_map/ppermute | solution.py:23
  146.6 4.1 %collective-permute-start.31 = (f32[64,512]{1,0:T(8,128)S(1)}, f32[64,512]{1,0:T(8,128)S(1)}, u32[]{:S(2)}, u32[]{:S(2)}) collective-permute-start(f32[64,512]{1,0:T(8,128)S(1)} %bitcast.118), channel_id=1, source_target_pairs={{0,1},{1,0},{2,3},{3,2},{4,5},{5,4},{6,7},{7,6},{8,9},{9,8},{10,11... | collective-permute-start | bytes 393224 | tf_op jit(solution)/shard_map/ppermute | solution.py:177
  (100 shorter events, 24.4 us)
Async XLA Ops:
  2.5 4.7 %collective-permute-start.16 = (f32[4,32,512]{2,1,0:T(8,128)S(1)}, f32[4,32,512]{2,1,0:T(8,128)S(1)}, u32[]{:S(2)}, u32[]{:S(2)}) collective-permute-start(f32[4,32,512]{2,1,0:T(8,128)S(1)} %get-tuple-element.24), channel_id=1, source_target_pairs={{0,1},{1,0},{2,3},{3,2},{4,5},{5,4},{6,7},{7,6},{8,9},{9,8},{10,11... | collective-permute-start | bytes 786440 | tf_op jit(solution)/shard_map/ppermute | solution.py:149
  5.8 7.0 %collective-permute-start.4 = (f32[512,512]{1,0:T(8,128)S(1)}, f32[512,512]{1,0:T(8,128)}, u32[]{:S(2)}, u32[]{:S(2)}) collective-permute-start(f32[512,512]{1,0:T(8,128)S(1)} %copy-done.9), channel_id=1, source_target_pairs={{0,1},{1,0},{2,3},{3,2},{4,5},{5,4},{6,7},{7,6},{8,9},{9,8},{10,11... | collective-permute-start | bytes 3145736 | tf_op jit(solution)/shard_map/ppermute | solution.py:159
  5.8 3.8 %collective-permute-start = (f32[4,32,512]{2,1,0:T(8,128)}, f32[4,32,512]{2,1,0:T(8,128)}, u32[]{:S(2)}, u32[]{:S(2)}) collective-permute-start(f32[4,32,512]{2,1,0:T(8,128)} %get-tuple-element.23), channel_id=1, source_target_pairs={{0,1},{1,0},{2,3},{3,2},{4,5},{5,4},{6,7},{7,6},{8,9},{9,8},{10,11... | collective-permute-start | bytes 786440 | tf_op jit(solution)/shard_map/ppermute | solution.py:149
  7.3 13.3 %collective-permute-start.17 = (f32[8,32,512]{2,1,0:T(8,128)S(1)}, f32[8,32,512]{2,1,0:T(8,128)S(1)}, u32[]{:S(2)}, u32[]{:S(2)}) collective-permute-start(f32[8,32,512]{2,1,0:T(8,128)S(1)} %maximum_select_fusion.2.b0), channel_id=1, source_target_pairs={{0,6},{2,0},{4,2},{6,4},{1,7},{3,1},{5,3},{7,5},{8,14},{10,8},{12,... | collective-permute-start | bytes 1572872 | tf_op jit(solution)/shard_map/ppermute | solution.py:23
  8.4 14.4 %collective-permute-start.18 = (f32[8,32,512]{2,1,0:T(8,128)S(1)}, f32[8,32,512]{2,1,0:T(8,128)S(1)}, u32[]{:S(2)}, u32[]{:S(2)}) collective-permute-start(f32[8,32,512]{2,1,0:T(8,128)S(1)} %maximum_select_fusion.2.b0), channel_id=1, source_target_pairs={{0,4},{2,6},{4,0},{6,2},{1,5},{3,7},{5,1},{7,3},{8,12},{10,14},{12... | collective-permute-start | bytes 1572872 | tf_op jit(solution)/shard_map/ppermute | solution.py:23
  8.8 27.2 %collective-permute-start.19 = (f32[8,32,512]{2,1,0:T(8,128)S(1)}, f32[8,32,512]{2,1,0:T(8,128)S(1)}, u32[]{:S(2)}, u32[]{:S(2)}) collective-permute-start(f32[8,32,512]{2,1,0:T(8,128)S(1)} %maximum_select_fusion.2.b0), channel_id=1, source_target_pairs={{0,2},{2,4},{4,6},{6,0},{1,3},{3,5},{5,7},{7,1},{8,10},{10,12},{12... | collective-permute-start | bytes 1572872 | tf_op jit(solution)/shard_map/ppermute | solution.py:23
  10.7 41.7 %collective-permute-start.1 = (f32[8,32,512]{2,1,0:T(8,128)S(1)}, f32[8,32,512]{2,1,0:T(8,128)S(1)}, u32[]{:S(2)}, u32[]{:S(2)}) collective-permute-start(f32[8,32,512]{2,1,0:T(8,128)S(1)} %maximum_select_fusion.1.b0), channel_id=1, source_target_pairs={{0,6},{2,0},{4,2},{6,4},{1,7},{3,1},{5,3},{7,5},{8,14},{10,8},{12,... | collective-permute-start | bytes 1572872 | tf_op jit(solution)/shard_map/ppermute | solution.py:23
  12.7 39.6 %collective-permute-start.2 = (f32[8,32,512]{2,1,0:T(8,128)S(1)}, f32[8,32,512]{2,1,0:T(8,128)S(1)}, u32[]{:S(2)}, u32[]{:S(2)}) collective-permute-start(f32[8,32,512]{2,1,0:T(8,128)S(1)} %maximum_select_fusion.1.b0), channel_id=1, source_target_pairs={{0,4},{2,6},{4,0},{6,2},{1,5},{3,7},{5,1},{7,3},{8,12},{10,14},{12... | collective-permute-start | bytes 1572872 | tf_op jit(solution)/shard_map/ppermute | solution.py:23
  21.4 36.0 %collective-permute-start.3 = (f32[8,32,512]{2,1,0:T(8,128)S(1)}, f32[8,32,512]{2,1,0:T(8,128)S(1)}, u32[]{:S(2)}, u32[]{:S(2)}) collective-permute-start(f32[8,32,512]{2,1,0:T(8,128)S(1)} %maximum_select_fusion.1.b0), channel_id=1, source_target_pairs={{0,2},{2,4},{4,6},{6,0},{1,3},{3,5},{5,7},{7,1},{8,10},{10,12},{12... | collective-permute-start | bytes 1572872 | tf_op jit(solution)/shard_map/ppermute | solution.py:23
  46.7 22.4 %collective-permute-start.24 = (f32[3,32,512]{2,1,0:T(8,128)S(1)}, f32[3,32,512]{2,1,0:T(8,128)S(1)}, u32[]{:S(2)}, u32[]{:S(2)}) collective-permute-start(f32[3,32,512]{2,1,0:T(8,128)S(1)} %get-tuple-element.40), channel_id=1, source_target_pairs={{0,56},{8,0},{16,8},{24,16},{32,24},{40,32},{48,40},{56,48},{1,57}... | collective-permute-start | bytes 589832 | tf_op jit(solution)/shard_map/ppermute | solution.py:23
  52.3 16.4 %collective-permute-start.20 = (f32[3,32,512]{2,1,0:T(8,128)S(1)}, f32[3,32,512]{2,1,0:T(8,128)S(1)}, u32[]{:S(2)}, u32[]{:S(2)}) collective-permute-start(f32[3,32,512]{2,1,0:T(8,128)S(1)} %get-tuple-element.39), channel_id=1, source_target_pairs={{0,8},{8,16},{16,24},{24,32},{32,40},{40,48},{48,56},{56,0},{1,9},... | collective-permute-start | bytes 589832 | tf_op jit(solution)/shard_map/ppermute | solution.py:23
  63.1 21.1 %collective-permute-start.9 = (f32[3,32,512]{2,1,0:T(8,128)S(1)}, f32[3,32,512]{2,1,0:T(8,128)S(1)}, u32[]{:S(2)}, u32[]{:S(2)}) collective-permute-start(f32[3,32,512]{2,1,0:T(8,128)S(1)} %get-tuple-element.31), channel_id=1, source_target_pairs={{0,56},{8,0},{16,8},{24,16},{32,24},{40,32},{48,40},{56,48},{1,57}... | collective-permute-start | bytes 589832 | tf_op jit(solution)/shard_map/ppermute | solution.py:23
  68.8 6.8 %collective-permute-start.5 = (f32[3,32,512]{2,1,0:T(8,128)S(1)}, f32[3,32,512]{2,1,0:T(8,128)S(1)}, u32[]{:S(2)}, u32[]{:S(2)}) collective-permute-start(f32[3,32,512]{2,1,0:T(8,128)S(1)} %get-tuple-element.30), channel_id=1, source_target_pairs={{0,8},{8,16},{16,24},{24,32},{32,40},{40,48},{48,56},{56,0},{1,9},... | collective-permute-start | bytes 589832 | tf_op jit(solution)/shard_map/ppermute | solution.py:23
  68.9 15.1 %collective-permute-start.21 = (f32[3,32,1024]{2,1,0:T(8,128)S(1)}, f32[3,32,1024]{2,1,0:T(8,128)S(1)}, u32[]{:S(2)}, u32[]{:S(2)}) collective-permute-start(f32[3,32,1024]{2,1,0:T(8,128)S(1)} %pad_maximum_fusion.2), channel_id=1, source_target_pairs={{0,8},{8,16},{16,24},{24,32},{32,40},{40,48},{48,56},{56,0},{1,9},... | collective-permute-start | bytes 1179656 | tf_op jit(solution)/shard_map/ppermute | solution.py:23
  69.2 23.3 %collective-permute-start.25 = (f32[3,32,1024]{2,1,0:T(8,128)S(1)}, f32[3,32,1024]{2,1,0:T(8,128)S(1)}, u32[]{:S(2)}, u32[]{:S(2)}) collective-permute-start(f32[3,32,1024]{2,1,0:T(8,128)S(1)} %pad_maximum_fusion.3), channel_id=1, source_target_pairs={{0,56},{8,0},{16,8},{24,16},{32,24},{40,32},{48,40},{56,48},{1,57}... | collective-permute-start | bytes 1179656 | tf_op jit(solution)/shard_map/ppermute | solution.py:23
  75.7 16.8 %collective-permute-start.6 = (f32[3,32,1024]{2,1,0:T(8,128)S(1)}, f32[3,32,1024]{2,1,0:T(8,128)S(1)}, u32[]{:S(2)}, u32[]{:S(2)}) collective-permute-start(f32[3,32,1024]{2,1,0:T(8,128)S(1)} %pad_maximum_fusion), channel_id=1, source_target_pairs={{0,8},{8,16},{16,24},{24,32},{32,40},{40,48},{48,56},{56,0},{1,9},... | collective-permute-start | bytes 1179656 | tf_op jit(solution)/shard_map/ppermute | solution.py:23
  84.1 16.8 %collective-permute-start.22 = (f32[3,32,1024]{2,1,0:T(8,128)S(1)}, f32[3,32,1024]{2,1,0:T(8,128)S(1)}, u32[]{:S(2)}, u32[]{:S(2)}) collective-permute-start(f32[3,32,1024]{2,1,0:T(8,128)S(1)} %fusion.4), channel_id=1, source_target_pairs={{0,8},{8,16},{16,24},{24,32},{32,40},{40,48},{48,56},{56,0},{1,9},... | collective-permute-start | bytes 1179656 | tf_op jit(solution)/shard_map/ppermute | solution.py:23
  84.3 16.8 %collective-permute-start.10 = (f32[3,32,1024]{2,1,0:T(8,128)S(1)}, f32[3,32,1024]{2,1,0:T(8,128)S(1)}, u32[]{:S(2)}, u32[]{:S(2)}) collective-permute-start(f32[3,32,1024]{2,1,0:T(8,128)S(1)} %pad_maximum_fusion.1), channel_id=1, source_target_pairs={{0,56},{8,0},{16,8},{24,16},{32,24},{40,32},{48,40},{56,48},{1,57}... | collective-permute-start | bytes 1179656 | tf_op jit(solution)/shard_map/ppermute | solution.py:23
  92.5 16.8 %collective-permute-start.7 = (f32[3,32,1024]{2,1,0:T(8,128)S(1)}, f32[3,32,1024]{2,1,0:T(8,128)S(1)}, u32[]{:S(2)}, u32[]{:S(2)}) collective-permute-start(f32[3,32,1024]{2,1,0:T(8,128)S(1)} %fusion.10), channel_id=1, source_target_pairs={{0,8},{8,16},{16,24},{24,32},{32,40},{40,48},{48,56},{56,0},{1,9},... | collective-permute-start | bytes 1179656 | tf_op jit(solution)/shard_map/ppermute | solution.py:23
  101.0 10.7 %collective-permute-start.26 = (f32[3,32,1024]{2,1,0:T(8,128)S(1)}, f32[3,32,1024]{2,1,0:T(8,128)S(1)}, u32[]{:S(2)}, u32[]{:S(2)}) collective-permute-start(f32[3,32,1024]{2,1,0:T(8,128)S(1)} %get-tuple-element.13), channel_id=1, source_target_pairs={{0,56},{8,0},{16,8},{24,16},{32,24},{40,32},{48,40},{56,48},{1,57}... | collective-permute-start | bytes 1179656 | tf_op jit(solution)/shard_map/ppermute | solution.py:23
  110.2 9.0 %collective-permute-start.11 = (f32[3,32,1024]{2,1,0:T(8,128)S(1)}, f32[3,32,1024]{2,1,0:T(8,128)S(1)}, u32[]{:S(2)}, u32[]{:S(2)}) collective-permute-start(f32[3,32,1024]{2,1,0:T(8,128)S(1)} %get-tuple-element.8), channel_id=1, source_target_pairs={{0,56},{8,0},{16,8},{24,16},{32,24},{40,32},{48,40},{56,48},{1,57}... | collective-permute-start | bytes 1179656 | tf_op jit(solution)/shard_map/ppermute | solution.py:23
  110.2 11.2 %collective-permute-start.23 = (f32[3,32,1024]{2,1,0:T(8,128)S(1)}, f32[3,32,1024]{2,1,0:T(8,128)}, u32[]{:S(2)}, u32[]{:S(2)}) collective-permute-start(f32[3,32,1024]{2,1,0:T(8,128)S(1)} %get-tuple-element.12), channel_id=1, source_target_pairs={{0,8},{8,16},{16,24},{24,32},{32,40},{40,48},{48,56},{56,0},{1,9},... | collective-permute-start | bytes 1179656 | tf_op jit(solution)/shard_map/ppermute | solution.py:23
  112.4 15.2 %collective-permute-start.27 = (f32[3,32,1024]{2,1,0:T(8,128)}, f32[3,32,1024]{2,1,0:T(8,128)}, u32[]{:S(2)}, u32[]{:S(2)}) collective-permute-start(f32[3,32,1024]{2,1,0:T(8,128)} %fusion.3), channel_id=1, source_target_pairs={{0,56},{8,0},{16,8},{24,16},{32,24},{40,32},{48,40},{56,48},{1,57}... | collective-permute-start | bytes 1179656 | tf_op jit(solution)/shard_map/ppermute | solution.py:23
  113.6 19.5 %collective-permute-start.8 = (f32[3,32,1024]{2,1,0:T(8,128)}, f32[3,32,1024]{2,1,0:T(8,128)}, u32[]{:S(2)}, u32[]{:S(2)}) collective-permute-start(f32[3,32,1024]{2,1,0:T(8,128)} %get-tuple-element.7), channel_id=1, source_target_pairs={{0,8},{8,16},{16,24},{24,32},{32,40},{40,48},{48,56},{56,0},{1,9},... | collective-permute-start | bytes 1179656 | tf_op jit(solution)/shard_map/ppermute | solution.py:23
  120.0 16.0 %collective-permute-start.12 = (f32[3,32,1024]{2,1,0:T(8,128)}, f32[3,32,1024]{2,1,0:T(8,128)}, u32[]{:S(2)}, u32[]{:S(2)}) collective-permute-start(f32[3,32,1024]{2,1,0:T(8,128)} %fusion.9), channel_id=1, source_target_pairs={{0,56},{8,0},{16,8},{24,16},{32,24},{40,32},{48,40},{56,48},{1,57}... | collective-permute-start | bytes 1179656 | tf_op jit(solution)/shard_map/ppermute | solution.py:23
  128.8 11.3 %collective-permute-start.28 = (f32[32,1024]{1,0:T(8,128)S(1)}, f32[32,1024]{1,0:T(8,128)S(1)}, u32[]{:S(2)}, u32[]{:S(2)}) collective-permute-start(f32[32,1024]{1,0:T(8,128)S(1)} %get-tuple-element.34), channel_id=1, source_target_pairs={{0,64},{64,128},{128,192},{192,0},{1,65},{65,129},{129,193},{193,1... | collective-permute-start | bytes 393224 | tf_op jit(solution)/shard_map/ppermute | solution.py:23
  130.1 11.5 %collective-permute-start.29 = (f32[32,1024]{1,0:T(8,128)S(1)}, f32[32,1024]{1,0:T(8,128)S(1)}, u32[]{:S(2)}, u32[]{:S(2)}) collective-permute-start(f32[32,1024]{1,0:T(8,128)S(1)} %get-tuple-element.36), channel_id=1, source_target_pairs={{0,192},{64,0},{128,64},{192,128},{1,193},{65,1},{129,65},{193,129... | collective-permute-start | bytes 393224 | tf_op jit(solution)/shard_map/ppermute | solution.py:23
  131.6 10.1 %collective-permute-start.30 = (f32[32,1024]{1,0:T(8,128)S(1)}, f32[32,1024]{1,0:T(8,128)S(1)}, u32[]{:S(2)}, u32[]{:S(2)}) collective-permute-start(f32[32,1024]{1,0:T(8,128)S(1)} %get-tuple-element.35), channel_id=1, source_target_pairs={{0,128},{64,192},{128,0},{192,64},{1,129},{65,193},{129,1},{193,65... | collective-permute-start | bytes 393224 | tf_op jit(solution)/shard_map/ppermute | solution.py:23
  137.3 6.5 %collective-permute-start.13 = (f32[32,1024]{1,0:T(8,128)S(1)}, f32[32,1024]{1,0:T(8,128)S(1)}, u32[]{:S(2)}, u32[]{:S(2)}) collective-permute-start(f32[32,1024]{1,0:T(8,128)S(1)} %get-tuple-element.25), channel_id=1, source_target_pairs={{0,64},{64,128},{128,192},{192,0},{1,65},{65,129},{129,193},{193,1... | collective-permute-start | bytes 393224 | tf_op jit(solution)/shard_map/ppermute | solution.py:23
  138.6 5.2 %collective-permute-start.14 = (f32[32,1024]{1,0:T(8,128)S(1)}, f32[32,1024]{1,0:T(8,128)S(1)}, u32[]{:S(2)}, u32[]{:S(2)}) collective-permute-start(f32[32,1024]{1,0:T(8,128)S(1)} %get-tuple-element.27), channel_id=1, source_target_pairs={{0,192},{64,0},{128,64},{192,128},{1,193},{65,1},{129,65},{193,129... | collective-permute-start | bytes 393224 | tf_op jit(solution)/shard_map/ppermute | solution.py:23
  140.1 5.9 %collective-permute-start.15 = (f32[32,1024]{1,0:T(8,128)S(1)}, f32[32,1024]{1,0:T(8,128)S(1)}, u32[]{:S(2)}, u32[]{:S(2)}) collective-permute-start(f32[32,1024]{1,0:T(8,128)S(1)} %get-tuple-element.26), channel_id=1, source_target_pairs={{0,128},{64,192},{128,0},{192,64},{1,129},{65,193},{129,1},{193,65... | collective-permute-start | bytes 393224 | tf_op jit(solution)/shard_map/ppermute | solution.py:23
  146.6 5.1 %collective-permute-start.31 = (f32[64,512]{1,0:T(8,128)S(1)}, f32[64,512]{1,0:T(8,128)S(1)}, u32[]{:S(2)}, u32[]{:S(2)}) collective-permute-start(f32[64,512]{1,0:T(8,128)S(1)} %bitcast.118), channel_id=1, source_target_pairs={{0,1},{1,0},{2,3},{3,2},{4,5},{5,4},{6,7},{7,6},{8,9},{9,8},{10,11... | collective-permute-start | bytes 393224 | tf_op jit(solution)/shard_map/ppermute | solution.py:177
  (11 other events, 104.2 us)

commit v2 on v1

--- a/solution.py
+++ b/solution.py
@@ -23,10 +23,10 @@
     return lax.ppermute(value, axis, ring(n, step))
 
 
-def chunk_kernel(kind, rows, sub, scalars, b0, b1, b2, b3, thi, tlo, lims, out, stage):
+def chunk_kernel(kind, rows, sub, first_k, scalars, b0, b1, b2u, b2d, b3, thi, tlo, lims, out, stage):
     x, z, y, c = scalars[0], scalars[1], scalars[2], scalars[3]
-    zz = scalars[4 + pl.program_id(0)]
-    lam = jnp.concatenate([b0[0], b1[0], b2[0], b3[0]], axis=0)
+    zz = scalars[4 + first_k + pl.program_id(0)]
+    lam = jnp.concatenate([b0[zz], b1[zz], b2u[zz], b2d[zz], b3[zz]], axis=0)
     hi = lam.astype(jnp.bfloat16)
     lo = (lam - hi.astype(jnp.float32)).astype(jnp.bfloat16)
     dot = functools.partial(jnp.dot, preferred_element_type=jnp.float32)
@@ -51,29 +51,28 @@
         out[0, 2] = stage[2]
 
 
-def chunks(kind, rows, sub, scalars, blocks, thi, tlo, lims):
-    lam_spec = pl.BlockSpec((1, rows, K), lambda k, s: (s[4 + k], 0, 0))
-    whole = lambda shape: pl.BlockSpec(shape, lambda k, s: (0, 0))
+def chunks(kind, rows, sub, scalars, blocks, thi, tlo, lims, first_k=0, count=NZ):
+    whole = pl.BlockSpec(memory_space=pltpu.VMEM)
     if kind == "A":
-        shape, block = (NZ, 3, rows, 2 * W), (1, 3, rows, 2 * W)
+        shape, block = (count, 3, rows, 2 * W), (1, 3, rows, 2 * W)
         out_map = lambda k, s: (k, 0, 0, 0)
     else:
-        shape, block = (NX, NZ, rows, 2 * W), (NX, 1, rows, 2 * W)
+        shape, block = (NX, count, rows, 2 * W), (NX, 1, rows, 2 * W)
         out_map = lambda k, s: (0, k, 0, 0)
     return pl.pallas_call(
-        functools.partial(chunk_kernel, kind, rows, sub),
+        functools.partial(chunk_kernel, kind, rows, sub, first_k),
         out_shape=jax.ShapeDtypeStruct(shape, jnp.float32),
         grid_spec=pltpu.PrefetchScalarGridSpec(
             num_scalar_prefetch=1,
-            grid=(NZ,),
-            in_specs=[lam_spec] * 4 + [whole((K, 2 * W))] * 2 + [whole((2, 2 * W))],
+            grid=(count,),
+            in_specs=[whole] * 8,
             out_specs=pl.BlockSpec(block, out_map),
             scratch_shapes=[pltpu.VMEM((NX, rows, 2 * W), jnp.float32)],
         ),
         compiler_params=pltpu.CompilerParams(vmem_limit_bytes=24 * 1024 * 1024),
         cost_estimate=pl.CostEstimate(
-            flops=2 * 3 * NZ * 4 * rows * K * 2 * W,
-            bytes_accessed=NZ * 4 * rows * K * 4 + 4 * K * 2 * W + NZ * 4 * rows * 2 * W * 4,
+            flops=2 * 3 * count * 4 * rows * K * 2 * W,
+            bytes_accessed=count * 4 * rows * K * 4 + 4 * K * 2 * W + count * 4 * rows * 2 * W * 4,
             transcendentals=0,
         ),
     )(scalars, *blocks, thi, tlo, lims)
@@ -90,15 +89,17 @@
 
 
 def z_phase(part):
-    half = part.shape[-1] // 2
+    half = part[0].shape[-1] // 2
+    both = lax.optimization_barrier
     up = shift(part[0][..., :half], "z", NZ, 1)
     down = shift(part[0][..., half:], "z", NZ, -1)
-    up = shift(add_left(part[1], up), "z", NZ, 1)
-    down = shift(add_right(part[2], down), "z", NZ, -1)
-    up = shift(part[3] + up, "z", NZ, 1)
-    down = shift(part[4] + down, "z", NZ, -1)
-    up = shift(part[5] + up, "z", NZ, 1)
-    down = shift(part[6] + down, "z", NZ, -1)
+    up, down = both((up, down))
+    up, down = both((add_left(part[1], up), add_right(part[2], down)))
+    up, down = shift(up, "z", NZ, 1), shift(down, "z", NZ, -1)
+    for k in (3, 5):
+        up, down = both((up, down))
+        up, down = both((part[k] + up, part[k + 1] + down))
+        up, down = shift(up, "z", NZ, 1), shift(down, "z", NZ, -1)
     return part[7] + up + down
 
 
@@ -112,7 +113,7 @@
 
 
 def stream_b(part):
-    half = part.shape[-1] // 2
+    half = part[0].shape[-1] // 2
     up = shift(part[0][..., :half], "x", NX, 1)
     down = shift(part[0][..., half:], "x", NX, -1)
     up = shift(add_left(part[1], up), "x", NX, 1)
@@ -142,31 +143,39 @@
         c == 0, jnp.concatenate([mine, other], axis), jnp.concatenate([other, mine], axis)
     )
 
+    barrier = lax.optimization_barrier
+    t2_other = lax.ppermute(t2_amps, "c", swap)
+    live = jnp.arange(K, dtype=jnp.int32)[:, None] < live_pairs[0]
     blocks = []
     sub = 0
     for kind, rows in STREAMS:
         mine = keep[:, sub:sub + rows]
         other = lax.ppermute(give[:, sub:sub + rows], "c", swap)
         own = both(mine, other, 0)
-        blocks.append((
-            own,
-            shift(own, "y", NY, -1),
-            shift(own, "y", NY, 2),
-            shift(own, "y", NY, 1),
-        ))
+        if blocks:
+            own, thi = barrier((own, thi))
+        up = shift(own, "y", NY, 1)
+        down = shift(own, "y", NY, -1)
+        if not blocks:
+            up, down, t2_other = barrier((up, down, t2_other))
+            t2_pair = jnp.where(live, both(t2_amps, t2_other, 1), 0.0)
+            t2_top = lax.reduce_precision(t2_pair, 8, 7)
+            thi = t2_top.astype(jnp.bfloat16)
+            tlo = (t2_pair - t2_top).astype(jnp.bfloat16)
+        far_up = shift(up[:, :rows // 2], "y", NY, 1)
+        far_down = shift(down[:, rows // 2:], "y", NY, -1)
+        blocks.append((own, down, far_up, far_down, up))
         sub += rows
-
-    t2_pair = both(t2_amps, lax.ppermute(t2_amps, "c", swap), 1)
-    live = jnp.arange(K, dtype=jnp.int32)[:, None] < live_pairs[0]
-    t2_pair = jnp.where(live, t2_pair, 0.0)
-    t2_top = lax.reduce_precision(t2_pair, 8, 7)
-    thi = t2_top.astype(jnp.bfloat16)
-    tlo = (t2_pair - t2_top).astype(jnp.bfloat16)
 
     done = []
     sub = 0
     for (kind, rows), block in zip(STREAMS, blocks):
-        part = chunks(kind, rows, sub, scalars, block, thi, tlo, lims)
+        if kind == "A":
+            head = chunks(kind, rows, sub, scalars, block, thi, tlo, lims, 0, 3)
+            tail = chunks(kind, rows, sub, scalars, block, thi, tlo, lims, 3, 5)
+            part = [head[k] for k in range(3)] + [tail[k] for k in range(5)]
+        else:
+            part = chunks(kind, rows, sub, scalars, block, thi, tlo, lims)
         got = stream_a(part, x) if kind == "A" else stream_b(part)
         row = (x * 1024 + z * 128 + c * SUB + sub + jnp.arange(rows, dtype=jnp.int32))[:, None]
         done.append(jnp.where((row >= lims[0:1]) & (row < lims[1:2]), got, 0.0))

time: 153 us -> 121 us (0.79)
  waiting for transfers between devices: 76.8 us -> 42.7 us
  starting transfers between devices: 43.7 us -> 54.4 us
  local copies, waits for them, and re-layouts: 9.98 us -> 2.65 us
  other arithmetic: 9.65 us -> 7.85 us
    ppermute x28 -> x30, waiting for transfers between devices: 75.8 us -> 41.3 us  [shift(): return lax.ppermute(value, axis, ring(n, step))]
    ppermute x28 -> x30, starting transfers between devices: 35.9 us -> 44.5 us  [shift(): return lax.ppermute(value, axis, ring(n, step))]
    unnamed x25 -> x7, local copies, waits for them, and re-layouts: 8.22 us -> 1.58 us
    ppermute x1, starting transfers between devices: 4.07 us -> 6.1 us  [body(): lax.ppermute(lax.dynamic_index_in_dim(rows_all, 1 - c, 1, keepdims=False)...]
    pallas_call x2 -> x4, Pallas kernels: 11.2 us -> 12.3 us  [chunks(): pl.pallas_call(functools.partial(chunk_kernel, kind, rows, sub, first_k),...]
  transfers between devices with their start and end apart: 32 -> 34, of which waited for: 15 -> 15; matrix products, arithmetic and copies ran while one was open for 6% -> 6% of each run, Pallas kernels for 7% -> 10%
where the time goes in v2:
time: 121 us
  starting transfers between devices  54.4 us (45%)
  waiting for transfers between devices  42.7 us (35%)
  Pallas kernels  12.3 us (10%)
  other arithmetic  7.85 us (6%)
  local copies, waits for them, and re-layouts  2.65 us (2%)
    ppermute x30, starting transfers between devices, shift(): return lax.ppermute(value, axis, ring(n, step))  44.5 us
    ppermute x30, waiting for transfers between devices, shift(): return lax.ppermute(value, axis, ring(n, step))  41.3 us
    pallas_call x4, Pallas kernels, chunks(): pl.pallas_call(functools.partial(chunk_kernel, kind, rows, sub, first_k),...  12.3 us
    ppermute x1, starting transfers between devices, body(): lax.ppermute(lax.dynamic_index_in_dim(rows_all, 1 - c, 1, keepdims=False)...  6.1 us
    ppermute x2, starting transfers between devices, body(): other = lax.ppermute(give[:, sub:sub + rows], 'c', swap)  3.74 us
    convert_element_type x1, other arithmetic, body(): tlo = (t2_pair - t2_top).astype(jnp.bfloat16)  2.65 us
    add x2, other arithmetic, z_phase(): return part[7] + up + down  2.47 us
  transfers between devices with their start and end apart: 34, of which 15 were waited for; matrix products, arithmetic and copies ran while one was open for 6% of the time, Pallas kernels for 10%

profile of v2, /device:TPU:1, one launch (start us, length us, event | category | flops | bytes accessed | tf_op | source)
XLA Modules:
  0.0 120.9 jit_solution(18236442097235833900)
XLA Ops:
  0.0 1.6 %copy.8 = f32[512,512]{0,1:T(8,128)S(1)} copy(f32[512,512]{1,0:T(8,128)} %param.5) | data formatting | bytes 2097152 | tf_op args[1]
  1.7 3.3 %collective-permute-start = (f32[4,32,512]{2,1,0:T(8,128)S(1)}, f32[4,32,512]{2,1,0:T(8,128)S(1)}, u32[]{:S(2)}, u32[]{:S(2)}) collective-permute-start(f32[4,32,512]{2,1,0:T(8,128)S(1)} %get-tuple-element.85), channel_id=1, source_target_pairs={{0,1},{1,0},{2,3},{3,2},{4,5},{5,4},{6,7},{7,6},{8,9},{9,8},{10,11... | collective-permute-start | bytes 786440 | tf_op jit(solution)/shard_map/ppermute | solution.py:153
  6.4 2.7 %collective-permute-start.2 = (f32[8,32,512]{2,1,0:T(8,128)S(1)}, f32[8,32,512]{2,1,0:T(8,128)S(1)}, u32[]{:S(2)}, u32[]{:S(2)}) collective-permute-start(f32[8,32,512]{2,1,0:T(8,128)S(1)} %maximum_select_fusion.1.b0), channel_id=1, source_target_pairs={{0,6},{2,0},{4,2},{6,4},{1,7},{3,1},{5,3},{7,5},{8,14},{10,8},{12,... | collective-permute-start | bytes 1572872 | tf_op jit(solution)/shard_map/ppermute | solution.py:23
  10.0 10.7 %collective-permute-done.1.b3 = f32[8,32,512]{2,1,0:T(8,128)S(1)} collective-permute-done((f32[8,32,512]{2,1,0:T(8,128)S(1)}, f32[8,32,512]{2,1,0:T(8,128)S(1)}, u32[]{:S(2)}, u32[]{:S(2)}) %collective-permute-start.1) | collective-permute-done | bytes 524320 | tf_op jit(solution)/shard_map/ppermute | solution.py:23
  20.8 2.7 %collective-permute-start.5 = (f32[8,16,512]{2,1,0:T(8,128)S(1)}, f32[8,16,512]{2,1,0:T(8,128)S(1)}, u32[]{:S(2)}, u32[]{:S(2)}) collective-permute-start(f32[8,16,512]{2,1,0:T(8,128)S(1)} %slice.111), channel_id=1, source_target_pairs={{0,6},{2,0},{4,2},{6,4},{1,7},{3,1},{5,3},{7,5},{8,14},{10,8},{12,... | collective-permute-start | bytes 786440 | tf_op jit(solution)/shard_map/ppermute | solution.py:23
  23.6 2.7 %fusion = (bf16[512,1024]{1,0:T(8,128)(2,1)S(1)}, bf16[512,1024]{1,0:T(8,128)(2,1)S(1)}) fusion(f32[512,512]{1,0:T(8,128)} %param.4, f32[512,512]{1,0:T(8,128)} %collective-permute-done.3, pred[512]{0:T(512)(128)(4,1)S(1)} %iota_compare_fusion, pred[]{:T(512)S(6)} %eq.2), kind=kLoop, calls=%fused_computation.2 | loop fusion | flops 4194304 | bytes 4194817 | tf_op jit(solution)/shard_map/convert_element_type | solution.py:164
  26.2 1.2 %collective-permute-start.18 = (f32[8,32,512]{2,1,0:T(8,128)S(1)}, f32[8,32,512]{2,1,0:T(8,128)S(1)}, u32[]{:S(2)}, u32[]{:S(2)}) collective-permute-start(f32[8,32,512]{2,1,0:T(8,128)S(1)} %maximum_select_fusion.2.b0), channel_id=1, source_target_pairs={{0,6},{2,0},{4,2},{6,4},{1,7},{3,1},{5,3},{7,5},{8,14},{10,8},{12,... | collective-permute-start | bytes 1572872 | tf_op jit(solution)/shard_map/ppermute | solution.py:23
  28.6 2.5 %shard_map.47 = f32[3,3,32,1024]{3,2,1,0:T(8,128)S(1)} custom-call(s32[12]{0:T(128)S(1)} %stack.60.scalars, f32[8,32,512]{2,1,0:T(8,128)S(1)} %maximum_select_fusion.1.b0, f32[8,32,512]{2,1,0:T(8,128)S(1)} %collective-permute-done.2.b1, f32[8,16,512]{2,1,0:T(8,128)S(1)} %collective-permute-done.4.b2u, f32[8,16,512]{2,1,0:T(8,128)S(1)} %collective-permute-done.5.b2d, ...), custom_call_target="tpu_custom_call" | custom-call | flops 1207959552 | bytes 4456448 | tf_op jit(solution)/shard_map/pallas_call | solution.py:62
  31.4 4.0 %collective-permute-start.8 = (f32[3,32,512]{2,1,0:T(8,128)S(1)}, f32[3,32,512]{2,1,0:T(8,128)S(1)}, u32[]{:S(2)}, u32[]{:S(2)}) collective-permute-start(f32[3,32,512]{2,1,0:T(8,128)S(1)} %get-tuple-element.94), channel_id=1, source_target_pairs={{0,56},{8,0},{16,8},{24,16},{32,24},{40,32},{48,40},{56,48},{1,57}... | collective-permute-start | bytes 589832 | tf_op jit(solution)/shard_map/ppermute | solution.py:23
  35.4 3.3 %collective-permute-done.7 = f32[3,32,512]{2,1,0:T(8,128)S(1)} collective-permute-done((f32[3,32,512]{2,1,0:T(8,128)S(1)}, f32[3,32,512]{2,1,0:T(8,128)S(1)}, u32[]{:S(2)}, u32[]{:S(2)}) %collective-permute-start.7) | collective-permute-done | bytes 196640 | tf_op jit(solution)/shard_map/ppermute | solution.py:23
  39.9 2.9 %collective-permute-start.21 = (f32[8,16,512]{2,1,0:T(8,128)S(1)}, f32[8,16,512]{2,1,0:T(8,128)S(1)}, u32[]{:S(2)}, u32[]{:S(2)}) collective-permute-start(f32[8,16,512]{2,1,0:T(8,128)S(1)} %slice.163), channel_id=1, source_target_pairs={{0,6},{2,0},{4,2},{6,4},{1,7},{3,1},{5,3},{7,5},{8,14},{10,8},{12,... | collective-permute-start | bytes 786440 | tf_op jit(solution)/shard_map/ppermute | solution.py:23
  43.2 4.2 %collective-permute-start.10 = (f32[3,32,1024]{2,1,0:T(8,128)S(1)}, f32[3,32,1024]{2,1,0:T(8,128)S(1)}, u32[]{:S(2)}, u32[]{:S(2)}) collective-permute-start(f32[3,32,1024]{2,1,0:T(8,128)S(1)} %pad_maximum_fusion.1), channel_id=1, source_target_pairs={{0,56},{8,0},{16,8},{24,16},{32,24},{40,32},{48,40},{56,48},{1,57}... | collective-permute-start | bytes 1179656 | tf_op jit(solution)/shard_map/ppermute | solution.py:23
  47.4 2.4 %shard_map.49 = f32[3,3,32,1024]{3,2,1,0:T(8,128)S(1)} custom-call(s32[12]{0:T(128)S(1)} %stack.60.scalars, f32[8,32,512]{2,1,0:T(8,128)S(1)} %maximum_select_fusion.2.b0, f32[8,32,512]{2,1,0:T(8,128)S(1)} %collective-permute-done.18.b1, f32[8,16,512]{2,1,0:T(8,128)S(1)} %collective-permute-done.20.b2u, f32[8,16,512]{2,1,0:T(8,128)S(1)} %collective-permute-done.21.b2d, ...), custom_call_target="tpu_custom_call" | custom-call | flops 1207959552 | bytes 4456448 | tf_op jit(solution)/shard_map/pallas_call | solution.py:62
  50.1 3.2 %collective-permute-start.23 = (f32[3,32,512]{2,1,0:T(8,128)S(1)}, f32[3,32,512]{2,1,0:T(8,128)S(1)}, u32[]{:S(2)}, u32[]{:S(2)}) collective-permute-start(f32[3,32,512]{2,1,0:T(8,128)S(1)} %get-tuple-element.103), channel_id=1, source_target_pairs={{0,56},{8,0},{16,8},{24,16},{32,24},{40,32},{48,40},{56,48},{1,57}... | collective-permute-start | bytes 589832 | tf_op jit(solution)/shard_map/ppermute | solution.py:23
  53.3 3.7 %shard_map.46 = f32[5,3,32,1024]{3,2,1,0:T(8,128)S(1)} custom-call(s32[12]{0:T(128)S(1)} %stack.60.scalars, f32[8,32,512]{2,1,0:T(8,128)S(1)} %maximum_select_fusion.1.b0, f32[8,32,512]{2,1,0:T(8,128)S(1)} %collective-permute-done.2.b1, f32[8,16,512]{2,1,0:T(8,128)S(1)} %collective-permute-done.4.b2u, f32[8,16,512]{2,1,0:T(8,128)S(1)} %collective-permute-done.5.b2d, ...), custom_call_target="tpu_custom_call" | custom-call | flops 2013265920 | bytes 6029312 | tf_op jit(solution)/shard_map/pallas_call | solution.py:62
  57.1 1.7 %collective-permute-done.22 = f32[3,32,512]{2,1,0:T(8,128)S(1)} collective-permute-done((f32[3,32,512]{2,1,0:T(8,128)S(1)}, f32[3,32,512]{2,1,0:T(8,128)S(1)}, u32[]{:S(2)}, u32[]{:S(2)}) %collective-permute-start.22) | collective-permute-done | bytes 196640 | tf_op jit(solution)/shard_map/ppermute | solution.py:23
  59.0 2.8 %collective-permute-start.25 = (f32[3,32,1024]{2,1,0:T(8,128)S(1)}, f32[3,32,1024]{2,1,0:T(8,128)S(1)}, u32[]{:S(2)}, u32[]{:S(2)}) collective-permute-start(f32[3,32,1024]{2,1,0:T(8,128)S(1)} %pad_maximum_fusion.3), channel_id=1, source_target_pairs={{0,56},{8,0},{16,8},{24,16},{32,24},{40,32},{48,40},{56,48},{1,57}... | collective-permute-start | bytes 1179656 | tf_op jit(solution)/shard_map/ppermute | solution.py:23
  62.0 2.7 %collective-permute-start.12 = (f32[3,32,1024]{2,1,0:T(8,128)S(1)}, f32[3,32,1024]{2,1,0:T(8,128)S(1)}, u32[]{:S(2)}, u32[]{:S(2)}) collective-permute-start(f32[3,32,1024]{2,1,0:T(8,128)S(1)} %get-tuple-element.45), channel_id=1, source_target_pairs={{0,56},{8,0},{16,8},{24,16},{32,24},{40,32},{48,40},{56,48},{1,57}... | collective-permute-start | bytes 1179656 | tf_op jit(solution)/shard_map/ppermute | solution.py:23
  64.7 3.7 %shard_map.48 = f32[5,3,32,1024]{3,2,1,0:T(8,128)S(1)} custom-call(s32[12]{0:T(128)S(1)} %stack.60.scalars, f32[8,32,512]{2,1,0:T(8,128)S(1)} %maximum_select_fusion.2.b0, f32[8,32,512]{2,1,0:T(8,128)S(1)} %collective-permute-done.18.b1, f32[8,16,512]{2,1,0:T(8,128)S(1)} %collective-permute-done.20.b2u, f32[8,16,512]{2,1,0:T(8,128)S(1)} %collective-permute-done.21.b2d, ...), custom_call_target="tpu_custom_call" | custom-call | flops 2013265920 | bytes 6029312 | tf_op jit(solution)/shard_map/pallas_call | solution.py:62
  69.7 1.6 %collective-permute-start.27 = (f32[3,32,1024]{2,1,0:T(8,128)S(1)}, f32[3,32,1024]{2,1,0:T(8,128)S(1)}, u32[]{:S(2)}, u32[]{:S(2)}) collective-permute-start(f32[3,32,1024]{2,1,0:T(8,128)S(1)} %get-tuple-element.58), channel_id=1, source_target_pairs={{0,56},{8,0},{16,8},{24,16},{32,24},{40,32},{48,40},{56,48},{1,57}... | collective-permute-start | bytes 1179656 | tf_op jit(solution)/shard_map/ppermute | solution.py:23
  71.3 5.2 %collective-permute-done.11 = f32[3,32,1024]{2,1,0:T(8,128)S(1)} collective-permute-done((f32[3,32,1024]{2,1,0:T(8,128)S(1)}, f32[3,32,1024]{2,1,0:T(8,128)S(1)}, u32[]{:S(2)}, u32[]{:S(2)}) %collective-permute-start.11) | collective-permute-done | bytes 393248 | tf_op jit(solution)/shard_map/ppermute | solution.py:23
  77.4 2.5 %collective-permute-start.14 = (f32[3,32,1024]{2,1,0:T(8,128)}, f32[3,32,1024]{2,1,0:T(8,128)}, u32[]{:S(2)}, u32[]{:S(2)}) collective-permute-start(f32[3,32,1024]{2,1,0:T(8,128)} %get-tuple-element.49), channel_id=1, source_target_pairs={{0,56},{8,0},{16,8},{24,16},{32,24},{40,32},{48,40},{56,48},{1,57}... | collective-permute-start | bytes 1179656 | tf_op jit(solution)/shard_map/ppermute | solution.py:23
  79.9 5.0 %collective-permute-done.26 = f32[3,32,1024]{2,1,0:T(8,128)S(1)} collective-permute-done((f32[3,32,1024]{2,1,0:T(8,128)S(1)}, f32[3,32,1024]{2,1,0:T(8,128)S(1)}, u32[]{:S(2)}, u32[]{:S(2)}) %collective-permute-start.26) | collective-permute-done | bytes 393248 | tf_op jit(solution)/shard_map/ppermute | solution.py:23
  85.1 2.6 %collective-permute-start.29 = (f32[3,32,1024]{2,1,0:T(8,128)S(1)}, f32[3,32,1024]{2,1,0:T(8,128)}, u32[]{:S(2)}, u32[]{:S(2)}) collective-permute-start(f32[3,32,1024]{2,1,0:T(8,128)S(1)} %get-tuple-element.62), channel_id=1, source_target_pairs={{0,56},{8,0},{16,8},{24,16},{32,24},{40,32},{48,40},{56,48},{1,57}... | collective-permute-start | bytes 1179656 | tf_op jit(solution)/shard_map/ppermute | solution.py:23
  87.7 4.9 %collective-permute-done.14 = f32[3,32,1024]{2,1,0:T(8,128)} collective-permute-done((f32[3,32,1024]{2,1,0:T(8,128)}, f32[3,32,1024]{2,1,0:T(8,128)}, u32[]{:S(2)}, u32[]{:S(2)}) %collective-permute-start.14) | collective-permute-done | bytes 393248 | tf_op jit(solution)/shard_map/ppermute | solution.py:23
  94.2 3.1 %collective-permute-start.17 = (f32[32,1024]{1,0:T(8,128)S(1)}, f32[32,1024]{1,0:T(8,128)S(1)}, u32[]{:S(2)}, u32[]{:S(2)}) collective-permute-start(f32[32,1024]{1,0:T(8,128)S(1)} %get-tuple-element.88), channel_id=1, source_target_pairs={{0,128},{64,192},{128,0},{192,64},{1,129},{65,193},{129,1},{193,65... | collective-permute-start | bytes 393224 | tf_op jit(solution)/shard_map/ppermute | solution.py:23
  98.7 2.2 %collective-permute-done.29 = f32[3,32,1024]{2,1,0:T(8,128)} collective-permute-done((f32[3,32,1024]{2,1,0:T(8,128)S(1)}, f32[3,32,1024]{2,1,0:T(8,128)}, u32[]{:S(2)}, u32[]{:S(2)}) %collective-permute-start.29) | collective-permute-done | bytes 393248 | tf_op jit(solution)/shard_map/ppermute | solution.py:23
  101.4 1.3 %fusion.7 = f32[3,32,1024]{2,1,0:T(8,128)S(1)} fusion(f32[3,32,1024]{2,1,0:T(8,128)} %collective-permute-done.29, f32[3,32,1024]{2,1,0:T(8,128)} %collective-permute-done.28, f32[5,3,32,1024]{3,2,1,0:T(8,128)} %copy-done), kind=kLoop, calls=%fused_computation.22 | loop fusion | flops 196608 | bytes 1572864 | tf_op jit(solution)/shard_map/add | solution.py:103
  102.7 2.8 %collective-permute-start.32 = (f32[32,1024]{1,0:T(8,128)S(1)}, f32[32,1024]{1,0:T(8,128)S(1)}, u32[]{:S(2)}, u32[]{:S(2)}) collective-permute-start(f32[32,1024]{1,0:T(8,128)S(1)} %get-tuple-element.97), channel_id=1, source_target_pairs={{0,128},{64,192},{128,0},{192,64},{1,129},{65,193},{129,1},{193,65... | collective-permute-start | bytes 393224 | tf_op jit(solution)/shard_map/ppermute | solution.py:23
  107.0 2.5 %collective-permute-done.32 = f32[32,1024]{1,0:T(8,128)S(1)} collective-permute-done((f32[32,1024]{1,0:T(8,128)S(1)}, f32[32,1024]{1,0:T(8,128)S(1)}, u32[]{:S(2)}, u32[]{:S(2)}) %collective-permute-start.32) | collective-permute-done | bytes 131104 | tf_op jit(solution)/shard_map/ppermute | solution.py:23
  109.6 2.9 %collective-permute-done.31 = f32[32,1024]{1,0:T(8,128)S(1)} collective-permute-done((f32[32,1024]{1,0:T(8,128)S(1)}, f32[32,1024]{1,0:T(8,128)S(1)}, u32[]{:S(2)}, u32[]{:S(2)}) %collective-permute-start.31) | collective-permute-done | bytes 131104 | tf_op jit(solution)/shard_map/ppermute | solution.py:23
  113.1 6.1 %collective-permute-start.33 = (f32[64,512]{1,0:T(8,128)S(1)}, f32[64,512]{1,0:T(8,128)S(1)}, u32[]{:S(2)}, u32[]{:S(2)}) collective-permute-start(f32[64,512]{1,0:T(8,128)S(1)} %bitcast.118), channel_id=1, source_target_pairs={{0,1},{1,0},{2,3},{3,2},{4,5},{5,4},{6,7},{7,6},{8,9},{9,8},{10,11... | collective-permute-start | bytes 393224 | tf_op jit(solution)/shard_map/ppermute | solution.py:186
  (88 shorter events, 15.0 us)
Async XLA Ops:
  5.1 15.6 %collective-permute-start.3 = (f32[512,512]{1,0:T(8,128)}, f32[512,512]{1,0:T(8,128)}, u32[]{:S(2)}, u32[]{:S(2)}) collective-permute-start(f32[512,512]{1,0:T(8,128)} %param.4), channel_id=1, source_target_pairs={{0,1},{1,0},{2,3},{3,2},{4,5},{5,4},{6,7},{7,6},{8,9},{9,8},{10,11... | collective-permute-start | bytes 3145736 | tf_op jit(solution)/shard_map/ppermute | solution.py:147
  6.3 14.4 %collective-permute-start.1 = (f32[8,32,512]{2,1,0:T(8,128)S(1)}, f32[8,32,512]{2,1,0:T(8,128)S(1)}, u32[]{:S(2)}, u32[]{:S(2)}) collective-permute-start(f32[8,32,512]{2,1,0:T(8,128)S(1)} %maximum_select_fusion.1.b0), channel_id=1, source_target_pairs={{0,2},{2,4},{4,6},{6,0},{1,3},{3,5},{5,7},{7,1},{8,10},{10,12},{12... | collective-permute-start | bytes 1572872 | tf_op jit(solution)/shard_map/ppermute | solution.py:23
  6.4 14.3 %collective-permute-start.2 = (f32[8,32,512]{2,1,0:T(8,128)S(1)}, f32[8,32,512]{2,1,0:T(8,128)S(1)}, u32[]{:S(2)}, u32[]{:S(2)}) collective-permute-start(f32[8,32,512]{2,1,0:T(8,128)S(1)} %maximum_select_fusion.1.b0), channel_id=1, source_target_pairs={{0,6},{2,0},{4,2},{6,4},{1,7},{3,1},{5,3},{7,5},{8,14},{10,8},{12,... | collective-permute-start | bytes 1572872 | tf_op jit(solution)/shard_map/ppermute | solution.py:23
  20.7 7.9 %collective-permute-start.4 = (f32[8,16,512]{2,1,0:T(8,128)S(1)}, f32[8,16,512]{2,1,0:T(8,128)S(1)}, u32[]{:S(2)}, u32[]{:S(2)}) collective-permute-start(f32[8,16,512]{2,1,0:T(8,128)S(1)} %slice.110), channel_id=1, source_target_pairs={{0,2},{2,4},{4,6},{6,0},{1,3},{3,5},{5,7},{7,1},{8,10},{10,12},{12... | collective-permute-start | bytes 786440 | tf_op jit(solution)/shard_map/ppermute | solution.py:23
  20.8 7.8 %collective-permute-start.5 = (f32[8,16,512]{2,1,0:T(8,128)S(1)}, f32[8,16,512]{2,1,0:T(8,128)S(1)}, u32[]{:S(2)}, u32[]{:S(2)}) collective-permute-start(f32[8,16,512]{2,1,0:T(8,128)S(1)} %slice.111), channel_id=1, source_target_pairs={{0,6},{2,0},{4,2},{6,4},{1,7},{3,1},{5,3},{7,5},{8,14},{10,8},{12,... | collective-permute-start | bytes 786440 | tf_op jit(solution)/shard_map/ppermute | solution.py:23
  26.2 13.6 %collective-permute-start.18 = (f32[8,32,512]{2,1,0:T(8,128)S(1)}, f32[8,32,512]{2,1,0:T(8,128)S(1)}, u32[]{:S(2)}, u32[]{:S(2)}) collective-permute-start(f32[8,32,512]{2,1,0:T(8,128)S(1)} %maximum_select_fusion.2.b0), channel_id=1, source_target_pairs={{0,6},{2,0},{4,2},{6,4},{1,7},{3,1},{5,3},{7,5},{8,14},{10,8},{12,... | collective-permute-start | bytes 1572872 | tf_op jit(solution)/shard_map/ppermute | solution.py:23
  27.5 12.3 %collective-permute-start.19 = (f32[8,32,512]{2,1,0:T(8,128)S(1)}, f32[8,32,512]{2,1,0:T(8,128)S(1)}, u32[]{:S(2)}, u32[]{:S(2)}) collective-permute-start(f32[8,32,512]{2,1,0:T(8,128)S(1)} %maximum_select_fusion.2.b0), channel_id=1, source_target_pairs={{0,2},{2,4},{4,6},{6,0},{1,3},{3,5},{5,7},{7,1},{8,10},{10,12},{12... | collective-permute-start | bytes 1572872 | tf_op jit(solution)/shard_map/ppermute | solution.py:23
  31.2 7.4 %collective-permute-start.7 = (f32[3,32,512]{2,1,0:T(8,128)S(1)}, f32[3,32,512]{2,1,0:T(8,128)S(1)}, u32[]{:S(2)}, u32[]{:S(2)}) collective-permute-start(f32[3,32,512]{2,1,0:T(8,128)S(1)} %get-tuple-element.95), channel_id=1, source_target_pairs={{0,8},{8,16},{16,24},{24,32},{32,40},{40,48},{48,56},{56,0},{1,9},... | collective-permute-start | bytes 589832 | tf_op jit(solution)/shard_map/ppermute | solution.py:23
  31.4 7.3 %collective-permute-start.8 = (f32[3,32,512]{2,1,0:T(8,128)S(1)}, f32[3,32,512]{2,1,0:T(8,128)S(1)}, u32[]{:S(2)}, u32[]{:S(2)}) collective-permute-start(f32[3,32,512]{2,1,0:T(8,128)S(1)} %get-tuple-element.94), channel_id=1, source_target_pairs={{0,56},{8,0},{16,8},{24,16},{32,24},{40,32},{48,40},{56,48},{1,57}... | collective-permute-start | bytes 589832 | tf_op jit(solution)/shard_map/ppermute | solution.py:23
  39.7 7.7 %collective-permute-start.20 = (f32[8,16,512]{2,1,0:T(8,128)S(1)}, f32[8,16,512]{2,1,0:T(8,128)S(1)}, u32[]{:S(2)}, u32[]{:S(2)}) collective-permute-start(f32[8,16,512]{2,1,0:T(8,128)S(1)} %slice.162), channel_id=1, source_target_pairs={{0,2},{2,4},{4,6},{6,0},{1,3},{3,5},{5,7},{7,1},{8,10},{10,12},{12... | collective-permute-start | bytes 786440 | tf_op jit(solution)/shard_map/ppermute | solution.py:23
  39.9 7.6 %collective-permute-start.21 = (f32[8,16,512]{2,1,0:T(8,128)S(1)}, f32[8,16,512]{2,1,0:T(8,128)S(1)}, u32[]{:S(2)}, u32[]{:S(2)}) collective-permute-start(f32[8,16,512]{2,1,0:T(8,128)S(1)} %slice.163), channel_id=1, source_target_pairs={{0,6},{2,0},{4,2},{6,4},{1,7},{3,1},{5,3},{7,5},{8,14},{10,8},{12,... | collective-permute-start | bytes 786440 | tf_op jit(solution)/shard_map/ppermute | solution.py:23
  42.9 14.1 %collective-permute-start.9 = (f32[3,32,1024]{2,1,0:T(8,128)S(1)}, f32[3,32,1024]{2,1,0:T(8,128)S(1)}, u32[]{:S(2)}, u32[]{:S(2)}) collective-permute-start(f32[3,32,1024]{2,1,0:T(8,128)S(1)} %pad_maximum_fusion), channel_id=1, source_target_pairs={{0,8},{8,16},{16,24},{24,32},{32,40},{40,48},{48,56},{56,0},{1,9},... | collective-permute-start | bytes 1179656 | tf_op jit(solution)/shard_map/ppermute | solution.py:23
  43.2 13.8 %collective-permute-start.10 = (f32[3,32,1024]{2,1,0:T(8,128)S(1)}, f32[3,32,1024]{2,1,0:T(8,128)S(1)}, u32[]{:S(2)}, u32[]{:S(2)}) collective-permute-start(f32[3,32,1024]{2,1,0:T(8,128)S(1)} %pad_maximum_fusion.1), channel_id=1, source_target_pairs={{0,56},{8,0},{16,8},{24,16},{32,24},{40,32},{48,40},{56,48},{1,57}... | collective-permute-start | bytes 1179656 | tf_op jit(solution)/shard_map/ppermute | solution.py:23
  50.0 8.7 %collective-permute-start.22 = (f32[3,32,512]{2,1,0:T(8,128)S(1)}, f32[3,32,512]{2,1,0:T(8,128)S(1)}, u32[]{:S(2)}, u32[]{:S(2)}) collective-permute-start(f32[3,32,512]{2,1,0:T(8,128)S(1)} %get-tuple-element.104), channel_id=1, source_target_pairs={{0,8},{8,16},{16,24},{24,32},{32,40},{40,48},{48,56},{56,0},{1,9},... | collective-permute-start | bytes 589832 | tf_op jit(solution)/shard_map/ppermute | solution.py:23
  50.1 8.6 %collective-permute-start.23 = (f32[3,32,512]{2,1,0:T(8,128)S(1)}, f32[3,32,512]{2,1,0:T(8,128)S(1)}, u32[]{:S(2)}, u32[]{:S(2)}) collective-permute-start(f32[3,32,512]{2,1,0:T(8,128)S(1)} %get-tuple-element.103), channel_id=1, source_target_pairs={{0,56},{8,0},{16,8},{24,16},{32,24},{40,32},{48,40},{56,48},{1,57}... | collective-permute-start | bytes 589832 | tf_op jit(solution)/shard_map/ppermute | solution.py:23
  58.9 9.5 %collective-permute-start.24 = (f32[3,32,1024]{2,1,0:T(8,128)S(1)}, f32[3,32,1024]{2,1,0:T(8,128)S(1)}, u32[]{:S(2)}, u32[]{:S(2)}) collective-permute-start(f32[3,32,1024]{2,1,0:T(8,128)S(1)} %pad_maximum_fusion.2), channel_id=1, source_target_pairs={{0,8},{8,16},{16,24},{24,32},{32,40},{40,48},{48,56},{56,0},{1,9},... | collective-permute-start | bytes 1179656 | tf_op jit(solution)/shard_map/ppermute | solution.py:23
  59.0 9.4 %collective-permute-start.25 = (f32[3,32,1024]{2,1,0:T(8,128)S(1)}, f32[3,32,1024]{2,1,0:T(8,128)S(1)}, u32[]{:S(2)}, u32[]{:S(2)}) collective-permute-start(f32[3,32,1024]{2,1,0:T(8,128)S(1)} %pad_maximum_fusion.3), channel_id=1, source_target_pairs={{0,56},{8,0},{16,8},{24,16},{32,24},{40,32},{48,40},{56,48},{1,57}... | collective-permute-start | bytes 1179656 | tf_op jit(solution)/shard_map/ppermute | solution.py:23
  61.9 14.6 %collective-permute-start.11 = (f32[3,32,1024]{2,1,0:T(8,128)S(1)}, f32[3,32,1024]{2,1,0:T(8,128)S(1)}, u32[]{:S(2)}, u32[]{:S(2)}) collective-permute-start(f32[3,32,1024]{2,1,0:T(8,128)S(1)} %get-tuple-element.44), channel_id=1, source_target_pairs={{0,8},{8,16},{16,24},{24,32},{32,40},{40,48},{48,56},{56,0},{1,9},... | collective-permute-start | bytes 1179656 | tf_op jit(solution)/shard_map/ppermute | solution.py:23
  62.0 14.5 %collective-permute-start.12 = (f32[3,32,1024]{2,1,0:T(8,128)S(1)}, f32[3,32,1024]{2,1,0:T(8,128)S(1)}, u32[]{:S(2)}, u32[]{:S(2)}) collective-permute-start(f32[3,32,1024]{2,1,0:T(8,128)S(1)} %get-tuple-element.45), channel_id=1, source_target_pairs={{0,56},{8,0},{16,8},{24,16},{32,24},{40,32},{48,40},{56,48},{1,57}... | collective-permute-start | bytes 1179656 | tf_op jit(solution)/shard_map/ppermute | solution.py:23
  68.5 16.4 %collective-permute-start.26 = (f32[3,32,1024]{2,1,0:T(8,128)S(1)}, f32[3,32,1024]{2,1,0:T(8,128)S(1)}, u32[]{:S(2)}, u32[]{:S(2)}) collective-permute-start(f32[3,32,1024]{2,1,0:T(8,128)S(1)} %get-tuple-element.57), channel_id=1, source_target_pairs={{0,8},{8,16},{16,24},{24,32},{32,40},{40,48},{48,56},{56,0},{1,9},... | collective-permute-start | bytes 1179656 | tf_op jit(solution)/shard_map/ppermute | solution.py:23
  69.7 15.2 %collective-permute-start.27 = (f32[3,32,1024]{2,1,0:T(8,128)S(1)}, f32[3,32,1024]{2,1,0:T(8,128)S(1)}, u32[]{:S(2)}, u32[]{:S(2)}) collective-permute-start(f32[3,32,1024]{2,1,0:T(8,128)S(1)} %get-tuple-element.58), channel_id=1, source_target_pairs={{0,56},{8,0},{16,8},{24,16},{32,24},{40,32},{48,40},{56,48},{1,57}... | collective-permute-start | bytes 1179656 | tf_op jit(solution)/shard_map/ppermute | solution.py:23
  77.4 15.2 %collective-permute-start.14 = (f32[3,32,1024]{2,1,0:T(8,128)}, f32[3,32,1024]{2,1,0:T(8,128)}, u32[]{:S(2)}, u32[]{:S(2)}) collective-permute-start(f32[3,32,1024]{2,1,0:T(8,128)} %get-tuple-element.49), channel_id=1, source_target_pairs={{0,56},{8,0},{16,8},{24,16},{32,24},{40,32},{48,40},{56,48},{1,57}... | collective-permute-start | bytes 1179656 | tf_op jit(solution)/shard_map/ppermute | solution.py:23
  79.9 13.0 %collective-permute-start.13 = (f32[3,32,1024]{2,1,0:T(8,128)S(1)}, f32[3,32,1024]{2,1,0:T(8,128)}, u32[]{:S(2)}, u32[]{:S(2)}) collective-permute-start(f32[3,32,1024]{2,1,0:T(8,128)S(1)} %get-tuple-element.48), channel_id=1, source_target_pairs={{0,8},{8,16},{16,24},{24,32},{32,40},{40,48},{48,56},{56,0},{1,9},... | collective-permute-start | bytes 1179656 | tf_op jit(solution)/shard_map/ppermute | solution.py:23
  85.1 15.9 %collective-permute-start.29 = (f32[3,32,1024]{2,1,0:T(8,128)S(1)}, f32[3,32,1024]{2,1,0:T(8,128)}, u32[]{:S(2)}, u32[]{:S(2)}) collective-permute-start(f32[3,32,1024]{2,1,0:T(8,128)S(1)} %get-tuple-element.62), channel_id=1, source_target_pairs={{0,56},{8,0},{16,8},{24,16},{32,24},{40,32},{48,40},{56,48},{1,57}... | collective-permute-start | bytes 1179656 | tf_op jit(solution)/shard_map/ppermute | solution.py:23
  87.7 13.7 %collective-permute-start.28 = (f32[3,32,1024]{2,1,0:T(8,128)S(1)}, f32[3,32,1024]{2,1,0:T(8,128)}, u32[]{:S(2)}, u32[]{:S(2)}) collective-permute-start(f32[3,32,1024]{2,1,0:T(8,128)S(1)} %get-tuple-element.61), channel_id=1, source_target_pairs={{0,8},{8,16},{16,24},{24,32},{32,40},{40,48},{48,56},{56,0},{1,9},... | collective-permute-start | bytes 1179656 | tf_op jit(solution)/shard_map/ppermute | solution.py:23
  94.2 12.2 %collective-permute-start.17 = (f32[32,1024]{1,0:T(8,128)S(1)}, f32[32,1024]{1,0:T(8,128)S(1)}, u32[]{:S(2)}, u32[]{:S(2)}) collective-permute-start(f32[32,1024]{1,0:T(8,128)S(1)} %get-tuple-element.88), channel_id=1, source_target_pairs={{0,128},{64,192},{128,0},{192,64},{1,129},{65,193},{129,1},{193,65... | collective-permute-start | bytes 393224 | tf_op jit(solution)/shard_map/ppermute | solution.py:23
  97.2 9.8 %collective-permute-start.16 = (f32[32,1024]{1,0:T(8,128)S(1)}, f32[32,1024]{1,0:T(8,128)S(1)}, u32[]{:S(2)}, u32[]{:S(2)}) collective-permute-start(f32[32,1024]{1,0:T(8,128)S(1)} %get-tuple-element.89), channel_id=1, source_target_pairs={{0,192},{64,0},{128,64},{192,128},{1,193},{65,1},{129,65},{193,129... | collective-permute-start | bytes 393224 | tf_op jit(solution)/shard_map/ppermute | solution.py:23
  98.1 8.9 %collective-permute-start.15 = (f32[32,1024]{1,0:T(8,128)S(1)}, f32[32,1024]{1,0:T(8,128)S(1)}, u32[]{:S(2)}, u32[]{:S(2)}) collective-permute-start(f32[32,1024]{1,0:T(8,128)S(1)} %get-tuple-element.87), channel_id=1, source_target_pairs={{0,64},{64,128},{128,192},{192,0},{1,65},{65,129},{129,193},{193,1... | collective-permute-start | bytes 393224 | tf_op jit(solution)/shard_map/ppermute | solution.py:23
  102.7 6.9 %collective-permute-start.32 = (f32[32,1024]{1,0:T(8,128)S(1)}, f32[32,1024]{1,0:T(8,128)S(1)}, u32[]{:S(2)}, u32[]{:S(2)}) collective-permute-start(f32[32,1024]{1,0:T(8,128)S(1)} %get-tuple-element.97), channel_id=1, source_target_pairs={{0,128},{64,192},{128,0},{192,64},{1,129},{65,193},{129,1},{193,65... | collective-permute-start | bytes 393224 | tf_op jit(solution)/shard_map/ppermute | solution.py:23
  105.5 7.0 %collective-permute-start.31 = (f32[32,1024]{1,0:T(8,128)S(1)}, f32[32,1024]{1,0:T(8,128)S(1)}, u32[]{:S(2)}, u32[]{:S(2)}) collective-permute-start(f32[32,1024]{1,0:T(8,128)S(1)} %get-tuple-element.98), channel_id=1, source_target_pairs={{0,192},{64,0},{128,64},{192,128},{1,193},{65,1},{129,65},{193,129... | collective-permute-start | bytes 393224 | tf_op jit(solution)/shard_map/ppermute | solution.py:23
  106.4 6.1 %collective-permute-start.30 = (f32[32,1024]{1,0:T(8,128)S(1)}, f32[32,1024]{1,0:T(8,128)S(1)}, u32[]{:S(2)}, u32[]{:S(2)}) collective-permute-start(f32[32,1024]{1,0:T(8,128)S(1)} %get-tuple-element.96), channel_id=1, source_target_pairs={{0,64},{64,128},{128,192},{192,0},{1,65},{65,129},{129,193},{193,1... | collective-permute-start | bytes 393224 | tf_op jit(solution)/shard_map/ppermute | solution.py:23
  113.1 7.1 %collective-permute-start.33 = (f32[64,512]{1,0:T(8,128)S(1)}, f32[64,512]{1,0:T(8,128)S(1)}, u32[]{:S(2)}, u32[]{:S(2)}) collective-permute-start(f32[64,512]{1,0:T(8,128)S(1)} %bitcast.118), channel_id=1, source_target_pairs={{0,1},{1,0},{2,3},{3,2},{4,5},{5,4},{6,7},{7,6},{8,9},{9,8},{10,11... | collective-permute-start | bytes 393224 | tf_op jit(solution)/shard_map/ppermute | solution.py:186
  (4 other events, 29.8 us)

commit v3 on v0

v3 whole, which is shorter than its diff:
```python
import functools
import jax
import jax.numpy as jnp
from jax import lax
from jax.experimental import pallas as pl
from jax.experimental.pallas import tpu as pltpu
from jax.sharding import Mesh, PartitionSpec as P

NX, NZ, NY, NC = 4, 8, 4, 2
K = 512
W = 512
SUB = 64
PART = 32
ZORDER = (4, 3, -3, 2, -2, 1, -1, 0)
HEAD = 3
GROUPS = 8


def even(n):
    return [(i, i ^ 1) for i in range(n)]


def odd(n):
    return [(i, (i + 1) % n if i % 2 else (i - 1) % n) for i in range(n)]


def flip(n, bits):
    return [(i, i ^ bits) for i in range(n)]


tie = lax.optimization_barrier


def place_of():
    return tuple(lax.axis_index(name).astype(jnp.int32) for name in "xzyc")


def chunk_kernel(first_k, count, adds, sizes, b0, b1, b2u, b2d, b3, top, low, *refs):
    before, outs, stage = refs[:adds], refs[adds:-1], refs[-1]
    x, z, y, c = place_of()
    sign = 1 - 2 * (z & 1)
    order = [(z + d * sign) & (NZ - 1) for d in ZORDER[first_k:first_k + count]]
    lam = []
    for zz in order:
        lam += [b0[zz], b1[zz], b2u[zz], b2d[zz], b3[zz]]
    lam = jnp.concatenate(lam, axis=0)
    hi = lam.astype(jnp.bfloat16)
    lo = (lam - hi.astype(jnp.float32)).astype(jnp.bfloat16)
    dot = functools.partial(jnp.dot, preferred_element_type=jnp.float32)
    acc = dot(hi, top[...]) + (dot(lo, top[...]) + dot(hi, low[...]))
    cols = y * 2 * W + lax.broadcasted_iota(jnp.int32, (1, 2 * W), 1)
    first = jnp.zeros((1, 2 * W), jnp.int32)
    last = first
    begin = jnp.int32(0)
    for g in range(GROUPS):
        end = begin + sizes[g]
        inside = (cols >= begin) & (cols < end)
        first = jnp.where(inside, begin, first)
        last = jnp.where(inside, end, last)
        begin = end
    place = c * SUB + (x & 1) * PART + lax.broadcasted_iota(jnp.int32, (PART, 1), 0)
    for k, zz in enumerate(order):
        for rel in range(NY):
            xp = y ^ rel
            row = place + (xp * 1024 + zz * 128)
            at = (k * NY + rel) * PART
            stage[xp] = jnp.where((row >= first) & (row < last), acc[at:at + PART], 0.0)
        for slot in range(3):
            value = stage[0] + stage[3] if slot == 0 else stage[slot]
            for h in range(2):
                piece = value[:, h * W:(h + 1) * W]
                if adds:
                    piece = piece + before[h][first_k + k, slot]
                outs[h][k, slot] = piece


def chunks(sizes, blocks, t2_parts, before, first_k, count):
    whole = pl.BlockSpec(memory_space=pltpu.VMEM)
    return pl.pallas_call(
        functools.partial(chunk_kernel, first_k, count, len(before)),
        out_shape=[jax.ShapeDtypeStruct((count, 3, PART, W), jnp.float32)] * 2,
        in_specs=[pl.BlockSpec(memory_space=pltpu.SMEM)] + [whole] * (7 + len(before)),
        out_specs=[whole, whole],
        scratch_shapes=[pltpu.VMEM((NX, PART, 2 * W), jnp.float32)],
        compiler_params=pltpu.CompilerParams(vmem_limit_bytes=20 * 1024 * 1024),
        cost_estimate=pl.CostEstimate(
            flops=2 * 3 * count * 4 * PART * K * 2 * W,
            bytes_accessed=count * 4 * PART * K * 4 + 4 * K * 2 * W + count * 3 * PART * 2 * W * 4,
            transcendentals=0,
        ),
    )(sizes, *blocks, *t2_parts, *before)


def add_left(full, left):
    n = left.shape[-1]
    return jnp.concatenate([full[..., :n] + left, full[..., n:]], axis=-1)


def add_right(full, right):
    n = full.shape[-1] - right.shape[-1]
    return jnp.concatenate([full[..., :n], full[..., n:] + right], axis=-1)


def step(value, other, axis, n):
    return lax.ppermute(value, axis, even(n)), lax.ppermute(other, axis, odd(n))


def z_phase(part):
    half = part[0].shape[-1] // 2
    one, two = step(part[0][..., :half], part[0][..., half:], "z", NZ)
    one, two = tie((one, two))
    one, two = step(*tie((add_right(part[1], two), add_left(part[2], one))), "z", NZ)
    for k in (3, 5):
        one, two = tie((one, two))
        one, two = step(*tie((part[k] + two, part[k + 1] + one)), "z", NZ)
    return part[7] + one + two


def split_kernel(masked, count, mine, other, top, low):
    live = lax.broadcasted_iota(jnp.int32, (K, 1), 0) < (count[0] if masked else K)
    c = lax.axis_index("c")

    def put(ref, at):
        value = jnp.where(live, ref[...], 0.0)
        hi = value.astype(jnp.bfloat16)
        top[:, at:at + W] = hi
        low[:, at:at + W] = (value - hi.astype(jnp.float32)).astype(jnp.bfloat16)

    @pl.when(c == 0)
    def _():
        put(mine, 0)
        put(other, W)

    @pl.when(c != 0)
    def _():
        put(other, 0)
        put(mine, W)


def split(masked, count, mine, other):
    whole = pl.BlockSpec(memory_space=pltpu.VMEM)
    return pl.pallas_call(
        functools.partial(split_kernel, masked),
        out_shape=[jax.ShapeDtypeStruct((K, 2 * W), jnp.bfloat16)] * 2,
        in_specs=[pl.BlockSpec(memory_space=pltpu.SMEM), whole, whole],
        out_specs=[whole, whole],
        compiler_params=pltpu.CompilerParams(vmem_limit_bytes=8 * 1024 * 1024),
        cost_estimate=pl.CostEstimate(flops=0, bytes_accessed=16 * K * W, transcendentals=0),
    )(count, mine, other)


def finish_kernel(sizes, mine, other, out):
    x, z, y, c = place_of()
    col = y * 2 * W + c * W + lax.broadcasted_iota(jnp.int32, (1, W), 1)
    first = jnp.zeros((1, W), jnp.int32)
    last = first
    begin = jnp.int32(0)
    for g in range(GROUPS):
        end = begin + sizes[g]
        inside = (col >= begin) & (col < end)
        first = jnp.where(inside, begin, first)
        last = jnp.where(inside, end, last)
        begin = end

    def put(ref, at):
        row = x * 1024 + z * 128 + at + lax.broadcasted_iota(jnp.int32, (SUB, 1), 0)
        out[at:at + SUB] = jnp.where((row >= first) & (row < last), ref[...], 0.0)

    @pl.when(c == 0)
    def _():
        put(mine, 0)
        put(other, SUB)

    @pl.when(c != 0)
    def _():
        put(other, 0)
        put(mine, SUB)


def finish(sizes, mine, other):
    whole = pl.BlockSpec(memory_space=pltpu.VMEM)
    return pl.pallas_call(
        finish_kernel,
        out_shape=jax.ShapeDtypeStruct((2 * SUB, W), jnp.float32),
        in_specs=[pl.BlockSpec(memory_space=pltpu.SMEM), whole, whole],
        out_specs=whole,
        compiler_params=pltpu.CompilerParams(vmem_limit_bytes=4 * 1024 * 1024),
        cost_estimate=pl.CostEstimate(flops=0, bytes_accessed=16 * SUB * W, transcendentals=0),
    )(sizes, mine, other)


def body(t2_amps, lambda_amps, live_pairs, block_sizes):
    x, c = (lax.axis_index(name).astype(jnp.int32) for name in "xc")
    swap = flip(NC, 1)
    places = [c, 1 - c, x & 1, 1 - (x & 1)] + [lax.rem(x ^ d, 3) for d in range(NX)]
    places = [place.astype(jnp.uint32) for place in places]
    lambda_amps, places, low_c, low_p = tie((lambda_amps, places, c == 0, (x & 1) == 0))
    c, not_c, p, not_p, *slots = places
    pick = lambda a, i, axis: lax.dynamic_index_in_dim(a, i, axis, keepdims=False, allow_negative_indices=False)

    def both(at, mine, other, axis):
        return jnp.where(at, jnp.concatenate([mine, other], axis), jnp.concatenate([other, mine], axis))

    lam_rows = lambda_amps.T.reshape(4, NC, SUB, K)
    keep, give = pick(lam_rows, c, 1), pick(lam_rows, not_c, 1)
    live = jnp.arange(K, dtype=jnp.int32)[:, None] < live_pairs[0]
    near = both(low_c, keep, lax.ppermute(give, "c", swap), 0).reshape(NZ, 2, PART, K)
    own = pick(near, p, 1)
    one, two = step(own, own, "y", NY)
    pair = lax.ppermute(pick(near, not_p, 1), "x", flip(NX, 1))

    t2_send, _ = tie((t2_amps, pair))
    t2_par = lax.ppermute(jnp.where(live, t2_send, 0.0), "x", flip(NX, 1))
    t2_own = split(True, live_pairs, t2_amps, lax.ppermute(t2_amps, "c", swap))

    half = PART // 2
    fars = two[:, half:], one[:, :half]
    pair, _ = tie((pair, (fars, t2_own)))
    far_down, far_up = step(*fars, "y", NY)
    blocks = (own, one, far_up, far_down, two)
    one, two = step(pair, pair, "y", NY)
    first = chunks(block_sizes, blocks, t2_own, (), 0, NZ)

    fars = two[:, half:], one[:, :half]
    fars, _ = tie((fars, (far_down, far_up)))
    t2_par, _ = tie((t2_par, fars))
    t2_both, _ = tie(((t2_par, lax.ppermute(t2_par, "c", swap)), first))
    t2_par = split(False, live_pairs, *t2_both)
    far_down, far_up = step(*fars, "y", NY)
    blocks = (pair, one, far_up, far_down, two)
    head = chunks(block_sizes, blocks, t2_par, first, 0, HEAD)
    tail = chunks(block_sizes, blocks, t2_par, first, HEAD, NZ - HEAD)

    done = []
    for h in range(2):
        got = z_phase([head[h][k] for k in range(HEAD)] + [tail[h][k] for k in range(NZ - HEAD)])
        slot = lambda d: pick(got, slots[d], 0)
        far = lax.ppermute(slot(2), "x", flip(NX, 2))
        near = lax.ppermute(slot(1), "x", flip(NX, 1))
        wrap = lax.ppermute(slot(3), "x", flip(NX, 3))
        done.append(both(low_p, slot(0) + far, near + wrap, 0))

    mine = jnp.where(low_c, done[0], done[1])
    other = lax.ppermute(jnp.where(low_c, done[1], done[0]), "c", swap)
    return finish(block_sizes, mine, other)


def solution(mesh):
    fine = Mesh(mesh.devices.reshape(NX, NZ, NY, NC), ("x", "z", "y", "c"))
    spec = P(("x", "z"), ("y", "c"))
    return jax.shard_map(
        body,
        mesh=fine,
        in_specs=(spec, spec, P(("x", "z")), P()),
        out_specs=spec,
        check_vma=False,
    )
```

time: 353 us -> 114 us (0.32)
  waiting for transfers between devices: 304 us -> 52 us
  starting transfers between devices: 0.04 us -> 45.2 us
  matrix products: 23.6 us -> 0 us
  between operations: 14.1 us -> 1.05 us
  Pallas kernels: 0 us -> 12 us
    reduce_scatter x1 -> x0, waiting for transfers between devices: 247 us -> none  [body(): lax.psum_scatter(lax.fori_loop(first_blk, last_blk, add_block, jnp.zeros(...]
    all_gather x1 -> x0, waiting for transfers between devices: 56.4 us -> none  [body(): full_lambda = lax.all_gather(lambda_amps, 'vir', axis=1, tiled=True)]
    ppermute x0 -> x36, waiting for transfers between devices: none -> 52 us  [the longest x12 23.2 us: step(): lax.ppermute(other, axis, odd(n))]
    ppermute x0 -> x36, starting transfers between devices: none -> 45.2 us  [the longest x12 18.3 us: step(): lax.ppermute(other, axis, odd(n))]
    dot_general x2 -> x0, matrix products: 23.6 us -> none  [add_block(): lax.dot_general(lam_block, amp_block, (((0,), (0,)), ((), ())), precision...]
    pallas_call x0 -> x6, Pallas kernels: none -> 12 us  [the longest x3 9.92 us: chunks(): pl.pallas_call(functools.partial(chunk_kernel, first_k, count, len(before...]
    broadcast_in_dim x1 -> x0, local copies, waits for them, and re-layouts: 4.28 us -> none  [body(): jnp.zeros((count, cols), jnp.float32)]
  transfers between devices with their start and end apart: 2 -> 36, of which waited for: 2 -> 22; matrix products, arithmetic and copies ran while one was open for 0% -> 1% of each run, Pallas kernels for 0% -> 7%
where the time goes in v3:
time: 114 us
  waiting for transfers between devices  52 us (46%)
  starting transfers between devices  45.2 us (40%)
  Pallas kernels  12 us (11%)
  local copies, waits for them, and re-layouts  3.04 us (3%)
    ppermute x12, waiting for transfers between devices, step(): lax.ppermute(other, axis, odd(n))  23.2 us
    ppermute x12, starting transfers between devices, step(): lax.ppermute(other, axis, odd(n))  18.3 us
    ppermute x12, waiting for transfers between devices, step(): lax.ppermute(value, axis, even(n))  12.2 us
    pallas_call x3, Pallas kernels, chunks(): pl.pallas_call(functools.partial(chunk_kernel, first_k, count, len(before...  9.92 us
    ppermute x1, waiting for transfers between devices, body(): pair = lax.ppermute(pick(near, not_p, 1), 'x', flip(NX, 1))  9.52 us
    ppermute x1, starting transfers between devices, body(): other = lax.ppermute(jnp.where(low_c, done[1], done[0]), 'c', swap)  8.35 us
    ppermute x12, starting transfers between devices, step(): lax.ppermute(value, axis, even(n))  5.6 us
    ppermute x2, waiting for transfers between devices, body(): far = lax.ppermute(slot(2), 'x', flip(NX, 2))  4.56 us
  transfers between devices with their start and end apart: 36, of which 22 were waited for; matrix products, arithmetic and copies ran while one was open for 1% of the time, Pallas kernels for 7%

profile of v3, /device:TPU:1, one launch (start us, length us, event | category | flops | bytes accessed | tf_op | source)
XLA Modules:
  0.0 114.1 jit_solution(7708659993295388137)
XLA Ops:
  0.0 1.6 %copy.5 = f32[512,512]{0,1:T(8,128)S(1)} copy(f32[512,512]{1,0:T(8,128)} %param.5) | data formatting | bytes 2097152 | tf_op jit(solution)/shard_map/optimization_barrier | solution.py:197
  1.7 3.3 %collective-permute-start = (f32[4,64,512]{2,1,0:T(8,128)S(1)}, f32[4,64,512]{2,1,0:T(8,128)S(1)}, u32[]{:S(2)}, u32[]{:S(2)}) collective-permute-start(f32[4,64,512]{2,1,0:T(8,128)S(1)} %get-tuple-element.112), channel_id=1, source_target_pairs={{0,1},{1,0},{2,3},{3,2},{4,5},{5,4},{6,7},{7,6},{8,9},{9,8},{10,11... | collective-permute-start | bytes 1572872 | tf_op jit(solution)/shard_map/ppermute | solution.py:207
  5.0 1.5 %collective-permute-done = f32[4,64,512]{2,1,0:T(8,128)S(1)} collective-permute-done((f32[4,64,512]{2,1,0:T(8,128)S(1)}, f32[4,64,512]{2,1,0:T(8,128)S(1)}, u32[]{:S(2)}, u32[]{:S(2)}) %collective-permute-start) | collective-permute-done | bytes 524320 | tf_op jit(solution)/shard_map/ppermute | solution.py:207
  8.9 1.5 %collective-permute-start.2 = (f32[8,32,512]{2,1,0:T(8,128)S(1)}, f32[8,32,512]{2,1,0:T(8,128)S(1)}, u32[]{:S(2)}, u32[]{:S(2)}) collective-permute-start(f32[8,32,512]{2,1,0:T(8,128)S(1)} %get-tuple-element.109.b0), channel_id=1, source_target_pairs={{0,6},{2,4},{4,2},{6,0},{1,7},{3,5},{5,3},{7,1},{8,14},{10,12},{12... | collective-permute-start | bytes 1572872 | tf_op jit(solution)/shard_map/ppermute | solution.py:105
  10.5 9.5 %collective-permute-done.1.b0 = f32[8,32,512]{2,1,0:T(8,128)S(1)} collective-permute-done((f32[8,32,512]{2,1,0:T(8,128)S(1)}, f32[8,32,512]{2,1,0:T(8,128)S(1)}, u32[]{:S(2)}, u32[]{:S(2)}) %collective-permute-start.1) | collective-permute-done | bytes 524320 | tf_op jit(solution)/shard_map/ppermute | solution.py:210
  20.5 3.1 %collective-permute-done.2.b3 = f32[8,32,512]{2,1,0:T(8,128)S(1)} collective-permute-done((f32[8,32,512]{2,1,0:T(8,128)S(1)}, f32[8,32,512]{2,1,0:T(8,128)S(1)}, u32[]{:S(2)}, u32[]{:S(2)}) %collective-permute-start.2) | collective-permute-done | bytes 524320 | tf_op jit(solution)/shard_map/ppermute | solution.py:105
  24.2 1.7 %collective-permute-start.6 = (f32[8,32,512]{2,1,0:T(8,128)S(1)}, f32[8,32,512]{2,1,0:T(8,128)S(1)}, u32[]{:S(2)}, u32[]{:S(2)}) collective-permute-start(f32[8,32,512]{2,1,0:T(8,128)S(1)} %collective-permute-done.1.b0), channel_id=1, source_target_pairs={{0,6},{2,4},{4,2},{6,0},{1,7},{3,5},{5,3},{7,1},{8,14},{10,12},{12... | collective-permute-start | bytes 1572872 | tf_op jit(solution)/shard_map/ppermute | solution.py:105
  25.9 1.5 %collective-permute-start.7 = (f32[8,16,512]{2,1,0:T(8,128)S(1)}, f32[8,16,512]{2,1,0:T(8,128)S(1)}, u32[]{:S(2)}, u32[]{:S(2)}) collective-permute-start(f32[8,16,512]{2,1,0:T(8,128)S(1)} %slice.128), channel_id=1, source_target_pairs={{0,2},{2,0},{4,6},{6,4},{1,3},{3,1},{5,7},{7,5},{8,10},{10,8},{12,... | collective-permute-start | bytes 786440 | tf_op jit(solution)/shard_map/ppermute | solution.py:105
  28.4 9.4 %collective-permute-done.6.b3 = f32[8,32,512]{2,1,0:T(8,128)S(1)} collective-permute-done((f32[8,32,512]{2,1,0:T(8,128)S(1)}, f32[8,32,512]{2,1,0:T(8,128)S(1)}, u32[]{:S(2)}, u32[]{:S(2)}) %collective-permute-start.6) | collective-permute-done | bytes 524320 | tf_op jit(solution)/shard_map/ppermute | solution.py:105
  38.2 5.6 %collective-permute-done.7.b2d = f32[8,16,512]{2,1,0:T(8,128)S(1)} collective-permute-done((f32[8,16,512]{2,1,0:T(8,128)S(1)}, f32[8,16,512]{2,1,0:T(8,128)S(1)}, u32[]{:S(2)}, u32[]{:S(2)}) %collective-permute-start.7) | collective-permute-done | bytes 262176 | tf_op jit(solution)/shard_map/ppermute | solution.py:105
  43.8 2.0 %collective-permute-start.12 = (f32[512,512]{1,0:T(8,128)S(1)}, f32[512,512]{1,0:T(8,128)S(1)}, u32[]{:S(2)}, u32[]{:S(2)}) collective-permute-start(f32[512,512]{1,0:T(8,128)S(1)} %collective-permute-done.11.mine), channel_id=1, source_target_pairs={{0,1},{1,0},{2,3},{3,2},{4,5},{5,4},{6,7},{7,6},{8,9},{9,8},{10,11... | collective-permute-start | bytes 3145736 | tf_op jit(solution)/shard_map/ppermute | solution.py:227
  45.8 1.4 %collective-permute-start.9 = (f32[8,16,512]{2,1,0:T(8,128)S(1)}, f32[8,16,512]{2,1,0:T(8,128)S(1)}, u32[]{:S(2)}, u32[]{:S(2)}) collective-permute-start(f32[8,16,512]{2,1,0:T(8,128)S(1)} %slice.131), channel_id=1, source_target_pairs={{0,6},{2,4},{4,2},{6,0},{1,7},{3,5},{5,3},{7,1},{8,14},{10,12},{12... | collective-permute-start | bytes 786440 | tf_op jit(solution)/shard_map/ppermute | solution.py:105
  47.3 4.5 %shard_map.47 = (f32[8,3,32,512]{3,2,1,0:T(8,128)S(1)}, f32[8,3,32,512]{3,2,1,0:T(8,128)S(1)}) custom-call(s32[8]{0:T(128)S(1)} %copy-done.1, f32[8,32,512]{2,1,0:T(8,128)S(1)} %get-tuple-element.109.b0, f32[8,32,512]{2,1,0:T(8,128)S(1)} %collective-permute-done.3.b1, f32[8,16,512]{2,1,0:T(8,128)S(1)} %collective-permute-done.8.b2u, ...), custom_call_target="tpu_custom_call" | custom-call | flops 3221225472 | bytes 7340032 | tf_op jit(solution)/shard_map/pallas_call | solution.py:79
  52.1 1.5 %collective-permute-done.10.b2d = f32[8,16,512]{2,1,0:T(8,128)S(1)} collective-permute-done((f32[8,16,512]{2,1,0:T(8,128)S(1)}, f32[8,16,512]{2,1,0:T(8,128)S(1)}, u32[]{:S(2)}, u32[]{:S(2)}) %collective-permute-start.10) | collective-permute-done | bytes 262176 | tf_op jit(solution)/shard_map/ppermute | solution.py:105
  54.6 2.2 %shard_map.50 = (f32[3,3,32,512]{3,2,1,0:T(8,128)S(1)}, f32[3,3,32,512]{3,2,1,0:T(8,128)S(1)}) custom-call(s32[8]{0:T(128)S(1)} %copy-done.1, f32[8,32,512]{2,1,0:T(8,128)S(1)} %collective-permute-done.1.b0, f32[8,32,512]{2,1,0:T(8,128)S(1)} %collective-permute-done.5.b1, f32[8,16,512]{2,1,0:T(8,128)S(1)} %collective-permute-done.9.b2u, ...), custom_call_target="tpu_custom_call" | custom-call | flops 1207959552 | bytes 4063232 | tf_op jit(solution)/shard_map/pallas_call | solution.py:79
  56.9 1.7 %collective-permute-start.13 = (f32[3,32,256]{2,1,0:T(8,128)S(1)}, f32[3,32,256]{2,1,0:T(8,128)S(1)}, u32[]{:S(2)}, u32[]{:S(2)}) collective-permute-start(f32[3,32,256]{2,1,0:T(8,128)S(1)} %get-tuple-element.137), channel_id=1, source_target_pairs={{0,8},{8,0},{16,24},{24,16},{32,40},{40,32},{48,56},{56,48},{1,9},... | collective-permute-start | bytes 294920 | tf_op jit(solution)/shard_map/ppermute | solution.py:105
  58.7 4.7 %collective-permute-start.14 = (f32[3,32,256]{2,1,0:T(8,128)S(1)}, f32[3,32,256]{2,1,0:T(8,128)S(1)}, u32[]{:S(2)}, u32[]{:S(2)}) collective-permute-start(f32[3,32,256]{2,1,0:T(8,128)S(1)} %get-tuple-element.136), channel_id=1, source_target_pairs={{0,56},{8,16},{16,8},{24,32},{32,24},{40,48},{48,40},{56,0},{1,57}... | collective-permute-start | bytes 294920 | tf_op jit(solution)/shard_map/ppermute | solution.py:105
  63.4 1.4 %collective-permute-start.25 = (f32[3,32,256]{2,1,0:T(8,128)S(1)}, f32[3,32,256]{2,1,0:T(8,128)S(1)}, u32[]{:S(2)}, u32[]{:S(2)}) collective-permute-start(f32[3,32,256]{2,1,0:T(8,128)S(1)} %get-tuple-element.145), channel_id=1, source_target_pairs={{0,56},{8,16},{16,8},{24,32},{32,24},{40,48},{48,40},{56,0},{1,57}... | collective-permute-start | bytes 294920 | tf_op jit(solution)/shard_map/ppermute | solution.py:105
  64.9 3.2 %shard_map.49 = (f32[5,3,32,512]{3,2,1,0:T(8,128)S(1)}, f32[5,3,32,512]{3,2,1,0:T(8,128)S(1)}) custom-call(s32[8]{0:T(128)S(1)} %copy-done.1, f32[8,32,512]{2,1,0:T(8,128)S(1)} %collective-permute-done.1.b0, f32[8,32,512]{2,1,0:T(8,128)S(1)} %collective-permute-done.5.b1, f32[8,16,512]{2,1,0:T(8,128)S(1)} %collective-permute-done.9.b2u, ...), custom_call_target="tpu_custom_call" | custom-call | flops 2013265920 | bytes 5373952 | tf_op jit(solution)/shard_map/pallas_call | solution.py:79
  72.8 1.9 %collective-permute-done.16 = f32[3,32,512]{2,1,0:T(8,128)S(1)} collective-permute-done((f32[3,32,512]{2,1,0:T(8,128)S(1)}, f32[3,32,512]{2,1,0:T(8,128)S(1)}, u32[]{:S(2)}, u32[]{:S(2)}) %collective-permute-start.16) | collective-permute-done | bytes 196640 | tf_op jit(solution)/shard_map/ppermute | solution.py:105
  76.6 1.7 %collective-permute-done.27 = f32[3,32,512]{2,1,0:T(8,128)S(1)} collective-permute-done((f32[3,32,512]{2,1,0:T(8,128)S(1)}, f32[3,32,512]{2,1,0:T(8,128)S(1)}, u32[]{:S(2)}, u32[]{:S(2)}) %collective-permute-start.27) | collective-permute-done | bytes 196640 | tf_op jit(solution)/shard_map/ppermute | solution.py:105
  78.4 1.8 %collective-permute-start.29 = (f32[3,32,512]{2,1,0:T(8,128)S(1)}, f32[3,32,512]{2,1,0:T(8,128)S(1)}, u32[]{:S(2)}, u32[]{:S(2)}) collective-permute-start(f32[3,32,512]{2,1,0:T(8,128)S(1)} %get-tuple-element.104), channel_id=1, source_target_pairs={{0,56},{8,16},{16,8},{24,32},{32,24},{40,48},{48,40},{56,0},{1,57}... | collective-permute-start | bytes 589832 | tf_op jit(solution)/shard_map/ppermute | solution.py:105
  80.2 1.4 %collective-permute-done.17 = f32[3,32,512]{2,1,0:T(8,128)S(1)} collective-permute-done((f32[3,32,512]{2,1,0:T(8,128)S(1)}, f32[3,32,512]{2,1,0:T(8,128)S(1)}, u32[]{:S(2)}, u32[]{:S(2)}) %collective-permute-start.17) | collective-permute-done | bytes 196640 | tf_op jit(solution)/shard_map/ppermute | solution.py:105
  81.6 1.9 %collective-permute-done.18 = f32[3,32,512]{2,1,0:T(8,128)S(1)} collective-permute-done((f32[3,32,512]{2,1,0:T(8,128)S(1)}, f32[3,32,512]{2,1,0:T(8,128)S(1)}, u32[]{:S(2)}, u32[]{:S(2)}) %collective-permute-start.18) | collective-permute-done | bytes 196640 | tf_op jit(solution)/shard_map/ppermute | solution.py:105
  84.5 2.1 %collective-permute-done.29 = f32[3,32,512]{2,1,0:T(8,128)S(1)} collective-permute-done((f32[3,32,512]{2,1,0:T(8,128)S(1)}, f32[3,32,512]{2,1,0:T(8,128)S(1)}, u32[]{:S(2)}, u32[]{:S(2)}) %collective-permute-start.29) | collective-permute-done | bytes 196640 | tf_op jit(solution)/shard_map/ppermute | solution.py:105
  87.5 2.0 %collective-permute-done.19 = f32[3,32,512]{2,1,0:T(8,128)S(1)} collective-permute-done((f32[3,32,512]{2,1,0:T(8,128)S(1)}, f32[3,32,512]{2,1,0:T(8,128)S(1)}, u32[]{:S(2)}, u32[]{:S(2)}) %collective-permute-start.19) | collective-permute-done | bytes 196640 | tf_op jit(solution)/shard_map/ppermute | solution.py:105
  89.5 1.5 %collective-permute-done.20 = f32[3,32,512]{2,1,0:T(8,128)S(1)} collective-permute-done((f32[3,32,512]{2,1,0:T(8,128)S(1)}, f32[3,32,512]{2,1,0:T(8,128)S(1)}, u32[]{:S(2)}, u32[]{:S(2)}) %collective-permute-start.20) | collective-permute-done | bytes 196640 | tf_op jit(solution)/shard_map/ppermute | solution.py:105
  92.0 1.9 %collective-permute-start.23 = (f32[32,512]{1,0:T(8,128)S(1)}, f32[32,512]{1,0:T(8,128)S(1)}, u32[]{:S(2)}, u32[]{:S(2)}) collective-permute-start(f32[32,512]{1,0:T(8,128)S(1)} %get-tuple-element.129), channel_id=1, source_target_pairs={{0,192},{64,128},{128,64},{192,0},{1,193},{65,129},{129,65},{193,1... | collective-permute-start | bytes 196616 | tf_op jit(solution)/shard_map/ppermute | solution.py:240
  96.3 1.9 %collective-permute-start.34 = (f32[32,512]{1,0:T(8,128)S(1)}, f32[32,512]{1,0:T(8,128)S(1)}, u32[]{:S(2)}, u32[]{:S(2)}) collective-permute-start(f32[32,512]{1,0:T(8,128)S(1)} %get-tuple-element.138), channel_id=1, source_target_pairs={{0,192},{64,128},{128,64},{192,0},{1,193},{65,129},{129,65},{193,1... | collective-permute-start | bytes 196616 | tf_op jit(solution)/shard_map/ppermute | solution.py:240
  99.1 4.2 %collective-permute-done.32 = f32[32,512]{1,0:T(8,128)S(1)} collective-permute-done((f32[32,512]{1,0:T(8,128)S(1)}, f32[32,512]{1,0:T(8,128)S(1)}, u32[]{:S(2)}, u32[]{:S(2)}) %collective-permute-start.32) | collective-permute-done | bytes 65568 | tf_op jit(solution)/shard_map/ppermute | solution.py:238
  103.4 8.3 %collective-permute-start.35 = (f32[64,512]{1,0:T(8,128)S(1)}, f32[64,512]{1,0:T(8,128)S(1)}, u32[]{:S(2)}, u32[]{:S(2)}) collective-permute-start(f32[64,512]{1,0:T(8,128)S(1)} %get-tuple-element.127), channel_id=1, source_target_pairs={{0,1},{1,0},{2,3},{3,2},{4,5},{5,4},{6,7},{7,6},{8,9},{9,8},{10,11... | collective-permute-start | bytes 393224 | tf_op jit(solution)/shard_map/ppermute | solution.py:244
  112.7 1.3 %shard_map.51 = f32[128,512]{1,0:T(8,128)} custom-call(s32[8]{0:T(128)S(1)} %copy-done.1, f32[64,512]{1,0:T(8,128)S(1)} %get-tuple-element.128.mine, f32[64,512]{1,0:T(8,128)S(1)} %collective-permute-done.35.other), custom_call_target="tpu_custom_call" | custom-call | bytes 524288 | tf_op jit(solution)/shard_map/pallas_call | solution.py:182
  (84 shorter events, 19.8 us)
Async XLA Ops:
  6.8 13.2 %collective-permute-start.1 = (f32[8,32,512]{2,1,0:T(8,128)S(1)}, f32[8,32,512]{2,1,0:T(8,128)S(1)}, u32[]{:S(2)}, u32[]{:S(2)}) collective-permute-start(f32[8,32,512]{2,1,0:T(8,128)S(1)} %get-tuple-element.110), channel_id=1, source_target_pairs={{0,64},{64,0},{128,192},{192,128},{1,65},{65,1},{129,193},{193,129... | collective-permute-start | bytes 1572872 | tf_op jit(solution)/shard_map/ppermute | solution.py:210
  7.9 15.8 %collective-permute-start.4 = (f32[512,512]{1,0:T(8,128)S(1)}, f32[512,512]{1,0:T(8,128)S(1)}, u32[]{:S(2)}, u32[]{:S(2)}) collective-permute-start(f32[512,512]{1,0:T(8,128)S(1)} %copy-done), channel_id=1, source_target_pairs={{0,1},{1,0},{2,3},{3,2},{4,5},{5,4},{6,7},{7,6},{8,9},{9,8},{10,11... | collective-permute-start | bytes 3145736 | tf_op jit(solution)/shard_map/ppermute | solution.py:214
  8.9 14.7 %collective-permute-start.2 = (f32[8,32,512]{2,1,0:T(8,128)S(1)}, f32[8,32,512]{2,1,0:T(8,128)S(1)}, u32[]{:S(2)}, u32[]{:S(2)}) collective-permute-start(f32[8,32,512]{2,1,0:T(8,128)S(1)} %get-tuple-element.109.b0), channel_id=1, source_target_pairs={{0,6},{2,4},{4,2},{6,0},{1,7},{3,5},{5,3},{7,1},{8,14},{10,12},{12... | collective-permute-start | bytes 1572872 | tf_op jit(solution)/shard_map/ppermute | solution.py:105
  10.5 13.2 %collective-permute-start.3 = (f32[8,32,512]{2,1,0:T(8,128)S(1)}, f32[8,32,512]{2,1,0:T(8,128)S(1)}, u32[]{:S(2)}, u32[]{:S(2)}) collective-permute-start(f32[8,32,512]{2,1,0:T(8,128)S(1)} %get-tuple-element.109.b0), channel_id=1, source_target_pairs={{0,2},{2,0},{4,6},{6,4},{1,3},{3,1},{5,7},{7,5},{8,10},{10,8},{12,... | collective-permute-start | bytes 1572872 | tf_op jit(solution)/shard_map/ppermute | solution.py:105
  20.1 23.7 %collective-permute-start.11 = (f32[512,512]{1,0:T(8,128)S(1)}, f32[512,512]{1,0:T(8,128)S(1)}, u32[]{:S(2)}, u32[]{:S(2)}) collective-permute-start(f32[512,512]{1,0:T(8,128)S(1)} %broadcast_select_fusion), channel_id=1, source_target_pairs={{0,64},{64,0},{128,192},{192,128},{1,65},{65,1},{129,193},{193,129... | collective-permute-start | bytes 3145736 | tf_op jit(solution)/shard_map/ppermute | solution.py:213
  24.2 13.6 %collective-permute-start.6 = (f32[8,32,512]{2,1,0:T(8,128)S(1)}, f32[8,32,512]{2,1,0:T(8,128)S(1)}, u32[]{:S(2)}, u32[]{:S(2)}) collective-permute-start(f32[8,32,512]{2,1,0:T(8,128)S(1)} %collective-permute-done.1.b0), channel_id=1, source_target_pairs={{0,6},{2,4},{4,2},{6,0},{1,7},{3,5},{5,3},{7,1},{8,14},{10,12},{12... | collective-permute-start | bytes 1572872 | tf_op jit(solution)/shard_map/ppermute | solution.py:105
  25.9 12.3 %collective-permute-start.5 = (f32[8,32,512]{2,1,0:T(8,128)S(1)}, f32[8,32,512]{2,1,0:T(8,128)S(1)}, u32[]{:S(2)}, u32[]{:S(2)}) collective-permute-start(f32[8,32,512]{2,1,0:T(8,128)S(1)} %collective-permute-done.1.b0), channel_id=1, source_target_pairs={{0,2},{2,0},{4,6},{6,4},{1,3},{3,1},{5,7},{7,5},{8,10},{10,8},{12,... | collective-permute-start | bytes 1572872 | tf_op jit(solution)/shard_map/ppermute | solution.py:105
  25.9 18.0 %collective-permute-start.7 = (f32[8,16,512]{2,1,0:T(8,128)S(1)}, f32[8,16,512]{2,1,0:T(8,128)S(1)}, u32[]{:S(2)}, u32[]{:S(2)}) collective-permute-start(f32[8,16,512]{2,1,0:T(8,128)S(1)} %slice.128), channel_id=1, source_target_pairs={{0,2},{2,0},{4,6},{6,4},{1,3},{3,1},{5,7},{7,5},{8,10},{10,8},{12,... | collective-permute-start | bytes 786440 | tf_op jit(solution)/shard_map/ppermute | solution.py:105
  27.3 16.5 %collective-permute-start.8 = (f32[8,16,512]{2,1,0:T(8,128)S(1)}, f32[8,16,512]{2,1,0:T(8,128)S(1)}, u32[]{:S(2)}, u32[]{:S(2)}) collective-permute-start(f32[8,16,512]{2,1,0:T(8,128)S(1)} %slice.129), channel_id=1, source_target_pairs={{0,6},{2,4},{4,2},{6,0},{1,7},{3,5},{5,3},{7,1},{8,14},{10,12},{12... | collective-permute-start | bytes 786440 | tf_op jit(solution)/shard_map/ppermute | solution.py:105
  43.8 8.0 %collective-permute-start.12 = (f32[512,512]{1,0:T(8,128)S(1)}, f32[512,512]{1,0:T(8,128)S(1)}, u32[]{:S(2)}, u32[]{:S(2)}) collective-permute-start(f32[512,512]{1,0:T(8,128)S(1)} %collective-permute-done.11.mine), channel_id=1, source_target_pairs={{0,1},{1,0},{2,3},{3,2},{4,5},{5,4},{6,7},{7,6},{8,9},{9,8},{10,11... | collective-permute-start | bytes 3145736 | tf_op jit(solution)/shard_map/ppermute | solution.py:227
  45.8 7.9 %collective-permute-start.10 = (f32[8,16,512]{2,1,0:T(8,128)S(1)}, f32[8,16,512]{2,1,0:T(8,128)S(1)}, u32[]{:S(2)}, u32[]{:S(2)}) collective-permute-start(f32[8,16,512]{2,1,0:T(8,128)S(1)} %slice.130), channel_id=1, source_target_pairs={{0,2},{2,0},{4,6},{6,4},{1,3},{3,1},{5,7},{7,5},{8,10},{10,8},{12,... | collective-permute-start | bytes 786440 | tf_op jit(solution)/shard_map/ppermute | solution.py:105
  45.8 8.7 %collective-permute-start.9 = (f32[8,16,512]{2,1,0:T(8,128)S(1)}, f32[8,16,512]{2,1,0:T(8,128)S(1)}, u32[]{:S(2)}, u32[]{:S(2)}) collective-permute-start(f32[8,16,512]{2,1,0:T(8,128)S(1)} %slice.131), channel_id=1, source_target_pairs={{0,6},{2,4},{4,2},{6,0},{1,7},{3,5},{5,3},{7,1},{8,14},{10,12},{12... | collective-permute-start | bytes 786440 | tf_op jit(solution)/shard_map/ppermute | solution.py:105
  56.9 11.2 %collective-permute-start.13 = (f32[3,32,256]{2,1,0:T(8,128)S(1)}, f32[3,32,256]{2,1,0:T(8,128)S(1)}, u32[]{:S(2)}, u32[]{:S(2)}) collective-permute-start(f32[3,32,256]{2,1,0:T(8,128)S(1)} %get-tuple-element.137), channel_id=1, source_target_pairs={{0,8},{8,0},{16,24},{24,16},{32,40},{40,32},{48,56},{56,48},{1,9},... | collective-permute-start | bytes 294920 | tf_op jit(solution)/shard_map/ppermute | solution.py:105
  58.7 9.5 %collective-permute-start.14 = (f32[3,32,256]{2,1,0:T(8,128)S(1)}, f32[3,32,256]{2,1,0:T(8,128)S(1)}, u32[]{:S(2)}, u32[]{:S(2)}) collective-permute-start(f32[3,32,256]{2,1,0:T(8,128)S(1)} %get-tuple-element.136), channel_id=1, source_target_pairs={{0,56},{8,16},{16,8},{24,32},{32,24},{40,48},{48,40},{56,0},{1,57}... | collective-permute-start | bytes 294920 | tf_op jit(solution)/shard_map/ppermute | solution.py:105
  63.3 6.4 %collective-permute-start.24 = (f32[3,32,256]{2,1,0:T(8,128)S(1)}, f32[3,32,256]{2,1,0:T(8,128)S(1)}, u32[]{:S(2)}, u32[]{:S(2)}) collective-permute-start(f32[3,32,256]{2,1,0:T(8,128)S(1)} %get-tuple-element.146), channel_id=1, source_target_pairs={{0,8},{8,0},{16,24},{24,16},{32,40},{40,32},{48,56},{56,48},{1,9},... | collective-permute-start | bytes 294920 | tf_op jit(solution)/shard_map/ppermute | solution.py:105
  63.4 6.3 %collective-permute-start.25 = (f32[3,32,256]{2,1,0:T(8,128)S(1)}, f32[3,32,256]{2,1,0:T(8,128)S(1)}, u32[]{:S(2)}, u32[]{:S(2)}) collective-permute-start(f32[3,32,256]{2,1,0:T(8,128)S(1)} %get-tuple-element.145), channel_id=1, source_target_pairs={{0,56},{8,16},{16,8},{24,32},{32,24},{40,48},{48,40},{56,0},{1,57}... | collective-permute-start | bytes 294920 | tf_op jit(solution)/shard_map/ppermute | solution.py:105
  69.1 5.7 %collective-permute-start.16 = (f32[3,32,512]{2,1,0:T(8,128)S(1)}, f32[3,32,512]{2,1,0:T(8,128)S(1)}, u32[]{:S(2)}, u32[]{:S(2)}) collective-permute-start(f32[3,32,512]{2,1,0:T(8,128)S(1)} %pad_maximum_fusion.1), channel_id=1, source_target_pairs={{0,56},{8,16},{16,8},{24,32},{32,24},{40,48},{48,40},{56,0},{1,57}... | collective-permute-start | bytes 589832 | tf_op jit(solution)/shard_map/ppermute | solution.py:105
  69.8 6.8 %collective-permute-start.26 = (f32[3,32,512]{2,1,0:T(8,128)S(1)}, f32[3,32,512]{2,1,0:T(8,128)S(1)}, u32[]{:S(2)}, u32[]{:S(2)}) collective-permute-start(f32[3,32,512]{2,1,0:T(8,128)S(1)} %pad_maximum_fusion.2), channel_id=1, source_target_pairs={{0,8},{8,0},{16,24},{24,16},{32,40},{40,32},{48,56},{56,48},{1,9},... | collective-permute-start | bytes 589832 | tf_op jit(solution)/shard_map/ppermute | solution.py:105
  70.7 7.6 %collective-permute-start.27 = (f32[3,32,512]{2,1,0:T(8,128)S(1)}, f32[3,32,512]{2,1,0:T(8,128)S(1)}, u32[]{:S(2)}, u32[]{:S(2)}) collective-permute-start(f32[3,32,512]{2,1,0:T(8,128)S(1)} %pad_maximum_fusion.3), channel_id=1, source_target_pairs={{0,56},{8,16},{16,8},{24,32},{32,24},{40,48},{48,40},{56,0},{1,57}... | collective-permute-start | bytes 589832 | tf_op jit(solution)/shard_map/ppermute | solution.py:105
  74.8 6.7 %collective-permute-start.17 = (f32[3,32,512]{2,1,0:T(8,128)S(1)}, f32[3,32,512]{2,1,0:T(8,128)S(1)}, u32[]{:S(2)}, u32[]{:S(2)}) collective-permute-start(f32[3,32,512]{2,1,0:T(8,128)S(1)} %get-tuple-element.85), channel_id=1, source_target_pairs={{0,8},{8,0},{16,24},{24,16},{32,40},{40,32},{48,56},{56,48},{1,9},... | collective-permute-start | bytes 589832 | tf_op jit(solution)/shard_map/ppermute | solution.py:105
  75.2 8.3 %collective-permute-start.18 = (f32[3,32,512]{2,1,0:T(8,128)S(1)}, f32[3,32,512]{2,1,0:T(8,128)S(1)}, u32[]{:S(2)}, u32[]{:S(2)}) collective-permute-start(f32[3,32,512]{2,1,0:T(8,128)S(1)} %get-tuple-element.86), channel_id=1, source_target_pairs={{0,56},{8,16},{16,8},{24,32},{32,24},{40,48},{48,40},{56,0},{1,57}... | collective-permute-start | bytes 589832 | tf_op jit(solution)/shard_map/ppermute | solution.py:105
  78.3 6.2 %collective-permute-start.28 = (f32[3,32,512]{2,1,0:T(8,128)S(1)}, f32[3,32,512]{2,1,0:T(8,128)S(1)}, u32[]{:S(2)}, u32[]{:S(2)}) collective-permute-start(f32[3,32,512]{2,1,0:T(8,128)S(1)} %get-tuple-element.103), channel_id=1, source_target_pairs={{0,8},{8,0},{16,24},{24,16},{32,40},{40,32},{48,56},{56,48},{1,9},... | collective-permute-start | bytes 589832 | tf_op jit(solution)/shard_map/ppermute | solution.py:105
  78.4 8.1 %collective-permute-start.29 = (f32[3,32,512]{2,1,0:T(8,128)S(1)}, f32[3,32,512]{2,1,0:T(8,128)S(1)}, u32[]{:S(2)}, u32[]{:S(2)}) collective-permute-start(f32[3,32,512]{2,1,0:T(8,128)S(1)} %get-tuple-element.104), channel_id=1, source_target_pairs={{0,56},{8,16},{16,8},{24,32},{32,24},{40,48},{48,40},{56,0},{1,57}... | collective-permute-start | bytes 589832 | tf_op jit(solution)/shard_map/ppermute | solution.py:105
  83.5 6.0 %collective-permute-start.19 = (f32[3,32,512]{2,1,0:T(8,128)S(1)}, f32[3,32,512]{2,1,0:T(8,128)S(1)}, u32[]{:S(2)}, u32[]{:S(2)}) collective-permute-start(f32[3,32,512]{2,1,0:T(8,128)S(1)} %get-tuple-element.89), channel_id=1, source_target_pairs={{0,8},{8,0},{16,24},{24,16},{32,40},{40,32},{48,56},{56,48},{1,9},... | collective-permute-start | bytes 589832 | tf_op jit(solution)/shard_map/ppermute | solution.py:105
  83.6 7.5 %collective-permute-start.20 = (f32[3,32,512]{2,1,0:T(8,128)S(1)}, f32[3,32,512]{2,1,0:T(8,128)S(1)}, u32[]{:S(2)}, u32[]{:S(2)}) collective-permute-start(f32[3,32,512]{2,1,0:T(8,128)S(1)} %get-tuple-element.90), channel_id=1, source_target_pairs={{0,56},{8,16},{16,8},{24,32},{32,24},{40,48},{48,40},{56,0},{1,57}... | collective-permute-start | bytes 589832 | tf_op jit(solution)/shard_map/ppermute | solution.py:105
  86.6 7.9 %collective-permute-start.30 = (f32[3,32,512]{2,1,0:T(8,128)S(1)}, f32[3,32,512]{2,1,0:T(8,128)S(1)}, u32[]{:S(2)}, u32[]{:S(2)}) collective-permute-start(f32[3,32,512]{2,1,0:T(8,128)S(1)} %get-tuple-element.107), channel_id=1, source_target_pairs={{0,8},{8,0},{16,24},{24,16},{32,40},{40,32},{48,56},{56,48},{1,9},... | collective-permute-start | bytes 589832 | tf_op jit(solution)/shard_map/ppermute | solution.py:105
  86.7 8.6 %collective-permute-start.31 = (f32[3,32,512]{2,1,0:T(8,128)S(1)}, f32[3,32,512]{2,1,0:T(8,128)S(1)}, u32[]{:S(2)}, u32[]{:S(2)}) collective-permute-start(f32[3,32,512]{2,1,0:T(8,128)S(1)} %get-tuple-element.108), channel_id=1, source_target_pairs={{0,56},{8,16},{16,8},{24,32},{32,24},{40,48},{48,40},{56,0},{1,57}... | collective-permute-start | bytes 589832 | tf_op jit(solution)/shard_map/ppermute | solution.py:105
  91.1 12.1 %collective-permute-start.22 = (f32[32,512]{1,0:T(8,128)S(1)}, f32[32,512]{1,0:T(8,128)S(1)}, u32[]{:S(2)}, u32[]{:S(2)}) collective-permute-start(f32[32,512]{1,0:T(8,128)S(1)} %get-tuple-element.130), channel_id=1, source_target_pairs={{0,64},{64,0},{128,192},{192,128},{1,65},{65,1},{129,193},{193,129... | collective-permute-start | bytes 196616 | tf_op jit(solution)/shard_map/ppermute | solution.py:239
  92.0 11.3 %collective-permute-start.23 = (f32[32,512]{1,0:T(8,128)S(1)}, f32[32,512]{1,0:T(8,128)S(1)}, u32[]{:S(2)}, u32[]{:S(2)}) collective-permute-start(f32[32,512]{1,0:T(8,128)S(1)} %get-tuple-element.129), channel_id=1, source_target_pairs={{0,192},{64,128},{128,64},{192,0},{1,193},{65,129},{129,65},{193,1... | collective-permute-start | bytes 196616 | tf_op jit(solution)/shard_map/ppermute | solution.py:240
  95.4 8.0 %collective-permute-start.33 = (f32[32,512]{1,0:T(8,128)S(1)}, f32[32,512]{1,0:T(8,128)S(1)}, u32[]{:S(2)}, u32[]{:S(2)}) collective-permute-start(f32[32,512]{1,0:T(8,128)S(1)} %get-tuple-element.139), channel_id=1, source_target_pairs={{0,64},{64,0},{128,192},{192,128},{1,65},{65,1},{129,193},{193,129... | collective-permute-start | bytes 196616 | tf_op jit(solution)/shard_map/ppermute | solution.py:239
  96.3 7.1 %collective-permute-start.34 = (f32[32,512]{1,0:T(8,128)S(1)}, f32[32,512]{1,0:T(8,128)S(1)}, u32[]{:S(2)}, u32[]{:S(2)}) collective-permute-start(f32[32,512]{1,0:T(8,128)S(1)} %get-tuple-element.138), channel_id=1, source_target_pairs={{0,192},{64,128},{128,64},{192,0},{1,193},{65,129},{129,65},{193,1... | collective-permute-start | bytes 196616 | tf_op jit(solution)/shard_map/ppermute | solution.py:240
  103.4 9.3 %collective-permute-start.35 = (f32[64,512]{1,0:T(8,128)S(1)}, f32[64,512]{1,0:T(8,128)S(1)}, u32[]{:S(2)}, u32[]{:S(2)}) collective-permute-start(f32[64,512]{1,0:T(8,128)S(1)} %get-tuple-element.127), channel_id=1, source_target_pairs={{0,1},{1,0},{2,3},{3,2},{4,5},{5,4},{6,7},{7,6},{8,9},{9,8},{10,11... | collective-permute-start | bytes 393224 | tf_op jit(solution)/shard_map/ppermute | solution.py:244
  (6 other events, 43.5 us)

commit v4 on v3

--- a/solution.py
+++ b/solution.py
@@ -105,15 +105,18 @@
     return lax.ppermute(value, axis, even(n)), lax.ppermute(other, axis, odd(n))
 
 
-def z_phase(part):
+def z_first(part):
     half = part[0].shape[-1] // 2
-    one, two = step(part[0][..., :half], part[0][..., half:], "z", NZ)
-    one, two = tie((one, two))
-    one, two = step(*tie((add_right(part[1], two), add_left(part[2], one))), "z", NZ)
-    for k in (3, 5):
+    one, two = tie(step(part[0][..., :half], part[0][..., half:], "z", NZ))
+    return tie((add_right(part[1], two), add_left(part[2], one)))
+
+
+def z_rest(ready, part):
+    one, two = step(*ready, "z", NZ)
+    for k in (0, 2):
         one, two = tie((one, two))
         one, two = step(*tie((part[k] + two, part[k + 1] + one)), "z", NZ)
-    return part[7] + one + two
+    return part[4] + one + two
 
 
 def split_kernel(masked, count, mine, other, top, low):
@@ -229,16 +232,17 @@
     far_down, far_up = step(*fars, "y", NY)
     blocks = (pair, one, far_up, far_down, two)
     head = chunks(block_sizes, blocks, t2_par, first, 0, HEAD)
-    tail = chunks(block_sizes, blocks, t2_par, first, HEAD, NZ - HEAD)
-
-    done = []
-    for h in range(2):
-        got = z_phase([head[h][k] for k in range(HEAD)] + [tail[h][k] for k in range(NZ - HEAD)])
-        slot = lambda d: pick(got, slots[d], 0)
-        far = lax.ppermute(slot(2), "x", flip(NX, 2))
-        near = lax.ppermute(slot(1), "x", flip(NX, 1))
-        wrap = lax.ppermute(slot(3), "x", flip(NX, 3))
-        done.append(both(low_p, slot(0) + far, near + wrap, 0))
+    ready = [z_first(head[h]) for h in range(2)]
+    late, ready[0] = tie((block_sizes, ready[0]))
+    tail = chunks(late, blocks, t2_par, first, HEAD, NZ - HEAD)
+    gots = [z_rest(ready[h], tail[h]) for h in range(2)]
+    slot = lambda d: jnp.stack([pick(got, slots[d], 0) for got in gots])
+    far = lax.ppermute(slot(2), "x", flip(NX, 2))
+    near = lax.ppermute(slot(1), "x", flip(NX, 1))
+    wrap = lax.ppermute(slot(3), "x", flip(NX, 3))
+    same = slot(0) + far
+    (near, wrap), _ = tie(((near, wrap), same))
+    done = both(low_p, same, near + wrap, 1)
 
     mine = jnp.where(low_c, done[0], done[1])
     other = lax.ppermute(jnp.where(low_c, done[1], done[0]), "c", swap)

time: 114 us -> 110 us (0.965)
  waiting for transfers between devices: 52 us -> 47.8 us
    ppermute x12, starting transfers between devices: 18.3 us -> 24 us  [step(): lax.ppermute(other, axis, odd(n))]
    ppermute x12, waiting for transfers between devices: 23.2 us -> 19.3 us  [step(): lax.ppermute(other, axis, odd(n))]
    ppermute x2 -> x1, starting transfers between devices: 3.85 us -> 0.84 us  [body(): wrap = lax.ppermute(slot(3), 'x', flip(NX, 3))]
    ppermute x2 -> x1, waiting for transfers between devices: 4.56 us -> 1.91 us  [body(): far = lax.ppermute(slot(2), 'x', flip(NX, 2))]
    ppermute x2 -> x1, waiting for transfers between devices: 0.01 us -> 2.23 us  [body(): wrap = lax.ppermute(slot(3), 'x', flip(NX, 3))]
    ppermute x1, starting transfers between devices: 8.35 us -> 6.35 us  [body(): other = lax.ppermute(jnp.where(low_c, done[1], done[0]), 'c', swap)]
    ppermute x2 -> x1, starting transfers between devices: 1.79 us -> 0.09 us  [body(): near = lax.ppermute(slot(1), 'x', flip(NX, 1))]
    ppermute x2 -> x1, starting transfers between devices: 1.05 us -> 2.53 us  [body(): far = lax.ppermute(slot(2), 'x', flip(NX, 2))]
  transfers between devices with their start and end apart: 36 -> 33, of which waited for: 22 -> 21; matrix products, arithmetic and copies ran while one was open for 1% -> 1% of each run, Pallas kernels for 7% -> 8%
where the time goes in v4:
time: 110 us
  waiting for transfers between devices  47.8 us (43%)
  starting transfers between devices  44.8 us (41%)
  Pallas kernels  12 us (11%)
  local copies, waits for them, and re-layouts  3.05 us (3%)
    ppermute x12, starting transfers between devices, step(): lax.ppermute(other, axis, odd(n))  24 us
    ppermute x12, waiting for transfers between devices, step(): lax.ppermute(other, axis, odd(n))  19.3 us
    ppermute x12, waiting for transfers between devices, step(): lax.ppermute(value, axis, even(n))  12.3 us
    pallas_call x3, Pallas kernels, chunks(): pl.pallas_call(functools.partial(chunk_kernel, first_k, count, len(before...  9.92 us
    ppermute x1, waiting for transfers between devices, body(): pair = lax.ppermute(pick(near, not_p, 1), 'x', flip(NX, 1))  9.52 us
    ppermute x1, starting transfers between devices, body(): other = lax.ppermute(jnp.where(low_c, done[1], done[0]), 'c', swap)  6.35 us
    ppermute x12, starting transfers between devices, step(): lax.ppermute(value, axis, even(n))  4.81 us
    ppermute x1, starting transfers between devices, body(): lax.ppermute(give, 'c', swap)  3.33 us
  transfers between devices with their start and end apart: 33, of which 21 were waited for; matrix products, arithmetic and copies ran while one was open for 1% of the time, Pallas kernels for 8%

profile of v4, /device:TPU:1, one launch (start us, length us, event | category | flops | bytes accessed | tf_op | source)
XLA Modules:
  0.0 109.5 jit_solution(14716296169810546098)
XLA Ops:
  0.0 1.6 %copy.5 = f32[512,512]{0,1:T(8,128)S(1)} copy(f32[512,512]{1,0:T(8,128)} %param.5) | data formatting | bytes 2097152 | tf_op jit(solution)/shard_map/optimization_barrier | solution.py:200
  1.7 3.3 %collective-permute-start = (f32[4,64,512]{2,1,0:T(8,128)S(1)}, f32[4,64,512]{2,1,0:T(8,128)S(1)}, u32[]{:S(2)}, u32[]{:S(2)}) collective-permute-start(f32[4,64,512]{2,1,0:T(8,128)S(1)} %get-tuple-element.122), channel_id=1, source_target_pairs={{0,1},{1,0},{2,3},{3,2},{4,5},{5,4},{6,7},{7,6},{8,9},{9,8},{10,11... | collective-permute-start | bytes 1572872 | tf_op jit(solution)/shard_map/ppermute | solution.py:210
  5.0 1.5 %collective-permute-done = f32[4,64,512]{2,1,0:T(8,128)S(1)} collective-permute-done((f32[4,64,512]{2,1,0:T(8,128)S(1)}, f32[4,64,512]{2,1,0:T(8,128)S(1)}, u32[]{:S(2)}, u32[]{:S(2)}) %collective-permute-start) | collective-permute-done | bytes 524320 | tf_op jit(solution)/shard_map/ppermute | solution.py:210
  8.9 1.5 %collective-permute-start.2 = (f32[8,32,512]{2,1,0:T(8,128)S(1)}, f32[8,32,512]{2,1,0:T(8,128)S(1)}, u32[]{:S(2)}, u32[]{:S(2)}) collective-permute-start(f32[8,32,512]{2,1,0:T(8,128)S(1)} %get-tuple-element.119.b0), channel_id=1, source_target_pairs={{0,6},{2,4},{4,2},{6,0},{1,7},{3,5},{5,3},{7,1},{8,14},{10,12},{12... | collective-permute-start | bytes 1572872 | tf_op jit(solution)/shard_map/ppermute | solution.py:105
  10.5 9.5 %collective-permute-done.1.b0 = f32[8,32,512]{2,1,0:T(8,128)S(1)} collective-permute-done((f32[8,32,512]{2,1,0:T(8,128)S(1)}, f32[8,32,512]{2,1,0:T(8,128)S(1)}, u32[]{:S(2)}, u32[]{:S(2)}) %collective-permute-start.1) | collective-permute-done | bytes 524320 | tf_op jit(solution)/shard_map/ppermute | solution.py:213
  20.5 3.1 %collective-permute-done.2.b3 = f32[8,32,512]{2,1,0:T(8,128)S(1)} collective-permute-done((f32[8,32,512]{2,1,0:T(8,128)S(1)}, f32[8,32,512]{2,1,0:T(8,128)S(1)}, u32[]{:S(2)}, u32[]{:S(2)}) %collective-permute-start.2) | collective-permute-done | bytes 524320 | tf_op jit(solution)/shard_map/ppermute | solution.py:105
  24.2 1.7 %collective-permute-start.6 = (f32[8,32,512]{2,1,0:T(8,128)S(1)}, f32[8,32,512]{2,1,0:T(8,128)S(1)}, u32[]{:S(2)}, u32[]{:S(2)}) collective-permute-start(f32[8,32,512]{2,1,0:T(8,128)S(1)} %collective-permute-done.1.b0), channel_id=1, source_target_pairs={{0,6},{2,4},{4,2},{6,0},{1,7},{3,5},{5,3},{7,1},{8,14},{10,12},{12... | collective-permute-start | bytes 1572872 | tf_op jit(solution)/shard_map/ppermute | solution.py:105
  25.9 1.5 %collective-permute-start.7 = (f32[8,16,512]{2,1,0:T(8,128)S(1)}, f32[8,16,512]{2,1,0:T(8,128)S(1)}, u32[]{:S(2)}, u32[]{:S(2)}) collective-permute-start(f32[8,16,512]{2,1,0:T(8,128)S(1)} %slice.140), channel_id=1, source_target_pairs={{0,2},{2,0},{4,6},{6,4},{1,3},{3,1},{5,7},{7,5},{8,10},{10,8},{12,... | collective-permute-start | bytes 786440 | tf_op jit(solution)/shard_map/ppermute | solution.py:105
  28.4 9.4 %collective-permute-done.6.b3 = f32[8,32,512]{2,1,0:T(8,128)S(1)} collective-permute-done((f32[8,32,512]{2,1,0:T(8,128)S(1)}, f32[8,32,512]{2,1,0:T(8,128)S(1)}, u32[]{:S(2)}, u32[]{:S(2)}) %collective-permute-start.6) | collective-permute-done | bytes 524320 | tf_op jit(solution)/shard_map/ppermute | solution.py:105
  38.2 5.6 %collective-permute-done.7.b2d = f32[8,16,512]{2,1,0:T(8,128)S(1)} collective-permute-done((f32[8,16,512]{2,1,0:T(8,128)S(1)}, f32[8,16,512]{2,1,0:T(8,128)S(1)}, u32[]{:S(2)}, u32[]{:S(2)}) %collective-permute-start.7) | collective-permute-done | bytes 262176 | tf_op jit(solution)/shard_map/ppermute | solution.py:105
  43.8 2.0 %collective-permute-start.12 = (f32[512,512]{1,0:T(8,128)S(1)}, f32[512,512]{1,0:T(8,128)S(1)}, u32[]{:S(2)}, u32[]{:S(2)}) collective-permute-start(f32[512,512]{1,0:T(8,128)S(1)} %collective-permute-done.11.mine), channel_id=1, source_target_pairs={{0,1},{1,0},{2,3},{3,2},{4,5},{5,4},{6,7},{7,6},{8,9},{9,8},{10,11... | collective-permute-start | bytes 3145736 | tf_op jit(solution)/shard_map/ppermute | solution.py:230
  45.8 1.4 %collective-permute-start.9 = (f32[8,16,512]{2,1,0:T(8,128)S(1)}, f32[8,16,512]{2,1,0:T(8,128)S(1)}, u32[]{:S(2)}, u32[]{:S(2)}) collective-permute-start(f32[8,16,512]{2,1,0:T(8,128)S(1)} %slice.143), channel_id=1, source_target_pairs={{0,6},{2,4},{4,2},{6,0},{1,7},{3,5},{5,3},{7,1},{8,14},{10,12},{12... | collective-permute-start | bytes 786440 | tf_op jit(solution)/shard_map/ppermute | solution.py:105
  47.3 4.5 %shard_map.47 = (f32[8,3,32,512]{3,2,1,0:T(8,128)S(1)}, f32[8,3,32,512]{3,2,1,0:T(8,128)S(1)}) custom-call(s32[8]{0:T(128)S(1)} %copy-done.1, f32[8,32,512]{2,1,0:T(8,128)S(1)} %get-tuple-element.119.b0, f32[8,32,512]{2,1,0:T(8,128)S(1)} %collective-permute-done.3.b1, f32[8,16,512]{2,1,0:T(8,128)S(1)} %collective-permute-done.8.b2u, ...), custom_call_target="tpu_custom_call" | custom-call | flops 3221225472 | bytes 7340032 | tf_op jit(solution)/shard_map/pallas_call | solution.py:79
  52.1 1.5 %collective-permute-done.10.b2d = f32[8,16,512]{2,1,0:T(8,128)S(1)} collective-permute-done((f32[8,16,512]{2,1,0:T(8,128)S(1)}, f32[8,16,512]{2,1,0:T(8,128)S(1)}, u32[]{:S(2)}, u32[]{:S(2)}) %collective-permute-start.10) | collective-permute-done | bytes 262176 | tf_op jit(solution)/shard_map/ppermute | solution.py:105
  54.6 2.2 %shard_map.49 = (f32[3,3,32,512]{3,2,1,0:T(8,128)S(1)}, f32[3,3,32,512]{3,2,1,0:T(8,128)S(1)}) custom-call(s32[8]{0:T(128)S(1)} %copy-done.1, f32[8,32,512]{2,1,0:T(8,128)S(1)} %collective-permute-done.1.b0, f32[8,32,512]{2,1,0:T(8,128)S(1)} %collective-permute-done.5.b1, f32[8,16,512]{2,1,0:T(8,128)S(1)} %collective-permute-done.9.b2u, ...), custom_call_target="tpu_custom_call" | custom-call | flops 1207959552 | bytes 4063232 | tf_op jit(solution)/shard_map/pallas_call | solution.py:79
  56.9 1.7 %collective-permute-start.13 = (f32[3,32,256]{2,1,0:T(8,128)S(1)}, f32[3,32,256]{2,1,0:T(8,128)S(1)}, u32[]{:S(2)}, u32[]{:S(2)}) collective-permute-start(f32[3,32,256]{2,1,0:T(8,128)S(1)} %get-tuple-element.152), channel_id=1, source_target_pairs={{0,8},{8,0},{16,24},{24,16},{32,40},{40,32},{48,56},{56,48},{1,9},... | collective-permute-start | bytes 294920 | tf_op jit(solution)/shard_map/ppermute | solution.py:105
  58.6 4.7 %collective-permute-start.14 = (f32[3,32,256]{2,1,0:T(8,128)S(1)}, f32[3,32,256]{2,1,0:T(8,128)S(1)}, u32[]{:S(2)}, u32[]{:S(2)}) collective-permute-start(f32[3,32,256]{2,1,0:T(8,128)S(1)} %get-tuple-element.151), channel_id=1, source_target_pairs={{0,56},{8,16},{16,8},{24,32},{32,24},{40,48},{48,40},{56,0},{1,57}... | collective-permute-start | bytes 294920 | tf_op jit(solution)/shard_map/ppermute | solution.py:105
  63.4 1.4 %collective-permute-start.22 = (f32[3,32,256]{2,1,0:T(8,128)S(1)}, f32[3,32,256]{2,1,0:T(8,128)S(1)}, u32[]{:S(2)}, u32[]{:S(2)}) collective-permute-start(f32[3,32,256]{2,1,0:T(8,128)S(1)} %get-tuple-element.157), channel_id=1, source_target_pairs={{0,56},{8,16},{16,8},{24,32},{32,24},{40,48},{48,40},{56,0},{1,57}... | collective-permute-start | bytes 294920 | tf_op jit(solution)/shard_map/ppermute | solution.py:105
  65.8 2.5 %collective-permute-start.16 = (f32[3,32,512]{2,1,0:T(8,128)S(1)}, f32[3,32,512]{2,1,0:T(8,128)S(1)}, u32[]{:S(2)}, u32[]{:S(2)}) collective-permute-start(f32[3,32,512]{2,1,0:T(8,128)S(1)} %pad_maximum_fusion.1), channel_id=1, source_target_pairs={{0,56},{8,16},{16,8},{24,32},{32,24},{40,48},{48,40},{56,0},{1,57}... | collective-permute-start | bytes 589832 | tf_op jit(solution)/shard_map/ppermute | solution.py:105
  68.8 2.1 %collective-permute-start.24 = (f32[3,32,512]{2,1,0:T(8,128)S(1)}, f32[3,32,512]{2,1,0:T(8,128)S(1)}, u32[]{:S(2)}, u32[]{:S(2)}) collective-permute-start(f32[3,32,512]{2,1,0:T(8,128)S(1)} %pad_maximum_fusion.3), channel_id=1, source_target_pairs={{0,56},{8,16},{16,8},{24,32},{32,24},{40,48},{48,40},{56,0},{1,57}... | collective-permute-start | bytes 589832 | tf_op jit(solution)/shard_map/ppermute | solution.py:105
  70.9 3.2 %shard_map.50 = (f32[5,3,32,512]{3,2,1,0:T(8,128)S(1)}, f32[5,3,32,512]{3,2,1,0:T(8,128)S(1)}) custom-call(s32[8]{0:T(128)S(1)} %copy-done.1, f32[8,32,512]{2,1,0:T(8,128)S(1)} %collective-permute-done.1.b0, f32[8,32,512]{2,1,0:T(8,128)S(1)} %collective-permute-done.5.b1, f32[8,16,512]{2,1,0:T(8,128)S(1)} %collective-permute-done.9.b2u, ...), custom_call_target="tpu_custom_call" | custom-call | flops 2013265920 | bytes 5373952 | tf_op jit(solution)/shard_map/pallas_call | solution.py:79
  74.5 2.1 %collective-permute-start.18 = (f32[3,32,512]{2,1,0:T(8,128)S(1)}, f32[3,32,512]{2,1,0:T(8,128)S(1)}, u32[]{:S(2)}, u32[]{:S(2)}) collective-permute-start(f32[3,32,512]{2,1,0:T(8,128)S(1)} %get-tuple-element.94), channel_id=1, source_target_pairs={{0,56},{8,16},{16,8},{24,32},{32,24},{40,48},{48,40},{56,0},{1,57}... | collective-permute-start | bytes 589832 | tf_op jit(solution)/shard_map/ppermute | solution.py:105
  78.1 1.7 %collective-permute-done.17 = f32[3,32,512]{2,1,0:T(8,128)S(1)} collective-permute-done((f32[3,32,512]{2,1,0:T(8,128)S(1)}, f32[3,32,512]{2,1,0:T(8,128)S(1)}, u32[]{:S(2)}, u32[]{:S(2)}) %collective-permute-start.17) | collective-permute-done | bytes 196640 | tf_op jit(solution)/shard_map/ppermute | solution.py:105
  79.8 1.5 %collective-permute-done.18 = f32[3,32,512]{2,1,0:T(8,128)S(1)} collective-permute-done((f32[3,32,512]{2,1,0:T(8,128)S(1)}, f32[3,32,512]{2,1,0:T(8,128)S(1)}, u32[]{:S(2)}, u32[]{:S(2)}) %collective-permute-start.18) | collective-permute-done | bytes 196640 | tf_op jit(solution)/shard_map/ppermute | solution.py:105
  81.4 2.1 %collective-permute-start.20 = (f32[3,32,512]{2,1,0:T(8,128)S(1)}, f32[3,32,512]{2,1,0:T(8,128)S(1)}, u32[]{:S(2)}, u32[]{:S(2)}) collective-permute-start(f32[3,32,512]{2,1,0:T(8,128)S(1)} %get-tuple-element.98), channel_id=1, source_target_pairs={{0,56},{8,16},{16,8},{24,32},{32,24},{40,48},{48,40},{56,0},{1,57}... | collective-permute-start | bytes 589832 | tf_op jit(solution)/shard_map/ppermute | solution.py:105
  84.1 2.3 %collective-permute-start.28 = (f32[3,32,512]{2,1,0:T(8,128)S(1)}, f32[3,32,512]{2,1,0:T(8,128)S(1)}, u32[]{:S(2)}, u32[]{:S(2)}) collective-permute-start(f32[3,32,512]{2,1,0:T(8,128)S(1)} %get-tuple-element.113), channel_id=1, source_target_pairs={{0,56},{8,16},{16,8},{24,32},{32,24},{40,48},{48,40},{56,0},{1,57}... | collective-permute-start | bytes 589832 | tf_op jit(solution)/shard_map/ppermute | solution.py:105
  86.4 1.8 %collective-permute-done.19 = f32[3,32,512]{2,1,0:T(8,128)S(1)} collective-permute-done((f32[3,32,512]{2,1,0:T(8,128)S(1)}, f32[3,32,512]{2,1,0:T(8,128)S(1)}, u32[]{:S(2)}, u32[]{:S(2)}) %collective-permute-start.19) | collective-permute-done | bytes 196640 | tf_op jit(solution)/shard_map/ppermute | solution.py:105
  90.9 2.1 %collective-permute-done.28 = f32[3,32,512]{2,1,0:T(8,128)S(1)} collective-permute-done((f32[3,32,512]{2,1,0:T(8,128)S(1)}, f32[3,32,512]{2,1,0:T(8,128)S(1)}, u32[]{:S(2)}, u32[]{:S(2)}) %collective-permute-start.28) | collective-permute-done | bytes 196640 | tf_op jit(solution)/shard_map/ppermute | solution.py:105
  93.1 2.5 %collective-permute-start.29 = (f32[2,32,512]{2,1,0:T(8,128)S(1)}, f32[2,32,512]{2,1,0:T(8,128)S(1)}, u32[]{:S(2)}, u32[]{:S(2)}) collective-permute-start(f32[2,32,512]{2,1,0:T(8,128)S(1)} %pad_maximum_fusion.4), channel_id=1, source_target_pairs={{0,128},{64,192},{128,0},{192,64},{1,129},{65,193},{129,1},{193,65... | collective-permute-start | bytes 393224 | tf_op jit(solution)/shard_map/ppermute | solution.py:240
  96.6 1.9 %collective-permute-done.29 = f32[2,32,512]{2,1,0:T(8,128)S(1)} collective-permute-done((f32[2,32,512]{2,1,0:T(8,128)S(1)}, f32[2,32,512]{2,1,0:T(8,128)S(1)}, u32[]{:S(2)}, u32[]{:S(2)}) %collective-permute-start.29) | collective-permute-done | bytes 131104 | tf_op jit(solution)/shard_map/ppermute | solution.py:240
  98.6 2.2 %collective-permute-done.31 = f32[2,32,512]{2,1,0:T(8,128)S(1)} collective-permute-done((f32[2,32,512]{2,1,0:T(8,128)S(1)}, f32[2,32,512]{2,1,0:T(8,128)S(1)}, u32[]{:S(2)}, u32[]{:S(2)}) %collective-permute-start.31) | collective-permute-done | bytes 131104 | tf_op jit(solution)/shard_map/ppermute | solution.py:242
  100.9 6.4 %collective-permute-start.32 = (f32[64,512]{1,0:T(8,128)S(1)}, f32[64,512]{1,0:T(8,128)S(1)}, u32[]{:S(2)}, u32[]{:S(2)}) collective-permute-start(f32[64,512]{1,0:T(8,128)S(1)} %get-tuple-element.137), channel_id=1, source_target_pairs={{0,1},{1,0},{2,3},{3,2},{4,5},{5,4},{6,7},{7,6},{8,9},{9,8},{10,11... | collective-permute-start | bytes 393224 | tf_op jit(solution)/shard_map/ppermute | solution.py:248
  (80 shorter events, 16.0 us)
Async XLA Ops:
  1.7 4.9 %collective-permute-start = (f32[4,64,512]{2,1,0:T(8,128)S(1)}, f32[4,64,512]{2,1,0:T(8,128)S(1)}, u32[]{:S(2)}, u32[]{:S(2)}) collective-permute-start(f32[4,64,512]{2,1,0:T(8,128)S(1)} %get-tuple-element.122), channel_id=1, source_target_pairs={{0,1},{1,0},{2,3},{3,2},{4,5},{5,4},{6,7},{7,6},{8,9},{9,8},{10,11... | collective-permute-start | bytes 1572872 | tf_op jit(solution)/shard_map/ppermute | solution.py:210
  6.8 13.2 %collective-permute-start.1 = (f32[8,32,512]{2,1,0:T(8,128)S(1)}, f32[8,32,512]{2,1,0:T(8,128)S(1)}, u32[]{:S(2)}, u32[]{:S(2)}) collective-permute-start(f32[8,32,512]{2,1,0:T(8,128)S(1)} %get-tuple-element.120), channel_id=1, source_target_pairs={{0,64},{64,0},{128,192},{192,128},{1,65},{65,1},{129,193},{193,129... | collective-permute-start | bytes 1572872 | tf_op jit(solution)/shard_map/ppermute | solution.py:213
  7.9 15.8 %collective-permute-start.4 = (f32[512,512]{1,0:T(8,128)S(1)}, f32[512,512]{1,0:T(8,128)S(1)}, u32[]{:S(2)}, u32[]{:S(2)}) collective-permute-start(f32[512,512]{1,0:T(8,128)S(1)} %copy-done), channel_id=1, source_target_pairs={{0,1},{1,0},{2,3},{3,2},{4,5},{5,4},{6,7},{7,6},{8,9},{9,8},{10,11... | collective-permute-start | bytes 3145736 | tf_op jit(solution)/shard_map/ppermute | solution.py:217
  8.9 14.7 %collective-permute-start.2 = (f32[8,32,512]{2,1,0:T(8,128)S(1)}, f32[8,32,512]{2,1,0:T(8,128)S(1)}, u32[]{:S(2)}, u32[]{:S(2)}) collective-permute-start(f32[8,32,512]{2,1,0:T(8,128)S(1)} %get-tuple-element.119.b0), channel_id=1, source_target_pairs={{0,6},{2,4},{4,2},{6,0},{1,7},{3,5},{5,3},{7,1},{8,14},{10,12},{12... | collective-permute-start | bytes 1572872 | tf_op jit(solution)/shard_map/ppermute | solution.py:105
  10.5 13.2 %collective-permute-start.3 = (f32[8,32,512]{2,1,0:T(8,128)S(1)}, f32[8,32,512]{2,1,0:T(8,128)S(1)}, u32[]{:S(2)}, u32[]{:S(2)}) collective-permute-start(f32[8,32,512]{2,1,0:T(8,128)S(1)} %get-tuple-element.119.b0), channel_id=1, source_target_pairs={{0,2},{2,0},{4,6},{6,4},{1,3},{3,1},{5,7},{7,5},{8,10},{10,8},{12,... | collective-permute-start | bytes 1572872 | tf_op jit(solution)/shard_map/ppermute | solution.py:105
  20.1 23.7 %collective-permute-start.11 = (f32[512,512]{1,0:T(8,128)S(1)}, f32[512,512]{1,0:T(8,128)S(1)}, u32[]{:S(2)}, u32[]{:S(2)}) collective-permute-start(f32[512,512]{1,0:T(8,128)S(1)} %broadcast_select_fusion), channel_id=1, source_target_pairs={{0,64},{64,0},{128,192},{192,128},{1,65},{65,1},{129,193},{193,129... | collective-permute-start | bytes 3145736 | tf_op jit(solution)/shard_map/ppermute | solution.py:216
  24.2 13.6 %collective-permute-start.6 = (f32[8,32,512]{2,1,0:T(8,128)S(1)}, f32[8,32,512]{2,1,0:T(8,128)S(1)}, u32[]{:S(2)}, u32[]{:S(2)}) collective-permute-start(f32[8,32,512]{2,1,0:T(8,128)S(1)} %collective-permute-done.1.b0), channel_id=1, source_target_pairs={{0,6},{2,4},{4,2},{6,0},{1,7},{3,5},{5,3},{7,1},{8,14},{10,12},{12... | collective-permute-start | bytes 1572872 | tf_op jit(solution)/shard_map/ppermute | solution.py:105
  25.9 12.3 %collective-permute-start.5 = (f32[8,32,512]{2,1,0:T(8,128)S(1)}, f32[8,32,512]{2,1,0:T(8,128)S(1)}, u32[]{:S(2)}, u32[]{:S(2)}) collective-permute-start(f32[8,32,512]{2,1,0:T(8,128)S(1)} %collective-permute-done.1.b0), channel_id=1, source_target_pairs={{0,2},{2,0},{4,6},{6,4},{1,3},{3,1},{5,7},{7,5},{8,10},{10,8},{12,... | collective-permute-start | bytes 1572872 | tf_op jit(solution)/shard_map/ppermute | solution.py:105
  25.9 18.0 %collective-permute-start.7 = (f32[8,16,512]{2,1,0:T(8,128)S(1)}, f32[8,16,512]{2,1,0:T(8,128)S(1)}, u32[]{:S(2)}, u32[]{:S(2)}) collective-permute-start(f32[8,16,512]{2,1,0:T(8,128)S(1)} %slice.140), channel_id=1, source_target_pairs={{0,2},{2,0},{4,6},{6,4},{1,3},{3,1},{5,7},{7,5},{8,10},{10,8},{12,... | collective-permute-start | bytes 786440 | tf_op jit(solution)/shard_map/ppermute | solution.py:105
  27.3 16.5 %collective-permute-start.8 = (f32[8,16,512]{2,1,0:T(8,128)S(1)}, f32[8,16,512]{2,1,0:T(8,128)S(1)}, u32[]{:S(2)}, u32[]{:S(2)}) collective-permute-start(f32[8,16,512]{2,1,0:T(8,128)S(1)} %slice.141), channel_id=1, source_target_pairs={{0,6},{2,4},{4,2},{6,0},{1,7},{3,5},{5,3},{7,1},{8,14},{10,12},{12... | collective-permute-start | bytes 786440 | tf_op jit(solution)/shard_map/ppermute | solution.py:105
  43.8 8.0 %collective-permute-start.12 = (f32[512,512]{1,0:T(8,128)S(1)}, f32[512,512]{1,0:T(8,128)S(1)}, u32[]{:S(2)}, u32[]{:S(2)}) collective-permute-start(f32[512,512]{1,0:T(8,128)S(1)} %collective-permute-done.11.mine), channel_id=1, source_target_pairs={{0,1},{1,0},{2,3},{3,2},{4,5},{5,4},{6,7},{7,6},{8,9},{9,8},{10,11... | collective-permute-start | bytes 3145736 | tf_op jit(solution)/shard_map/ppermute | solution.py:230
  45.8 7.9 %collective-permute-start.10 = (f32[8,16,512]{2,1,0:T(8,128)S(1)}, f32[8,16,512]{2,1,0:T(8,128)S(1)}, u32[]{:S(2)}, u32[]{:S(2)}) collective-permute-start(f32[8,16,512]{2,1,0:T(8,128)S(1)} %slice.142), channel_id=1, source_target_pairs={{0,2},{2,0},{4,6},{6,4},{1,3},{3,1},{5,7},{7,5},{8,10},{10,8},{12,... | collective-permute-start | bytes 786440 | tf_op jit(solution)/shard_map/ppermute | solution.py:105
  45.8 8.7 %collective-permute-start.9 = (f32[8,16,512]{2,1,0:T(8,128)S(1)}, f32[8,16,512]{2,1,0:T(8,128)S(1)}, u32[]{:S(2)}, u32[]{:S(2)}) collective-permute-start(f32[8,16,512]{2,1,0:T(8,128)S(1)} %slice.143), channel_id=1, source_target_pairs={{0,6},{2,4},{4,2},{6,0},{1,7},{3,5},{5,3},{7,1},{8,14},{10,12},{12... | collective-permute-start | bytes 786440 | tf_op jit(solution)/shard_map/ppermute | solution.py:105
  56.9 8.0 %collective-permute-start.13 = (f32[3,32,256]{2,1,0:T(8,128)S(1)}, f32[3,32,256]{2,1,0:T(8,128)S(1)}, u32[]{:S(2)}, u32[]{:S(2)}) collective-permute-start(f32[3,32,256]{2,1,0:T(8,128)S(1)} %get-tuple-element.152), channel_id=1, source_target_pairs={{0,8},{8,0},{16,24},{24,16},{32,40},{40,32},{48,56},{56,48},{1,9},... | collective-permute-start | bytes 294920 | tf_op jit(solution)/shard_map/ppermute | solution.py:105
  58.6 6.7 %collective-permute-start.14 = (f32[3,32,256]{2,1,0:T(8,128)S(1)}, f32[3,32,256]{2,1,0:T(8,128)S(1)}, u32[]{:S(2)}, u32[]{:S(2)}) collective-permute-start(f32[3,32,256]{2,1,0:T(8,128)S(1)} %get-tuple-element.151), channel_id=1, source_target_pairs={{0,56},{8,16},{16,8},{24,32},{32,24},{40,48},{48,40},{56,0},{1,57}... | collective-permute-start | bytes 294920 | tf_op jit(solution)/shard_map/ppermute | solution.py:105
  63.3 4.9 %collective-permute-start.21 = (f32[3,32,256]{2,1,0:T(8,128)S(1)}, f32[3,32,256]{2,1,0:T(8,128)S(1)}, u32[]{:S(2)}, u32[]{:S(2)}) collective-permute-start(f32[3,32,256]{2,1,0:T(8,128)S(1)} %get-tuple-element.158), channel_id=1, source_target_pairs={{0,8},{8,0},{16,24},{24,16},{32,40},{40,32},{48,56},{56,48},{1,9},... | collective-permute-start | bytes 294920 | tf_op jit(solution)/shard_map/ppermute | solution.py:105
  63.4 4.8 %collective-permute-start.22 = (f32[3,32,256]{2,1,0:T(8,128)S(1)}, f32[3,32,256]{2,1,0:T(8,128)S(1)}, u32[]{:S(2)}, u32[]{:S(2)}) collective-permute-start(f32[3,32,256]{2,1,0:T(8,128)S(1)} %get-tuple-element.157), channel_id=1, source_target_pairs={{0,56},{8,16},{16,8},{24,32},{32,24},{40,48},{48,40},{56,0},{1,57}... | collective-permute-start | bytes 294920 | tf_op jit(solution)/shard_map/ppermute | solution.py:105
  65.4 8.7 %collective-permute-start.15 = (f32[3,32,512]{2,1,0:T(8,128)S(1)}, f32[3,32,512]{2,1,0:T(8,128)S(1)}, u32[]{:S(2)}, u32[]{:S(2)}) collective-permute-start(f32[3,32,512]{2,1,0:T(8,128)S(1)} %pad_maximum_fusion), channel_id=1, source_target_pairs={{0,8},{8,0},{16,24},{24,16},{32,40},{40,32},{48,56},{56,48},{1,9},... | collective-permute-start | bytes 589832 | tf_op jit(solution)/shard_map/ppermute | solution.py:105
  65.8 8.3 %collective-permute-start.16 = (f32[3,32,512]{2,1,0:T(8,128)S(1)}, f32[3,32,512]{2,1,0:T(8,128)S(1)}, u32[]{:S(2)}, u32[]{:S(2)}) collective-permute-start(f32[3,32,512]{2,1,0:T(8,128)S(1)} %pad_maximum_fusion.1), channel_id=1, source_target_pairs={{0,56},{8,16},{16,8},{24,32},{32,24},{40,48},{48,40},{56,0},{1,57}... | collective-permute-start | bytes 589832 | tf_op jit(solution)/shard_map/ppermute | solution.py:105
  68.4 8.3 %collective-permute-start.23 = (f32[3,32,512]{2,1,0:T(8,128)S(1)}, f32[3,32,512]{2,1,0:T(8,128)S(1)}, u32[]{:S(2)}, u32[]{:S(2)}) collective-permute-start(f32[3,32,512]{2,1,0:T(8,128)S(1)} %pad_maximum_fusion.2), channel_id=1, source_target_pairs={{0,8},{8,0},{16,24},{24,16},{32,40},{40,32},{48,56},{56,48},{1,9},... | collective-permute-start | bytes 589832 | tf_op jit(solution)/shard_map/ppermute | solution.py:105
  68.8 7.9 %collective-permute-start.24 = (f32[3,32,512]{2,1,0:T(8,128)S(1)}, f32[3,32,512]{2,1,0:T(8,128)S(1)}, u32[]{:S(2)}, u32[]{:S(2)}) collective-permute-start(f32[3,32,512]{2,1,0:T(8,128)S(1)} %pad_maximum_fusion.3), channel_id=1, source_target_pairs={{0,56},{8,16},{16,8},{24,32},{32,24},{40,48},{48,40},{56,0},{1,57}... | collective-permute-start | bytes 589832 | tf_op jit(solution)/shard_map/ppermute | solution.py:105
  74.2 5.6 %collective-permute-start.17 = (f32[3,32,512]{2,1,0:T(8,128)S(1)}, f32[3,32,512]{2,1,0:T(8,128)S(1)}, u32[]{:S(2)}, u32[]{:S(2)}) collective-permute-start(f32[3,32,512]{2,1,0:T(8,128)S(1)} %get-tuple-element.93), channel_id=1, source_target_pairs={{0,8},{8,0},{16,24},{24,16},{32,40},{40,32},{48,56},{56,48},{1,9},... | collective-permute-start | bytes 589832 | tf_op jit(solution)/shard_map/ppermute | solution.py:105
  74.5 6.7 %collective-permute-start.18 = (f32[3,32,512]{2,1,0:T(8,128)S(1)}, f32[3,32,512]{2,1,0:T(8,128)S(1)}, u32[]{:S(2)}, u32[]{:S(2)}) collective-permute-start(f32[3,32,512]{2,1,0:T(8,128)S(1)} %get-tuple-element.94), channel_id=1, source_target_pairs={{0,56},{8,16},{16,8},{24,32},{32,24},{40,48},{48,40},{56,0},{1,57}... | collective-permute-start | bytes 589832 | tf_op jit(solution)/shard_map/ppermute | solution.py:105
  76.8 6.7 %collective-permute-start.25 = (f32[3,32,512]{2,1,0:T(8,128)S(1)}, f32[3,32,512]{2,1,0:T(8,128)S(1)}, u32[]{:S(2)}, u32[]{:S(2)}) collective-permute-start(f32[3,32,512]{2,1,0:T(8,128)S(1)} %get-tuple-element.108), channel_id=1, source_target_pairs={{0,8},{8,0},{16,24},{24,16},{32,40},{40,32},{48,56},{56,48},{1,9},... | collective-permute-start | bytes 589832 | tf_op jit(solution)/shard_map/ppermute | solution.py:105
  77.0 7.0 %collective-permute-start.26 = (f32[3,32,512]{2,1,0:T(8,128)S(1)}, f32[3,32,512]{2,1,0:T(8,128)S(1)}, u32[]{:S(2)}, u32[]{:S(2)}) collective-permute-start(f32[3,32,512]{2,1,0:T(8,128)S(1)} %get-tuple-element.109), channel_id=1, source_target_pairs={{0,56},{8,16},{16,8},{24,32},{32,24},{40,48},{48,40},{56,0},{1,57}... | collective-permute-start | bytes 589832 | tf_op jit(solution)/shard_map/ppermute | solution.py:105
  81.3 6.9 %collective-permute-start.19 = (f32[3,32,512]{2,1,0:T(8,128)S(1)}, f32[3,32,512]{2,1,0:T(8,128)S(1)}, u32[]{:S(2)}, u32[]{:S(2)}) collective-permute-start(f32[3,32,512]{2,1,0:T(8,128)S(1)} %get-tuple-element.97), channel_id=1, source_target_pairs={{0,8},{8,0},{16,24},{24,16},{32,40},{40,32},{48,56},{56,48},{1,9},... | collective-permute-start | bytes 589832 | tf_op jit(solution)/shard_map/ppermute | solution.py:105
  81.4 8.2 %collective-permute-start.20 = (f32[3,32,512]{2,1,0:T(8,128)S(1)}, f32[3,32,512]{2,1,0:T(8,128)S(1)}, u32[]{:S(2)}, u32[]{:S(2)}) collective-permute-start(f32[3,32,512]{2,1,0:T(8,128)S(1)} %get-tuple-element.98), channel_id=1, source_target_pairs={{0,56},{8,16},{16,8},{24,32},{32,24},{40,48},{48,40},{56,0},{1,57}... | collective-permute-start | bytes 589832 | tf_op jit(solution)/shard_map/ppermute | solution.py:105
  84.0 6.9 %collective-permute-start.27 = (f32[3,32,512]{2,1,0:T(8,128)S(1)}, f32[3,32,512]{2,1,0:T(8,128)S(1)}, u32[]{:S(2)}, u32[]{:S(2)}) collective-permute-start(f32[3,32,512]{2,1,0:T(8,128)S(1)} %get-tuple-element.112), channel_id=1, source_target_pairs={{0,8},{8,0},{16,24},{24,16},{32,40},{40,32},{48,56},{56,48},{1,9},... | collective-permute-start | bytes 589832 | tf_op jit(solution)/shard_map/ppermute | solution.py:105
  84.1 8.9 %collective-permute-start.28 = (f32[3,32,512]{2,1,0:T(8,128)S(1)}, f32[3,32,512]{2,1,0:T(8,128)S(1)}, u32[]{:S(2)}, u32[]{:S(2)}) collective-permute-start(f32[3,32,512]{2,1,0:T(8,128)S(1)} %get-tuple-element.113), channel_id=1, source_target_pairs={{0,56},{8,16},{16,8},{24,32},{32,24},{40,48},{48,40},{56,0},{1,57}... | collective-permute-start | bytes 589832 | tf_op jit(solution)/shard_map/ppermute | solution.py:105
  93.1 5.4 %collective-permute-start.29 = (f32[2,32,512]{2,1,0:T(8,128)S(1)}, f32[2,32,512]{2,1,0:T(8,128)S(1)}, u32[]{:S(2)}, u32[]{:S(2)}) collective-permute-start(f32[2,32,512]{2,1,0:T(8,128)S(1)} %pad_maximum_fusion.4), channel_id=1, source_target_pairs={{0,128},{64,192},{128,0},{192,64},{1,129},{65,193},{129,1},{193,65... | collective-permute-start | bytes 393224 | tf_op jit(solution)/shard_map/ppermute | solution.py:240
  95.7 5.1 %collective-permute-start.31 = (f32[2,32,512]{2,1,0:T(8,128)S(1)}, f32[2,32,512]{2,1,0:T(8,128)S(1)}, u32[]{:S(2)}, u32[]{:S(2)}) collective-permute-start(f32[2,32,512]{2,1,0:T(8,128)S(1)} %pad_maximum_fusion.6), channel_id=1, source_target_pairs={{0,192},{64,128},{128,64},{192,0},{1,193},{65,129},{129,65},{193,1... | collective-permute-start | bytes 393224 | tf_op jit(solution)/shard_map/ppermute | solution.py:242
  100.9 7.3 %collective-permute-start.32 = (f32[64,512]{1,0:T(8,128)S(1)}, f32[64,512]{1,0:T(8,128)S(1)}, u32[]{:S(2)}, u32[]{:S(2)}) collective-permute-start(f32[64,512]{1,0:T(8,128)S(1)} %get-tuple-element.137), channel_id=1, source_target_pairs={{0,1},{1,0},{2,3},{3,2},{4,5},{5,4},{6,7},{7,6},{8,9},{9,8},{10,11... | collective-permute-start | bytes 393224 | tf_op jit(solution)/shard_map/ppermute | solution.py:248
  (3 other events, 29.0 us)

commit v5 on v4

--- a/solution.py
+++ b/solution.py
@@ -13,6 +13,7 @@
 PART = 32
 ZORDER = (4, 3, -3, 2, -2, 1, -1, 0)
 HEAD = 3
+EARLY = 64
 GROUPS = 8
 
 
@@ -213,19 +214,24 @@
     pair = lax.ppermute(pick(near, not_p, 1), "x", flip(NX, 1))
 
     t2_send, _ = tie((t2_amps, pair))
-    t2_par = lax.ppermute(jnp.where(live, t2_send, 0.0), "x", flip(NX, 1))
-    t2_own = split(True, live_pairs, t2_amps, lax.ppermute(t2_amps, "c", swap))
+    t2_soon, _ = tie((t2_amps[:EARLY], own))
+    t2_lead = lax.ppermute(jnp.where(live[:EARLY], t2_soon, 0.0), "x", flip(NX, 1))
+    t2_par = jnp.concatenate([
+        t2_lead,
+        lax.ppermute(jnp.where(live[EARLY:], t2_send[EARLY:], 0.0), "x", flip(NX, 1)),
+    ])
 
     half = PART // 2
     fars = two[:, half:], one[:, :half]
-    pair, _ = tie((pair, (fars, t2_own)))
+    pair, _ = tie((pair, (fars, t2_lead)))
     far_down, far_up = step(*fars, "y", NY)
     blocks = (own, one, far_up, far_down, two)
     one, two = step(pair, pair, "y", NY)
-    first = chunks(block_sizes, blocks, t2_own, (), 0, NZ)
-
     fars = two[:, half:], one[:, :half]
     fars, _ = tie((fars, (far_down, far_up)))
+    t2_late, _ = tie((t2_amps, fars))
+    t2_own = split(True, live_pairs, t2_late, lax.ppermute(t2_late, "c", swap))
+    first = chunks(block_sizes, blocks, t2_own, (), 0, NZ)
     t2_par, _ = tie((t2_par, fars))
     t2_both, _ = tie(((t2_par, lax.ppermute(t2_par, "c", swap)), first))
     t2_par = split(False, live_pairs, *t2_both)

time: 110 us -> 130 us (1.18)
  waiting for transfers between devices: 47.8 us -> 66.6 us
  starting transfers between devices: 44.8 us -> 46.5 us
    ppermute x2 -> x3, waiting for transfers between devices: 0.01 us -> 21.7 us  [the longest x1 21.2 us: body(): lax.ppermute(jnp.where(live[:EARLY], t2_soon, 0.0), 'x', flip(NX, 1))]
    ppermute x2 -> x3, starting transfers between devices: 0.78 us -> 4.68 us  [the longest x1 3.04 us: body(): t2_own = split(True, live_pairs, t2_late, lax.ppermute(t2_late, 'c', swap))]
    ppermute x1, starting transfers between devices: 1.99 us -> 0.09 us  [body(): t2_both, _ = tie(((t2_par, lax.ppermute(t2_par, 'c', swap)), first))]
    ppermute x12, waiting for transfers between devices: 12.3 us -> 10.5 us  [step(): lax.ppermute(value, axis, even(n))]
    ppermute x12, waiting for transfers between devices: 19.3 us -> 17.8 us  [step(): lax.ppermute(other, axis, odd(n))]
  transfers between devices with their start and end apart: 33 -> 34, of which waited for: 21 -> 22; matrix products, arithmetic and copies ran while one was open for 1% -> 1% of each run, Pallas kernels for 8% -> 7%
where the time goes in v5:
time: 130 us
  waiting for transfers between devices  66.6 us (51%)
  starting transfers between devices  46.5 us (36%)
  Pallas kernels  12.2 us (9%)
  local copies, waits for them, and re-layouts  2.12 us (2%)
    ppermute x12, starting transfers between devices, step(): lax.ppermute(other, axis, odd(n))  23.1 us
    ppermute x1, waiting for transfers between devices, body(): lax.ppermute(jnp.where(live[:EARLY], t2_soon, 0.0), 'x', flip(NX, 1))  21.2 us
    ppermute x12, waiting for transfers between devices, step(): lax.ppermute(other, axis, odd(n))  17.8 us
    ppermute x12, waiting for transfers between devices, step(): lax.ppermute(value, axis, even(n))  10.5 us
    ppermute x1, waiting for transfers between devices, body(): pair = lax.ppermute(pick(near, not_p, 1), 'x', flip(NX, 1))  10.1 us
    pallas_call x3, Pallas kernels, chunks(): pl.pallas_call(functools.partial(chunk_kernel, first_k, count, len(before...  9.92 us
    ppermute x1, starting transfers between devices, body(): other = lax.ppermute(jnp.where(low_c, done[1], done[0]), 'c', swap)  6.88 us
    ppermute x12, starting transfers between devices, step(): lax.ppermute(value, axis, even(n))  4.43 us
  transfers between devices with their start and end apart: 34, of which 22 were waited for; matrix products, arithmetic and copies ran while one was open for 1% of the time, Pallas kernels for 7%

profile of v5, /device:TPU:1, one launch (start us, length us, event | category | flops | bytes accessed | tf_op | source)
XLA Modules:
  0.0 129.6 jit_solution(1898926425929140020)
XLA Ops:
  0.0 1.6 %copy.5 = f32[512,512]{0,1:T(8,128)S(1)} copy(f32[512,512]{1,0:T(8,128)} %param.5) | data formatting | bytes 2097152 | tf_op jit(solution)/shard_map/optimization_barrier | solution.py:201
  1.7 3.3 %collective-permute-start = (f32[4,64,512]{2,1,0:T(8,128)S(1)}, f32[4,64,512]{2,1,0:T(8,128)S(1)}, u32[]{:S(2)}, u32[]{:S(2)}) collective-permute-start(f32[4,64,512]{2,1,0:T(8,128)S(1)} %get-tuple-element.126), channel_id=1, source_target_pairs={{0,1},{1,0},{2,3},{3,2},{4,5},{5,4},{6,7},{7,6},{8,9},{9,8},{10,11... | collective-permute-start | bytes 1572872 | tf_op jit(solution)/shard_map/ppermute | solution.py:211
  5.0 1.5 %collective-permute-done = f32[4,64,512]{2,1,0:T(8,128)S(1)} collective-permute-done((f32[4,64,512]{2,1,0:T(8,128)S(1)}, f32[4,64,512]{2,1,0:T(8,128)S(1)}, u32[]{:S(2)}, u32[]{:S(2)}) %collective-permute-start) | collective-permute-done | bytes 524320 | tf_op jit(solution)/shard_map/ppermute | solution.py:211
  7.7 2.2 %collective-permute-start.2 = (f32[8,32,512]{2,1,0:T(8,128)S(1)}, f32[8,32,512]{2,1,0:T(8,128)S(1)}, u32[]{:S(2)}, u32[]{:S(2)}) collective-permute-start(f32[8,32,512]{2,1,0:T(8,128)S(1)} %get-tuple-element.123.b0), channel_id=1, source_target_pairs={{0,6},{2,4},{4,2},{6,0},{1,7},{3,5},{5,3},{7,1},{8,14},{10,12},{12... | collective-permute-start | bytes 1572872 | tf_op jit(solution)/shard_map/ppermute | solution.py:106
  9.9 10.1 %collective-permute-done.1.b0 = f32[8,32,512]{2,1,0:T(8,128)S(1)} collective-permute-done((f32[8,32,512]{2,1,0:T(8,128)S(1)}, f32[8,32,512]{2,1,0:T(8,128)S(1)}, u32[]{:S(2)}, u32[]{:S(2)}) %collective-permute-start.1) | collective-permute-done | bytes 524320 | tf_op jit(solution)/shard_map/ppermute | solution.py:214
  22.4 21.2 %collective-permute-done.4 = f32[64,512]{1,0:T(8,128)S(1)} collective-permute-done((f32[64,512]{1,0:T(8,128)S(1)}, f32[64,512]{1,0:T(8,128)S(1)}, u32[]{:S(2)}, u32[]{:S(2)}) %collective-permute-start.4) | collective-permute-done | bytes 131104 | tf_op jit(solution)/shard_map/ppermute | solution.py:218
  44.7 1.5 %collective-permute-start.7 = (f32[8,16,512]{2,1,0:T(8,128)S(1)}, f32[8,16,512]{2,1,0:T(8,128)S(1)}, u32[]{:S(2)}, u32[]{:S(2)}) collective-permute-start(f32[8,16,512]{2,1,0:T(8,128)S(1)} %slice.156), channel_id=1, source_target_pairs={{0,2},{2,0},{4,6},{6,4},{1,3},{3,1},{5,7},{7,5},{8,10},{10,8},{12,... | collective-permute-start | bytes 786440 | tf_op jit(solution)/shard_map/ppermute | solution.py:106
  46.1 1.7 %collective-permute-start.8 = (f32[8,16,512]{2,1,0:T(8,128)S(1)}, f32[8,16,512]{2,1,0:T(8,128)S(1)}, u32[]{:S(2)}, u32[]{:S(2)}) collective-permute-start(f32[8,16,512]{2,1,0:T(8,128)S(1)} %slice.157), channel_id=1, source_target_pairs={{0,6},{2,4},{4,2},{6,0},{1,7},{3,5},{5,3},{7,1},{8,14},{10,12},{12... | collective-permute-start | bytes 786440 | tf_op jit(solution)/shard_map/ppermute | solution.py:106
  47.8 8.4 %collective-permute-done.6.b3 = f32[8,32,512]{2,1,0:T(8,128)S(1)} collective-permute-done((f32[8,32,512]{2,1,0:T(8,128)S(1)}, f32[8,32,512]{2,1,0:T(8,128)S(1)}, u32[]{:S(2)}, u32[]{:S(2)}) %collective-permute-start.6) | collective-permute-done | bytes 524320 | tf_op jit(solution)/shard_map/ppermute | solution.py:106
  56.2 5.1 %collective-permute-done.7.b2d = f32[8,16,512]{2,1,0:T(8,128)S(1)} collective-permute-done((f32[8,16,512]{2,1,0:T(8,128)S(1)}, f32[8,16,512]{2,1,0:T(8,128)S(1)}, u32[]{:S(2)}, u32[]{:S(2)}) %collective-permute-start.7) | collective-permute-done | bytes 262176 | tf_op jit(solution)/shard_map/ppermute | solution.py:106
  61.8 3.0 %collective-permute-start.13 = (f32[512,512]{1,0:T(8,128)S(1)}, f32[512,512]{1,0:T(8,128)S(1)}, u32[]{:S(2)}, u32[]{:S(2)}) collective-permute-start(f32[512,512]{1,0:T(8,128)S(1)} %copy-done), channel_id=1, source_target_pairs={{0,1},{1,0},{2,3},{3,2},{4,5},{5,4},{6,7},{7,6},{8,9},{9,8},{10,11... | collective-permute-start | bytes 3145736 | tf_op jit(solution)/shard_map/ppermute | solution.py:233
  65.1 1.6 %collective-permute-start.9 = (f32[8,16,512]{2,1,0:T(8,128)S(1)}, f32[8,16,512]{2,1,0:T(8,128)S(1)}, u32[]{:S(2)}, u32[]{:S(2)}) collective-permute-start(f32[8,16,512]{2,1,0:T(8,128)S(1)} %slice.160), channel_id=1, source_target_pairs={{0,6},{2,4},{4,2},{6,0},{1,7},{3,5},{5,3},{7,1},{8,14},{10,12},{12... | collective-permute-start | bytes 786440 | tf_op jit(solution)/shard_map/ppermute | solution.py:106
  67.8 4.5 %shard_map.47 = (f32[8,3,32,512]{3,2,1,0:T(8,128)S(1)}, f32[8,3,32,512]{3,2,1,0:T(8,128)S(1)}) custom-call(s32[8]{0:T(128)S(1)} %copy-done.1, f32[8,32,512]{2,1,0:T(8,128)S(1)} %get-tuple-element.123.b0, f32[8,32,512]{2,1,0:T(8,128)S(1)} %collective-permute-done.3.b1, f32[8,16,512]{2,1,0:T(8,128)S(1)} %collective-permute-done.8.b2u, ...), custom_call_target="tpu_custom_call" | custom-call | flops 3221225472 | bytes 7340032 | tf_op jit(solution)/shard_map/pallas_call | solution.py:80
  73.9 2.2 %shard_map.49 = (f32[3,3,32,512]{3,2,1,0:T(8,128)S(1)}, f32[3,3,32,512]{3,2,1,0:T(8,128)S(1)}) custom-call(s32[8]{0:T(128)S(1)} %copy-done.1, f32[8,32,512]{2,1,0:T(8,128)S(1)} %collective-permute-done.1.b0, f32[8,32,512]{2,1,0:T(8,128)S(1)} %collective-permute-done.5.b1, f32[8,16,512]{2,1,0:T(8,128)S(1)} %collective-permute-done.9.b2u, ...), custom_call_target="tpu_custom_call" | custom-call | flops 1207959552 | bytes 4063232 | tf_op jit(solution)/shard_map/pallas_call | solution.py:80
  77.6 4.7 %collective-permute-start.15 = (f32[3,32,256]{2,1,0:T(8,128)S(1)}, f32[3,32,256]{2,1,0:T(8,128)S(1)}, u32[]{:S(2)}, u32[]{:S(2)}) collective-permute-start(f32[3,32,256]{2,1,0:T(8,128)S(1)} %get-tuple-element.155), channel_id=1, source_target_pairs={{0,56},{8,16},{16,8},{24,32},{32,24},{40,48},{48,40},{56,0},{1,57}... | collective-permute-start | bytes 294920 | tf_op jit(solution)/shard_map/ppermute | solution.py:106
  82.3 1.4 %collective-permute-start.23 = (f32[3,32,256]{2,1,0:T(8,128)S(1)}, f32[3,32,256]{2,1,0:T(8,128)S(1)}, u32[]{:S(2)}, u32[]{:S(2)}) collective-permute-start(f32[3,32,256]{2,1,0:T(8,128)S(1)} %get-tuple-element.161), channel_id=1, source_target_pairs={{0,56},{8,16},{16,8},{24,32},{32,24},{40,48},{48,40},{56,0},{1,57}... | collective-permute-start | bytes 294920 | tf_op jit(solution)/shard_map/ppermute | solution.py:106
  84.7 2.5 %collective-permute-start.17 = (f32[3,32,512]{2,1,0:T(8,128)S(1)}, f32[3,32,512]{2,1,0:T(8,128)S(1)}, u32[]{:S(2)}, u32[]{:S(2)}) collective-permute-start(f32[3,32,512]{2,1,0:T(8,128)S(1)} %pad_maximum_fusion.2), channel_id=1, source_target_pairs={{0,56},{8,16},{16,8},{24,32},{32,24},{40,48},{48,40},{56,0},{1,57}... | collective-permute-start | bytes 589832 | tf_op jit(solution)/shard_map/ppermute | solution.py:106
  87.7 1.8 %collective-permute-start.25 = (f32[3,32,512]{2,1,0:T(8,128)S(1)}, f32[3,32,512]{2,1,0:T(8,128)S(1)}, u32[]{:S(2)}, u32[]{:S(2)}) collective-permute-start(f32[3,32,512]{2,1,0:T(8,128)S(1)} %pad_maximum_fusion.4), channel_id=1, source_target_pairs={{0,56},{8,16},{16,8},{24,32},{32,24},{40,48},{48,40},{56,0},{1,57}... | collective-permute-start | bytes 589832 | tf_op jit(solution)/shard_map/ppermute | solution.py:106
  89.5 3.2 %shard_map.50 = (f32[5,3,32,512]{3,2,1,0:T(8,128)S(1)}, f32[5,3,32,512]{3,2,1,0:T(8,128)S(1)}) custom-call(s32[8]{0:T(128)S(1)} %copy-done.1, f32[8,32,512]{2,1,0:T(8,128)S(1)} %collective-permute-done.1.b0, f32[8,32,512]{2,1,0:T(8,128)S(1)} %collective-permute-done.5.b1, f32[8,16,512]{2,1,0:T(8,128)S(1)} %collective-permute-done.9.b2u, ...), custom_call_target="tpu_custom_call" | custom-call | flops 2013265920 | bytes 5373952 | tf_op jit(solution)/shard_map/pallas_call | solution.py:80
  93.2 2.1 %collective-permute-start.19 = (f32[3,32,512]{2,1,0:T(8,128)S(1)}, f32[3,32,512]{2,1,0:T(8,128)S(1)}, u32[]{:S(2)}, u32[]{:S(2)}) collective-permute-start(f32[3,32,512]{2,1,0:T(8,128)S(1)} %get-tuple-element.98), channel_id=1, source_target_pairs={{0,56},{8,16},{16,8},{24,32},{32,24},{40,48},{48,40},{56,0},{1,57}... | collective-permute-start | bytes 589832 | tf_op jit(solution)/shard_map/ppermute | solution.py:106
  96.8 2.1 %collective-permute-done.18 = f32[3,32,512]{2,1,0:T(8,128)S(1)} collective-permute-done((f32[3,32,512]{2,1,0:T(8,128)S(1)}, f32[3,32,512]{2,1,0:T(8,128)S(1)}, u32[]{:S(2)}, u32[]{:S(2)}) %collective-permute-start.18) | collective-permute-done | bytes 196640 | tf_op jit(solution)/shard_map/ppermute | solution.py:106
  98.9 1.6 %collective-permute-done.19 = f32[3,32,512]{2,1,0:T(8,128)S(1)} collective-permute-done((f32[3,32,512]{2,1,0:T(8,128)S(1)}, f32[3,32,512]{2,1,0:T(8,128)S(1)}, u32[]{:S(2)}, u32[]{:S(2)}) %collective-permute-start.19) | collective-permute-done | bytes 196640 | tf_op jit(solution)/shard_map/ppermute | solution.py:106
  100.6 1.5 %collective-permute-start.21 = (f32[3,32,512]{2,1,0:T(8,128)S(1)}, f32[3,32,512]{2,1,0:T(8,128)S(1)}, u32[]{:S(2)}, u32[]{:S(2)}) collective-permute-start(f32[3,32,512]{2,1,0:T(8,128)S(1)} %get-tuple-element.102), channel_id=1, source_target_pairs={{0,56},{8,16},{16,8},{24,32},{32,24},{40,48},{48,40},{56,0},{1,57}... | collective-permute-start | bytes 589832 | tf_op jit(solution)/shard_map/ppermute | solution.py:106
  103.3 1.9 %collective-permute-start.29 = (f32[3,32,512]{2,1,0:T(8,128)S(1)}, f32[3,32,512]{2,1,0:T(8,128)S(1)}, u32[]{:S(2)}, u32[]{:S(2)}) collective-permute-start(f32[3,32,512]{2,1,0:T(8,128)S(1)} %get-tuple-element.117), channel_id=1, source_target_pairs={{0,56},{8,16},{16,8},{24,32},{32,24},{40,48},{48,40},{56,0},{1,57}... | collective-permute-start | bytes 589832 | tf_op jit(solution)/shard_map/ppermute | solution.py:106
  105.2 1.8 %collective-permute-done.20 = f32[3,32,512]{2,1,0:T(8,128)S(1)} collective-permute-done((f32[3,32,512]{2,1,0:T(8,128)S(1)}, f32[3,32,512]{2,1,0:T(8,128)S(1)}, u32[]{:S(2)}, u32[]{:S(2)}) %collective-permute-start.20) | collective-permute-done | bytes 196640 | tf_op jit(solution)/shard_map/ppermute | solution.py:106
  107.0 1.9 %collective-permute-done.21 = f32[3,32,512]{2,1,0:T(8,128)S(1)} collective-permute-done((f32[3,32,512]{2,1,0:T(8,128)S(1)}, f32[3,32,512]{2,1,0:T(8,128)S(1)}, u32[]{:S(2)}, u32[]{:S(2)}) %collective-permute-start.21) | collective-permute-done | bytes 196640 | tf_op jit(solution)/shard_map/ppermute | solution.py:106
  110.3 2.0 %collective-permute-done.29 = f32[3,32,512]{2,1,0:T(8,128)S(1)} collective-permute-done((f32[3,32,512]{2,1,0:T(8,128)S(1)}, f32[3,32,512]{2,1,0:T(8,128)S(1)}, u32[]{:S(2)}, u32[]{:S(2)}) %collective-permute-start.29) | collective-permute-done | bytes 196640 | tf_op jit(solution)/shard_map/ppermute | solution.py:106
  112.4 2.8 %collective-permute-start.30 = (f32[2,32,512]{2,1,0:T(8,128)S(1)}, f32[2,32,512]{2,1,0:T(8,128)S(1)}, u32[]{:S(2)}, u32[]{:S(2)}) collective-permute-start(f32[2,32,512]{2,1,0:T(8,128)S(1)} %pad_maximum_fusion.5), channel_id=1, source_target_pairs={{0,128},{64,192},{128,0},{192,64},{1,129},{65,193},{129,1},{193,65... | collective-permute-start | bytes 393224 | tf_op jit(solution)/shard_map/ppermute | solution.py:246
  116.3 1.5 %collective-permute-done.30 = f32[2,32,512]{2,1,0:T(8,128)S(1)} collective-permute-done((f32[2,32,512]{2,1,0:T(8,128)S(1)}, f32[2,32,512]{2,1,0:T(8,128)S(1)}, u32[]{:S(2)}, u32[]{:S(2)}) %collective-permute-start.30) | collective-permute-done | bytes 131104 | tf_op jit(solution)/shard_map/ppermute | solution.py:246
  117.8 2.5 %collective-permute-done.32 = f32[2,32,512]{2,1,0:T(8,128)S(1)} collective-permute-done((f32[2,32,512]{2,1,0:T(8,128)S(1)}, f32[2,32,512]{2,1,0:T(8,128)S(1)}, u32[]{:S(2)}, u32[]{:S(2)}) %collective-permute-start.32) | collective-permute-done | bytes 131104 | tf_op jit(solution)/shard_map/ppermute | solution.py:248
  120.4 6.9 %collective-permute-start.33 = (f32[64,512]{1,0:T(8,128)S(1)}, f32[64,512]{1,0:T(8,128)S(1)}, u32[]{:S(2)}, u32[]{:S(2)}) collective-permute-start(f32[64,512]{1,0:T(8,128)S(1)} %get-tuple-element.141), channel_id=1, source_target_pairs={{0,1},{1,0},{2,3},{3,2},{4,5},{5,4},{6,7},{7,6},{8,9},{9,8},{10,11... | collective-permute-start | bytes 393224 | tf_op jit(solution)/shard_map/ppermute | solution.py:254
  128.3 1.3 %shard_map.51 = f32[128,512]{1,0:T(8,128)} custom-call(s32[8]{0:T(128)S(1)} %copy-done.1, f32[64,512]{1,0:T(8,128)S(1)} %get-tuple-element.142.mine, f32[64,512]{1,0:T(8,128)S(1)} %collective-permute-done.33.other), custom_call_target="tpu_custom_call" | custom-call | bytes 524288 | tf_op jit(solution)/shard_map/pallas_call | solution.py:186
  (88 shorter events, 17.1 us)
Async XLA Ops:
  1.7 4.9 %collective-permute-start = (f32[4,64,512]{2,1,0:T(8,128)S(1)}, f32[4,64,512]{2,1,0:T(8,128)S(1)}, u32[]{:S(2)}, u32[]{:S(2)}) collective-permute-start(f32[4,64,512]{2,1,0:T(8,128)S(1)} %get-tuple-element.126), channel_id=1, source_target_pairs={{0,1},{1,0},{2,3},{3,2},{4,5},{5,4},{6,7},{7,6},{8,9},{9,8},{10,11... | collective-permute-start | bytes 1572872 | tf_op jit(solution)/shard_map/ppermute | solution.py:211
  6.8 13.2 %collective-permute-start.1 = (f32[8,32,512]{2,1,0:T(8,128)S(1)}, f32[8,32,512]{2,1,0:T(8,128)S(1)}, u32[]{:S(2)}, u32[]{:S(2)}) collective-permute-start(f32[8,32,512]{2,1,0:T(8,128)S(1)} %get-tuple-element.124), channel_id=1, source_target_pairs={{0,64},{64,0},{128,192},{192,128},{1,65},{65,1},{129,193},{193,129... | collective-permute-start | bytes 1572872 | tf_op jit(solution)/shard_map/ppermute | solution.py:214
  7.7 14.4 %collective-permute-start.2 = (f32[8,32,512]{2,1,0:T(8,128)S(1)}, f32[8,32,512]{2,1,0:T(8,128)S(1)}, u32[]{:S(2)}, u32[]{:S(2)}) collective-permute-start(f32[8,32,512]{2,1,0:T(8,128)S(1)} %get-tuple-element.123.b0), channel_id=1, source_target_pairs={{0,6},{2,4},{4,2},{6,0},{1,7},{3,5},{5,3},{7,1},{8,14},{10,12},{12... | collective-permute-start | bytes 1572872 | tf_op jit(solution)/shard_map/ppermute | solution.py:106
  9.9 12.5 %collective-permute-start.3 = (f32[8,32,512]{2,1,0:T(8,128)S(1)}, f32[8,32,512]{2,1,0:T(8,128)S(1)}, u32[]{:S(2)}, u32[]{:S(2)}) collective-permute-start(f32[8,32,512]{2,1,0:T(8,128)S(1)} %get-tuple-element.123.b0), channel_id=1, source_target_pairs={{0,2},{2,0},{4,6},{6,4},{1,3},{3,1},{5,7},{7,5},{8,10},{10,8},{12,... | collective-permute-start | bytes 1572872 | tf_op jit(solution)/shard_map/ppermute | solution.py:106
  20.1 44.7 %collective-permute-start.11 = (f32[448,512]{1,0:T(8,128)S(1)}, f32[448,512]{1,0:T(8,128)S(1)}, u32[]{:S(2)}, u32[]{:S(2)}) collective-permute-start(f32[448,512]{1,0:T(8,128)S(1)} %slice_select_fusion), channel_id=1, source_target_pairs={{0,64},{64,0},{128,192},{192,128},{1,65},{65,1},{129,193},{193,129... | collective-permute-start | bytes 2752520 | tf_op jit(solution)/shard_map/ppermute | solution.py:221
  20.6 23.0 %collective-permute-start.4 = (f32[64,512]{1,0:T(8,128)S(1)}, f32[64,512]{1,0:T(8,128)S(1)}, u32[]{:S(2)}, u32[]{:S(2)}) collective-permute-start(f32[64,512]{1,0:T(8,128)S(1)} %broadcast_select_fusion), channel_id=1, source_target_pairs={{0,64},{64,0},{128,192},{192,128},{1,65},{65,1},{129,193},{193,129... | collective-permute-start | bytes 393224 | tf_op jit(solution)/shard_map/ppermute | solution.py:218
  43.7 12.5 %collective-permute-start.6 = (f32[8,32,512]{2,1,0:T(8,128)S(1)}, f32[8,32,512]{2,1,0:T(8,128)S(1)}, u32[]{:S(2)}, u32[]{:S(2)}) collective-permute-start(f32[8,32,512]{2,1,0:T(8,128)S(1)} %collective-permute-done.1.b0), channel_id=1, source_target_pairs={{0,6},{2,4},{4,2},{6,0},{1,7},{3,5},{5,3},{7,1},{8,14},{10,12},{12... | collective-permute-start | bytes 1572872 | tf_op jit(solution)/shard_map/ppermute | solution.py:106
  44.7 11.5 %collective-permute-start.5 = (f32[8,32,512]{2,1,0:T(8,128)S(1)}, f32[8,32,512]{2,1,0:T(8,128)S(1)}, u32[]{:S(2)}, u32[]{:S(2)}) collective-permute-start(f32[8,32,512]{2,1,0:T(8,128)S(1)} %collective-permute-done.1.b0), channel_id=1, source_target_pairs={{0,2},{2,0},{4,6},{6,4},{1,3},{3,1},{5,7},{7,5},{8,10},{10,8},{12,... | collective-permute-start | bytes 1572872 | tf_op jit(solution)/shard_map/ppermute | solution.py:106
  44.7 16.6 %collective-permute-start.7 = (f32[8,16,512]{2,1,0:T(8,128)S(1)}, f32[8,16,512]{2,1,0:T(8,128)S(1)}, u32[]{:S(2)}, u32[]{:S(2)}) collective-permute-start(f32[8,16,512]{2,1,0:T(8,128)S(1)} %slice.156), channel_id=1, source_target_pairs={{0,2},{2,0},{4,6},{6,4},{1,3},{3,1},{5,7},{7,5},{8,10},{10,8},{12,... | collective-permute-start | bytes 786440 | tf_op jit(solution)/shard_map/ppermute | solution.py:106
  46.1 15.7 %collective-permute-start.8 = (f32[8,16,512]{2,1,0:T(8,128)S(1)}, f32[8,16,512]{2,1,0:T(8,128)S(1)}, u32[]{:S(2)}, u32[]{:S(2)}) collective-permute-start(f32[8,16,512]{2,1,0:T(8,128)S(1)} %slice.157), channel_id=1, source_target_pairs={{0,6},{2,4},{4,2},{6,0},{1,7},{3,5},{5,3},{7,1},{8,14},{10,12},{12... | collective-permute-start | bytes 786440 | tf_op jit(solution)/shard_map/ppermute | solution.py:106
  61.8 5.3 %collective-permute-start.13 = (f32[512,512]{1,0:T(8,128)S(1)}, f32[512,512]{1,0:T(8,128)S(1)}, u32[]{:S(2)}, u32[]{:S(2)}) collective-permute-start(f32[512,512]{1,0:T(8,128)S(1)} %copy-done), channel_id=1, source_target_pairs={{0,1},{1,0},{2,3},{3,2},{4,5},{5,4},{6,7},{7,6},{8,9},{9,8},{10,11... | collective-permute-start | bytes 3145736 | tf_op jit(solution)/shard_map/ppermute | solution.py:233
  64.9 7.4 %collective-permute-start.12 = (f32[512,512]{1,0:T(8,128)S(1)}, f32[512,512]{1,0:T(8,128)S(1)}, u32[]{:S(2)}, u32[]{:S(2)}) collective-permute-start(f32[512,512]{1,0:T(8,128)S(1)} %pad_maximum_fusion.mine), channel_id=1, source_target_pairs={{0,1},{1,0},{2,3},{3,2},{4,5},{5,4},{6,7},{7,6},{8,9},{9,8},{10,11... | collective-permute-start | bytes 3145736 | tf_op jit(solution)/shard_map/ppermute | solution.py:236
  65.0 7.6 %collective-permute-start.10 = (f32[8,16,512]{2,1,0:T(8,128)S(1)}, f32[8,16,512]{2,1,0:T(8,128)S(1)}, u32[]{:S(2)}, u32[]{:S(2)}) collective-permute-start(f32[8,16,512]{2,1,0:T(8,128)S(1)} %slice.159), channel_id=1, source_target_pairs={{0,2},{2,0},{4,6},{6,4},{1,3},{3,1},{5,7},{7,5},{8,10},{10,8},{12,... | collective-permute-start | bytes 786440 | tf_op jit(solution)/shard_map/ppermute | solution.py:106
  65.1 8.8 %collective-permute-start.9 = (f32[8,16,512]{2,1,0:T(8,128)S(1)}, f32[8,16,512]{2,1,0:T(8,128)S(1)}, u32[]{:S(2)}, u32[]{:S(2)}) collective-permute-start(f32[8,16,512]{2,1,0:T(8,128)S(1)} %slice.160), channel_id=1, source_target_pairs={{0,6},{2,4},{4,2},{6,0},{1,7},{3,5},{5,3},{7,1},{8,14},{10,12},{12... | collective-permute-start | bytes 786440 | tf_op jit(solution)/shard_map/ppermute | solution.py:106
  76.3 7.5 %collective-permute-start.14 = (f32[3,32,256]{2,1,0:T(8,128)S(1)}, f32[3,32,256]{2,1,0:T(8,128)S(1)}, u32[]{:S(2)}, u32[]{:S(2)}) collective-permute-start(f32[3,32,256]{2,1,0:T(8,128)S(1)} %get-tuple-element.156), channel_id=1, source_target_pairs={{0,8},{8,0},{16,24},{24,16},{32,40},{40,32},{48,56},{56,48},{1,9},... | collective-permute-start | bytes 294920 | tf_op jit(solution)/shard_map/ppermute | solution.py:106
  77.6 6.7 %collective-permute-start.15 = (f32[3,32,256]{2,1,0:T(8,128)S(1)}, f32[3,32,256]{2,1,0:T(8,128)S(1)}, u32[]{:S(2)}, u32[]{:S(2)}) collective-permute-start(f32[3,32,256]{2,1,0:T(8,128)S(1)} %get-tuple-element.155), channel_id=1, source_target_pairs={{0,56},{8,16},{16,8},{24,32},{32,24},{40,48},{48,40},{56,0},{1,57}... | collective-permute-start | bytes 294920 | tf_op jit(solution)/shard_map/ppermute | solution.py:106
  82.2 4.9 %collective-permute-start.22 = (f32[3,32,256]{2,1,0:T(8,128)S(1)}, f32[3,32,256]{2,1,0:T(8,128)S(1)}, u32[]{:S(2)}, u32[]{:S(2)}) collective-permute-start(f32[3,32,256]{2,1,0:T(8,128)S(1)} %get-tuple-element.162), channel_id=1, source_target_pairs={{0,8},{8,0},{16,24},{24,16},{32,40},{40,32},{48,56},{56,48},{1,9},... | collective-permute-start | bytes 294920 | tf_op jit(solution)/shard_map/ppermute | solution.py:106
  84.3 8.4 %collective-permute-start.16 = (f32[3,32,512]{2,1,0:T(8,128)S(1)}, f32[3,32,512]{2,1,0:T(8,128)S(1)}, u32[]{:S(2)}, u32[]{:S(2)}) collective-permute-start(f32[3,32,512]{2,1,0:T(8,128)S(1)} %pad_maximum_fusion.1), channel_id=1, source_target_pairs={{0,8},{8,0},{16,24},{24,16},{32,40},{40,32},{48,56},{56,48},{1,9},... | collective-permute-start | bytes 589832 | tf_op jit(solution)/shard_map/ppermute | solution.py:106
  84.7 8.0 %collective-permute-start.17 = (f32[3,32,512]{2,1,0:T(8,128)S(1)}, f32[3,32,512]{2,1,0:T(8,128)S(1)}, u32[]{:S(2)}, u32[]{:S(2)}) collective-permute-start(f32[3,32,512]{2,1,0:T(8,128)S(1)} %pad_maximum_fusion.2), channel_id=1, source_target_pairs={{0,56},{8,16},{16,8},{24,32},{32,24},{40,48},{48,40},{56,0},{1,57}... | collective-permute-start | bytes 589832 | tf_op jit(solution)/shard_map/ppermute | solution.py:106
  87.3 8.0 %collective-permute-start.24 = (f32[3,32,512]{2,1,0:T(8,128)S(1)}, f32[3,32,512]{2,1,0:T(8,128)S(1)}, u32[]{:S(2)}, u32[]{:S(2)}) collective-permute-start(f32[3,32,512]{2,1,0:T(8,128)S(1)} %pad_maximum_fusion.3), channel_id=1, source_target_pairs={{0,8},{8,0},{16,24},{24,16},{32,40},{40,32},{48,56},{56,48},{1,9},... | collective-permute-start | bytes 589832 | tf_op jit(solution)/shard_map/ppermute | solution.py:106
  87.7 8.0 %collective-permute-start.25 = (f32[3,32,512]{2,1,0:T(8,128)S(1)}, f32[3,32,512]{2,1,0:T(8,128)S(1)}, u32[]{:S(2)}, u32[]{:S(2)}) collective-permute-start(f32[3,32,512]{2,1,0:T(8,128)S(1)} %pad_maximum_fusion.4), channel_id=1, source_target_pairs={{0,56},{8,16},{16,8},{24,32},{32,24},{40,48},{48,40},{56,0},{1,57}... | collective-permute-start | bytes 589832 | tf_op jit(solution)/shard_map/ppermute | solution.py:106
  92.8 6.1 %collective-permute-start.18 = (f32[3,32,512]{2,1,0:T(8,128)S(1)}, f32[3,32,512]{2,1,0:T(8,128)S(1)}, u32[]{:S(2)}, u32[]{:S(2)}) collective-permute-start(f32[3,32,512]{2,1,0:T(8,128)S(1)} %get-tuple-element.97), channel_id=1, source_target_pairs={{0,8},{8,0},{16,24},{24,16},{32,40},{40,32},{48,56},{56,48},{1,9},... | collective-permute-start | bytes 589832 | tf_op jit(solution)/shard_map/ppermute | solution.py:106
  93.2 7.3 %collective-permute-start.19 = (f32[3,32,512]{2,1,0:T(8,128)S(1)}, f32[3,32,512]{2,1,0:T(8,128)S(1)}, u32[]{:S(2)}, u32[]{:S(2)}) collective-permute-start(f32[3,32,512]{2,1,0:T(8,128)S(1)} %get-tuple-element.98), channel_id=1, source_target_pairs={{0,56},{8,16},{16,8},{24,32},{32,24},{40,48},{48,40},{56,0},{1,57}... | collective-permute-start | bytes 589832 | tf_op jit(solution)/shard_map/ppermute | solution.py:106
  95.8 6.3 %collective-permute-start.26 = (f32[3,32,512]{2,1,0:T(8,128)S(1)}, f32[3,32,512]{2,1,0:T(8,128)S(1)}, u32[]{:S(2)}, u32[]{:S(2)}) collective-permute-start(f32[3,32,512]{2,1,0:T(8,128)S(1)} %get-tuple-element.112), channel_id=1, source_target_pairs={{0,8},{8,0},{16,24},{24,16},{32,40},{40,32},{48,56},{56,48},{1,9},... | collective-permute-start | bytes 589832 | tf_op jit(solution)/shard_map/ppermute | solution.py:106
  95.9 7.2 %collective-permute-start.27 = (f32[3,32,512]{2,1,0:T(8,128)S(1)}, f32[3,32,512]{2,1,0:T(8,128)S(1)}, u32[]{:S(2)}, u32[]{:S(2)}) collective-permute-start(f32[3,32,512]{2,1,0:T(8,128)S(1)} %get-tuple-element.113), channel_id=1, source_target_pairs={{0,56},{8,16},{16,8},{24,32},{32,24},{40,48},{48,40},{56,0},{1,57}... | collective-permute-start | bytes 589832 | tf_op jit(solution)/shard_map/ppermute | solution.py:106
  100.5 6.4 %collective-permute-start.20 = (f32[3,32,512]{2,1,0:T(8,128)S(1)}, f32[3,32,512]{2,1,0:T(8,128)S(1)}, u32[]{:S(2)}, u32[]{:S(2)}) collective-permute-start(f32[3,32,512]{2,1,0:T(8,128)S(1)} %get-tuple-element.101), channel_id=1, source_target_pairs={{0,8},{8,0},{16,24},{24,16},{32,40},{40,32},{48,56},{56,48},{1,9},... | collective-permute-start | bytes 589832 | tf_op jit(solution)/shard_map/ppermute | solution.py:106
  100.6 8.3 %collective-permute-start.21 = (f32[3,32,512]{2,1,0:T(8,128)S(1)}, f32[3,32,512]{2,1,0:T(8,128)S(1)}, u32[]{:S(2)}, u32[]{:S(2)}) collective-permute-start(f32[3,32,512]{2,1,0:T(8,128)S(1)} %get-tuple-element.102), channel_id=1, source_target_pairs={{0,56},{8,16},{16,8},{24,32},{32,24},{40,48},{48,40},{56,0},{1,57}... | collective-permute-start | bytes 589832 | tf_op jit(solution)/shard_map/ppermute | solution.py:106
  103.2 7.1 %collective-permute-start.28 = (f32[3,32,512]{2,1,0:T(8,128)S(1)}, f32[3,32,512]{2,1,0:T(8,128)S(1)}, u32[]{:S(2)}, u32[]{:S(2)}) collective-permute-start(f32[3,32,512]{2,1,0:T(8,128)S(1)} %get-tuple-element.116), channel_id=1, source_target_pairs={{0,8},{8,0},{16,24},{24,16},{32,40},{40,32},{48,56},{56,48},{1,9},... | collective-permute-start | bytes 589832 | tf_op jit(solution)/shard_map/ppermute | solution.py:106
  103.3 9.0 %collective-permute-start.29 = (f32[3,32,512]{2,1,0:T(8,128)S(1)}, f32[3,32,512]{2,1,0:T(8,128)S(1)}, u32[]{:S(2)}, u32[]{:S(2)}) collective-permute-start(f32[3,32,512]{2,1,0:T(8,128)S(1)} %get-tuple-element.117), channel_id=1, source_target_pairs={{0,56},{8,16},{16,8},{24,32},{32,24},{40,48},{48,40},{56,0},{1,57}... | collective-permute-start | bytes 589832 | tf_op jit(solution)/shard_map/ppermute | solution.py:106
  112.4 5.4 %collective-permute-start.30 = (f32[2,32,512]{2,1,0:T(8,128)S(1)}, f32[2,32,512]{2,1,0:T(8,128)S(1)}, u32[]{:S(2)}, u32[]{:S(2)}) collective-permute-start(f32[2,32,512]{2,1,0:T(8,128)S(1)} %pad_maximum_fusion.5), channel_id=1, source_target_pairs={{0,128},{64,192},{128,0},{192,64},{1,129},{65,193},{129,1},{193,65... | collective-permute-start | bytes 393224 | tf_op jit(solution)/shard_map/ppermute | solution.py:246
  115.2 5.1 %collective-permute-start.32 = (f32[2,32,512]{2,1,0:T(8,128)S(1)}, f32[2,32,512]{2,1,0:T(8,128)S(1)}, u32[]{:S(2)}, u32[]{:S(2)}) collective-permute-start(f32[2,32,512]{2,1,0:T(8,128)S(1)} %pad_maximum_fusion.7), channel_id=1, source_target_pairs={{0,192},{64,128},{128,64},{192,0},{1,193},{65,129},{129,65},{193,1... | collective-permute-start | bytes 393224 | tf_op jit(solution)/shard_map/ppermute | solution.py:248
  120.4 7.9 %collective-permute-start.33 = (f32[64,512]{1,0:T(8,128)S(1)}, f32[64,512]{1,0:T(8,128)S(1)}, u32[]{:S(2)}, u32[]{:S(2)}) collective-permute-start(f32[64,512]{1,0:T(8,128)S(1)} %get-tuple-element.141), channel_id=1, source_target_pairs={{0,1},{1,0},{2,3},{3,2},{4,5},{5,4},{6,7},{7,6},{8,9},{9,8},{10,11... | collective-permute-start | bytes 393224 | tf_op jit(solution)/shard_map/ppermute | solution.py:254
  (5 other events, 39.0 us)

commit v6 on v4

--- a/solution.py
+++ b/solution.py
@@ -16,6 +16,10 @@
 GROUPS = 8
 
 
+def ring(n, away):
+    return [(i, (i + away) % n) for i in range(n)]
+
+
 def even(n):
     return [(i, i ^ 1) for i in range(n)]
 
@@ -38,8 +42,7 @@
 def chunk_kernel(first_k, count, adds, sizes, b0, b1, b2u, b2d, b3, top, low, *refs):
     before, outs, stage = refs[:adds], refs[adds:-1], refs[-1]
     x, z, y, c = place_of()
-    sign = 1 - 2 * (z & 1)
-    order = [(z + d * sign) & (NZ - 1) for d in ZORDER[first_k:first_k + count]]
+    order = [(z + d) & (NZ - 1) for d in ZORDER[first_k:first_k + count]]
     lam = []
     for zz in order:
         lam += [b0[zz], b1[zz], b2u[zz], b2d[zz], b3[zz]]
@@ -105,17 +108,21 @@
     return lax.ppermute(value, axis, even(n)), lax.ppermute(other, axis, odd(n))
 
 
+def turn(up, down):
+    return lax.ppermute(up, "z", ring(NZ, 1)), lax.ppermute(down, "z", ring(NZ, -1))
+
+
 def z_first(part):
     half = part[0].shape[-1] // 2
-    one, two = tie(step(part[0][..., :half], part[0][..., half:], "z", NZ))
-    return tie((add_right(part[1], two), add_left(part[2], one)))
+    one, two = tie(turn(part[0][..., :half], part[0][..., half:]))
+    return tie((add_left(part[1], one), add_right(part[2], two)))
 
 
 def z_rest(ready, part):
-    one, two = step(*ready, "z", NZ)
+    one, two = turn(*ready)
     for k in (0, 2):
         one, two = tie((one, two))
-        one, two = step(*tie((part[k] + two, part[k + 1] + one)), "z", NZ)
+        one, two = turn(*tie((part[k] + one, part[k + 1] + two)))
     return part[4] + one + two
 
 
@@ -214,18 +221,18 @@
 
     t2_send, _ = tie((t2_amps, pair))
     t2_par = lax.ppermute(jnp.where(live, t2_send, 0.0), "x", flip(NX, 1))
-    t2_own = split(True, live_pairs, t2_amps, lax.ppermute(t2_amps, "c", swap))
 
     half = PART // 2
     fars = two[:, half:], one[:, :half]
-    pair, _ = tie((pair, (fars, t2_own)))
+    pair, _ = tie((pair, fars))
     far_down, far_up = step(*fars, "y", NY)
     blocks = (own, one, far_up, far_down, two)
     one, two = step(pair, pair, "y", NY)
-    first = chunks(block_sizes, blocks, t2_own, (), 0, NZ)
-
     fars = two[:, half:], one[:, :half]
     fars, _ = tie((fars, (far_down, far_up)))
+    t2_late, _ = tie((t2_amps, fars))
+    t2_own = split(True, live_pairs, t2_late, lax.ppermute(t2_late, "c", swap))
+    first = chunks(block_sizes, blocks, t2_own, (), 0, NZ)
     t2_par, _ = tie((t2_par, fars))
     t2_both, _ = tie(((t2_par, lax.ppermute(t2_par, "c", swap)), first))
     t2_par = split(False, live_pairs, *t2_both)

time: 110 us -> 110 us (level)
  starting transfers between devices: 44.8 us -> 51.2 us
  waiting for transfers between devices: 47.8 us -> 42.3 us
    ppermute x1 -> x17, starting transfers between devices: 0.37 us -> 27.4 us  [the longest x8 19.4 us: turn(): lax.ppermute(down, 'z', ring(NZ, -1))]
    ppermute x12 -> x4, starting transfers between devices: 24 us -> 5.95 us  [step(): lax.ppermute(other, axis, odd(n))]
    ppermute x1 -> x17, waiting for transfers between devices: 0.01 us -> 6.57 us  [the longest x8 6.47 us: turn(): lax.ppermute(up, 'z', ring(NZ, 1))]
    ppermute x12 -> x4, waiting for transfers between devices: 19.3 us -> 12.7 us  [step(): lax.ppermute(other, axis, odd(n))]
    ppermute x12 -> x4, waiting for transfers between devices: 12.3 us -> 6.21 us  [step(): lax.ppermute(value, axis, even(n))]
    ppermute x12 -> x4, starting transfers between devices: 4.81 us -> 1.47 us  [step(): lax.ppermute(value, axis, even(n))]
  transfers between devices with their start and end apart: 33 -> 33, of which waited for: 21 -> 16; matrix products, arithmetic and copies ran while one was open for 1% -> 1% of each run, Pallas kernels for 8% -> 8%
where the time goes in v6:
time: 110 us
  starting transfers between devices  51.2 us (47%)
  waiting for transfers between devices  42.3 us (38%)
  Pallas kernels  12.2 us (11%)
  local copies, waits for them, and re-layouts  2.02 us (2%)
  between operations  1.1 us (1%)
    ppermute x8, starting transfers between devices, turn(): lax.ppermute(down, 'z', ring(NZ, -1))  19.4 us
    ppermute x4, waiting for transfers between devices, step(): lax.ppermute(other, axis, odd(n))  12.7 us
    ppermute x1, waiting for transfers between devices, body(): pair = lax.ppermute(pick(near, not_p, 1), 'x', flip(NX, 1))  10.2 us
    pallas_call x3, Pallas kernels, chunks(): pl.pallas_call(functools.partial(chunk_kernel, first_k, count, len(before...  9.92 us
    ppermute x1, starting transfers between devices, body(): other = lax.ppermute(jnp.where(low_c, done[1], done[0]), 'c', swap)  6.84 us
    ppermute x8, waiting for transfers between devices, turn(): lax.ppermute(up, 'z', ring(NZ, 1))  6.47 us
    ppermute x4, waiting for transfers between devices, step(): lax.ppermute(value, axis, even(n))  6.21 us
    ppermute x4, starting transfers between devices, step(): lax.ppermute(other, axis, odd(n))  5.95 us
  transfers between devices with their start and end apart: 33, of which 16 were waited for; matrix products, arithmetic and copies ran while one was open for 1% of the time, Pallas kernels for 8%

profile of v6, /device:TPU:1, one launch (start us, length us, event | category | flops | bytes accessed | tf_op | source)
XLA Modules:
  0.0 109.6 jit_solution(2375892085923111655)
XLA Ops:
  0.0 1.6 %copy.5 = f32[512,512]{0,1:T(8,128)S(1)} copy(f32[512,512]{1,0:T(8,128)} %param.5) | data formatting | bytes 2097152 | tf_op jit(solution)/shard_map/optimization_barrier | solution.py:207
  1.7 3.3 %collective-permute-start = (f32[4,64,512]{2,1,0:T(8,128)S(1)}, f32[4,64,512]{2,1,0:T(8,128)S(1)}, u32[]{:S(2)}, u32[]{:S(2)}) collective-permute-start(f32[4,64,512]{2,1,0:T(8,128)S(1)} %get-tuple-element.124), channel_id=1, source_target_pairs={{0,1},{1,0},{2,3},{3,2},{4,5},{5,4},{6,7},{7,6},{8,9},{9,8},{10,11... | collective-permute-start | bytes 1572872 | tf_op jit(solution)/shard_map/ppermute | solution.py:217
  5.0 1.5 %collective-permute-done = f32[4,64,512]{2,1,0:T(8,128)S(1)} collective-permute-done((f32[4,64,512]{2,1,0:T(8,128)S(1)}, f32[4,64,512]{2,1,0:T(8,128)S(1)}, u32[]{:S(2)}, u32[]{:S(2)}) %collective-permute-start) | collective-permute-done | bytes 524320 | tf_op jit(solution)/shard_map/ppermute | solution.py:217
  7.6 2.2 %collective-permute-start.2 = (f32[8,32,512]{2,1,0:T(8,128)S(1)}, f32[8,32,512]{2,1,0:T(8,128)S(1)}, u32[]{:S(2)}, u32[]{:S(2)}) collective-permute-start(f32[8,32,512]{2,1,0:T(8,128)S(1)} %get-tuple-element.121.b0), channel_id=1, source_target_pairs={{0,6},{2,4},{4,2},{6,0},{1,7},{3,5},{5,3},{7,1},{8,14},{10,12},{12... | collective-permute-start | bytes 1572872 | tf_op jit(solution)/shard_map/ppermute | solution.py:108
  9.8 10.2 %collective-permute-done.1.b0 = f32[8,32,512]{2,1,0:T(8,128)S(1)} collective-permute-done((f32[8,32,512]{2,1,0:T(8,128)S(1)}, f32[8,32,512]{2,1,0:T(8,128)S(1)}, u32[]{:S(2)}, u32[]{:S(2)}) %collective-permute-start.1) | collective-permute-done | bytes 524320 | tf_op jit(solution)/shard_map/ppermute | solution.py:220
  20.5 1.5 %collective-permute-done.2.b3 = f32[8,32,512]{2,1,0:T(8,128)S(1)} collective-permute-done((f32[8,32,512]{2,1,0:T(8,128)S(1)}, f32[8,32,512]{2,1,0:T(8,128)S(1)}, u32[]{:S(2)}, u32[]{:S(2)}) %collective-permute-start.2) | collective-permute-done | bytes 524320 | tf_op jit(solution)/shard_map/ppermute | solution.py:108
  22.3 1.7 %collective-permute-start.5 = (f32[8,32,512]{2,1,0:T(8,128)S(1)}, f32[8,32,512]{2,1,0:T(8,128)S(1)}, u32[]{:S(2)}, u32[]{:S(2)}) collective-permute-start(f32[8,32,512]{2,1,0:T(8,128)S(1)} %collective-permute-done.1.b0), channel_id=1, source_target_pairs={{0,6},{2,4},{4,2},{6,0},{1,7},{3,5},{5,3},{7,1},{8,14},{10,12},{12... | collective-permute-start | bytes 1572872 | tf_op jit(solution)/shard_map/ppermute | solution.py:108
  24.0 1.5 %collective-permute-start.6 = (f32[8,16,512]{2,1,0:T(8,128)S(1)}, f32[8,16,512]{2,1,0:T(8,128)S(1)}, u32[]{:S(2)}, u32[]{:S(2)}) collective-permute-start(f32[8,16,512]{2,1,0:T(8,128)S(1)} %slice.140), channel_id=1, source_target_pairs={{0,2},{2,0},{4,6},{6,4},{1,3},{3,1},{5,7},{7,5},{8,10},{10,8},{12,... | collective-permute-start | bytes 786440 | tf_op jit(solution)/shard_map/ppermute | solution.py:108
  26.5 8.6 %collective-permute-done.5.b3 = f32[8,32,512]{2,1,0:T(8,128)S(1)} collective-permute-done((f32[8,32,512]{2,1,0:T(8,128)S(1)}, f32[8,32,512]{2,1,0:T(8,128)S(1)}, u32[]{:S(2)}, u32[]{:S(2)}) %collective-permute-start.5) | collective-permute-done | bytes 524320 | tf_op jit(solution)/shard_map/ppermute | solution.py:108
  35.6 5.6 %collective-permute-done.6.b2d = f32[8,16,512]{2,1,0:T(8,128)S(1)} collective-permute-done((f32[8,16,512]{2,1,0:T(8,128)S(1)}, f32[8,16,512]{2,1,0:T(8,128)S(1)}, u32[]{:S(2)}, u32[]{:S(2)}) %collective-permute-start.6) | collective-permute-done | bytes 262176 | tf_op jit(solution)/shard_map/ppermute | solution.py:108
  41.2 2.7 %collective-permute-start.12 = (f32[512,512]{1,0:T(8,128)S(1)}, f32[512,512]{1,0:T(8,128)S(1)}, u32[]{:S(2)}, u32[]{:S(2)}) collective-permute-start(f32[512,512]{1,0:T(8,128)S(1)} %copy-done), channel_id=1, source_target_pairs={{0,1},{1,0},{2,3},{3,2},{4,5},{5,4},{6,7},{7,6},{8,9},{9,8},{10,11... | collective-permute-start | bytes 3145736 | tf_op jit(solution)/shard_map/ppermute | solution.py:234
  43.9 1.9 %collective-permute-start.11 = (f32[512,512]{1,0:T(8,128)S(1)}, f32[512,512]{1,0:T(8,128)S(1)}, u32[]{:S(2)}, u32[]{:S(2)}) collective-permute-start(f32[512,512]{1,0:T(8,128)S(1)} %collective-permute-done.10.mine), channel_id=1, source_target_pairs={{0,1},{1,0},{2,3},{3,2},{4,5},{5,4},{6,7},{7,6},{8,9},{9,8},{10,11... | collective-permute-start | bytes 3145736 | tf_op jit(solution)/shard_map/ppermute | solution.py:237
  47.4 4.5 %shard_map.47 = (f32[8,3,32,512]{3,2,1,0:T(8,128)S(1)}, f32[8,3,32,512]{3,2,1,0:T(8,128)S(1)}) custom-call(s32[8]{0:T(128)S(1)} %copy-done.1, f32[8,32,512]{2,1,0:T(8,128)S(1)} %get-tuple-element.121.b0, f32[8,32,512]{2,1,0:T(8,128)S(1)} %collective-permute-done.3.b1, f32[8,16,512]{2,1,0:T(8,128)S(1)} %collective-permute-done.7.b2u, ...), custom_call_target="tpu_custom_call" | custom-call | flops 3221225472 | bytes 7340032 | tf_op jit(solution)/shard_map/pallas_call | solution.py:82
  52.3 2.6 %collective-permute-done.8.b2u = f32[8,16,512]{2,1,0:T(8,128)S(1)} collective-permute-done((f32[8,16,512]{2,1,0:T(8,128)S(1)}, f32[8,16,512]{2,1,0:T(8,128)S(1)}, u32[]{:S(2)}, u32[]{:S(2)}) %collective-permute-start.8) | collective-permute-done | bytes 262176 | tf_op jit(solution)/shard_map/ppermute | solution.py:108
  54.9 2.2 %shard_map.49 = (f32[3,3,32,512]{3,2,1,0:T(8,128)S(1)}, f32[3,3,32,512]{3,2,1,0:T(8,128)S(1)}) custom-call(s32[8]{0:T(128)S(1)} %copy-done.1, f32[8,32,512]{2,1,0:T(8,128)S(1)} %collective-permute-done.1.b0, f32[8,32,512]{2,1,0:T(8,128)S(1)} %collective-permute-done.4.b1, f32[8,16,512]{2,1,0:T(8,128)S(1)} %collective-permute-done.8.b2u, ...), custom_call_target="tpu_custom_call" | custom-call | flops 1207959552 | bytes 4063232 | tf_op jit(solution)/shard_map/pallas_call | solution.py:82
  58.5 4.0 %collective-permute-start.14 = (f32[3,32,256]{2,1,0:T(8,128)S(1)}, f32[3,32,256]{2,1,0:T(8,128)S(1)}, u32[]{:S(2)}, u32[]{:S(2)}) collective-permute-start(f32[3,32,256]{2,1,0:T(8,128)S(1)} %get-tuple-element.153), channel_id=1, source_target_pairs={{0,56},{8,0},{16,8},{24,16},{32,24},{40,32},{48,40},{56,48},{1,57}... | collective-permute-start | bytes 294920 | tf_op jit(solution)/shard_map/ppermute | solution.py:112
  62.6 2.7 %collective-permute-start.22 = (f32[3,32,256]{2,1,0:T(8,128)S(1)}, f32[3,32,256]{2,1,0:T(8,128)S(1)}, u32[]{:S(2)}, u32[]{:S(2)}) collective-permute-start(f32[3,32,256]{2,1,0:T(8,128)S(1)} %get-tuple-element.159), channel_id=1, source_target_pairs={{0,56},{8,0},{16,8},{24,16},{32,24},{40,32},{48,40},{56,48},{1,57}... | collective-permute-start | bytes 294920 | tf_op jit(solution)/shard_map/ppermute | solution.py:112
  65.5 2.7 %collective-permute-start.16 = (f32[3,32,512]{2,1,0:T(8,128)S(1)}, f32[3,32,512]{2,1,0:T(8,128)S(1)}, u32[]{:S(2)}, u32[]{:S(2)}) collective-permute-start(f32[3,32,512]{2,1,0:T(8,128)S(1)} %pad_maximum_fusion.1), channel_id=1, source_target_pairs={{0,56},{8,0},{16,8},{24,16},{32,24},{40,32},{48,40},{56,48},{1,57}... | collective-permute-start | bytes 589832 | tf_op jit(solution)/shard_map/ppermute | solution.py:112
  68.3 2.7 %collective-permute-start.24 = (f32[3,32,512]{2,1,0:T(8,128)S(1)}, f32[3,32,512]{2,1,0:T(8,128)S(1)}, u32[]{:S(2)}, u32[]{:S(2)}) collective-permute-start(f32[3,32,512]{2,1,0:T(8,128)S(1)} %pad_maximum_fusion.3), channel_id=1, source_target_pairs={{0,56},{8,0},{16,8},{24,16},{32,24},{40,32},{48,40},{56,48},{1,57}... | collective-permute-start | bytes 589832 | tf_op jit(solution)/shard_map/ppermute | solution.py:112
  71.0 3.2 %shard_map.50 = (f32[5,3,32,512]{3,2,1,0:T(8,128)S(1)}, f32[5,3,32,512]{3,2,1,0:T(8,128)S(1)}) custom-call(s32[8]{0:T(128)S(1)} %copy-done.1, f32[8,32,512]{2,1,0:T(8,128)S(1)} %collective-permute-done.1.b0, f32[8,32,512]{2,1,0:T(8,128)S(1)} %collective-permute-done.4.b1, f32[8,16,512]{2,1,0:T(8,128)S(1)} %collective-permute-done.8.b2u, ...), custom_call_target="tpu_custom_call" | custom-call | flops 2013265920 | bytes 5373952 | tf_op jit(solution)/shard_map/pallas_call | solution.py:82
  74.4 2.7 %collective-permute-start.18 = (f32[3,32,512]{2,1,0:T(8,128)S(1)}, f32[3,32,512]{2,1,0:T(8,128)S(1)}, u32[]{:S(2)}, u32[]{:S(2)}) collective-permute-start(f32[3,32,512]{2,1,0:T(8,128)S(1)} %get-tuple-element.96), channel_id=1, source_target_pairs={{0,56},{8,0},{16,8},{24,16},{32,24},{40,32},{48,40},{56,48},{1,57}... | collective-permute-start | bytes 589832 | tf_op jit(solution)/shard_map/ppermute | solution.py:112
  77.7 2.2 %collective-permute-start.26 = (f32[3,32,512]{2,1,0:T(8,128)S(1)}, f32[3,32,512]{2,1,0:T(8,128)S(1)}, u32[]{:S(2)}, u32[]{:S(2)}) collective-permute-start(f32[3,32,512]{2,1,0:T(8,128)S(1)} %get-tuple-element.111), channel_id=1, source_target_pairs={{0,56},{8,0},{16,8},{24,16},{32,24},{40,32},{48,40},{56,48},{1,57}... | collective-permute-start | bytes 589832 | tf_op jit(solution)/shard_map/ppermute | solution.py:112
  80.2 2.0 %collective-permute-start.19 = (f32[3,32,512]{2,1,0:T(8,128)S(1)}, f32[3,32,512]{2,1,0:T(8,128)S(1)}, u32[]{:S(2)}, u32[]{:S(2)}) collective-permute-start(f32[3,32,512]{2,1,0:T(8,128)S(1)} %get-tuple-element.99), channel_id=1, source_target_pairs={{0,8},{8,16},{16,24},{24,32},{32,40},{40,48},{48,56},{56,0},{1,9},... | collective-permute-start | bytes 589832 | tf_op jit(solution)/shard_map/ppermute | solution.py:112
  83.1 1.6 %collective-permute-done.25 = f32[3,32,512]{2,1,0:T(8,128)S(1)} collective-permute-done((f32[3,32,512]{2,1,0:T(8,128)S(1)}, f32[3,32,512]{2,1,0:T(8,128)S(1)}, u32[]{:S(2)}, u32[]{:S(2)}) %collective-permute-start.25) | collective-permute-done | bytes 196640 | tf_op jit(solution)/shard_map/ppermute | solution.py:112
  85.9 1.6 %collective-permute-start.28 = (f32[3,32,512]{2,1,0:T(8,128)S(1)}, f32[3,32,512]{2,1,0:T(8,128)S(1)}, u32[]{:S(2)}, u32[]{:S(2)}) collective-permute-start(f32[3,32,512]{2,1,0:T(8,128)S(1)} %get-tuple-element.115), channel_id=1, source_target_pairs={{0,56},{8,0},{16,8},{24,16},{32,24},{40,32},{48,40},{56,48},{1,57}... | collective-permute-start | bytes 589832 | tf_op jit(solution)/shard_map/ppermute | solution.py:112
  87.5 1.4 %collective-permute-done.19 = f32[3,32,512]{2,1,0:T(8,128)S(1)} collective-permute-done((f32[3,32,512]{2,1,0:T(8,128)S(1)}, f32[3,32,512]{2,1,0:T(8,128)S(1)}, u32[]{:S(2)}, u32[]{:S(2)}) %collective-permute-start.19) | collective-permute-done | bytes 196640 | tf_op jit(solution)/shard_map/ppermute | solution.py:112
  89.0 3.3 %collective-permute-done.27 = f32[3,32,512]{2,1,0:T(8,128)S(1)} collective-permute-done((f32[3,32,512]{2,1,0:T(8,128)S(1)}, f32[3,32,512]{2,1,0:T(8,128)S(1)}, u32[]{:S(2)}, u32[]{:S(2)}) %collective-permute-start.27) | collective-permute-done | bytes 196640 | tf_op jit(solution)/shard_map/ppermute | solution.py:112
  92.4 2.8 %collective-permute-start.29 = (f32[2,32,512]{2,1,0:T(8,128)S(1)}, f32[2,32,512]{2,1,0:T(8,128)S(1)}, u32[]{:S(2)}, u32[]{:S(2)}) collective-permute-start(f32[2,32,512]{2,1,0:T(8,128)S(1)} %pad_maximum_fusion.4), channel_id=1, source_target_pairs={{0,128},{64,192},{128,0},{192,64},{1,129},{65,193},{129,1},{193,65... | collective-permute-start | bytes 393224 | tf_op jit(solution)/shard_map/ppermute | solution.py:247
  96.3 1.5 %collective-permute-done.29 = f32[2,32,512]{2,1,0:T(8,128)S(1)} collective-permute-done((f32[2,32,512]{2,1,0:T(8,128)S(1)}, f32[2,32,512]{2,1,0:T(8,128)S(1)}, u32[]{:S(2)}, u32[]{:S(2)}) %collective-permute-start.29) | collective-permute-done | bytes 131104 | tf_op jit(solution)/shard_map/ppermute | solution.py:247
  97.8 2.5 %collective-permute-done.31 = f32[2,32,512]{2,1,0:T(8,128)S(1)} collective-permute-done((f32[2,32,512]{2,1,0:T(8,128)S(1)}, f32[2,32,512]{2,1,0:T(8,128)S(1)}, u32[]{:S(2)}, u32[]{:S(2)}) %collective-permute-start.31) | collective-permute-done | bytes 131104 | tf_op jit(solution)/shard_map/ppermute | solution.py:249
  100.4 6.8 %collective-permute-start.32 = (f32[64,512]{1,0:T(8,128)S(1)}, f32[64,512]{1,0:T(8,128)S(1)}, u32[]{:S(2)}, u32[]{:S(2)}) collective-permute-start(f32[64,512]{1,0:T(8,128)S(1)} %get-tuple-element.139), channel_id=1, source_target_pairs={{0,1},{1,0},{2,3},{3,2},{4,5},{5,4},{6,7},{7,6},{8,9},{9,8},{10,11... | collective-permute-start | bytes 393224 | tf_op jit(solution)/shard_map/ppermute | solution.py:255
  108.3 1.3 %shard_map.51 = f32[128,512]{1,0:T(8,128)} custom-call(s32[8]{0:T(128)S(1)} %copy-done.1, f32[64,512]{1,0:T(8,128)S(1)} %get-tuple-element.140.mine, f32[64,512]{1,0:T(8,128)S(1)} %collective-permute-done.32.other), custom_call_target="tpu_custom_call" | custom-call | bytes 524288 | tf_op jit(solution)/shard_map/pallas_call | solution.py:192
  (80 shorter events, 12.1 us)
Async XLA Ops:
  1.7 4.9 %collective-permute-start = (f32[4,64,512]{2,1,0:T(8,128)S(1)}, f32[4,64,512]{2,1,0:T(8,128)S(1)}, u32[]{:S(2)}, u32[]{:S(2)}) collective-permute-start(f32[4,64,512]{2,1,0:T(8,128)S(1)} %get-tuple-element.124), channel_id=1, source_target_pairs={{0,1},{1,0},{2,3},{3,2},{4,5},{5,4},{6,7},{7,6},{8,9},{9,8},{10,11... | collective-permute-start | bytes 1572872 | tf_op jit(solution)/shard_map/ppermute | solution.py:217
  6.8 13.2 %collective-permute-start.1 = (f32[8,32,512]{2,1,0:T(8,128)S(1)}, f32[8,32,512]{2,1,0:T(8,128)S(1)}, u32[]{:S(2)}, u32[]{:S(2)}) collective-permute-start(f32[8,32,512]{2,1,0:T(8,128)S(1)} %get-tuple-element.122), channel_id=1, source_target_pairs={{0,64},{64,0},{128,192},{192,128},{1,65},{65,1},{129,193},{193,129... | collective-permute-start | bytes 1572872 | tf_op jit(solution)/shard_map/ppermute | solution.py:220
  7.6 14.4 %collective-permute-start.2 = (f32[8,32,512]{2,1,0:T(8,128)S(1)}, f32[8,32,512]{2,1,0:T(8,128)S(1)}, u32[]{:S(2)}, u32[]{:S(2)}) collective-permute-start(f32[8,32,512]{2,1,0:T(8,128)S(1)} %get-tuple-element.121.b0), channel_id=1, source_target_pairs={{0,6},{2,4},{4,2},{6,0},{1,7},{3,5},{5,3},{7,1},{8,14},{10,12},{12... | collective-permute-start | bytes 1572872 | tf_op jit(solution)/shard_map/ppermute | solution.py:108
  9.8 12.5 %collective-permute-start.3 = (f32[8,32,512]{2,1,0:T(8,128)S(1)}, f32[8,32,512]{2,1,0:T(8,128)S(1)}, u32[]{:S(2)}, u32[]{:S(2)}) collective-permute-start(f32[8,32,512]{2,1,0:T(8,128)S(1)} %get-tuple-element.121.b0), channel_id=1, source_target_pairs={{0,2},{2,0},{4,6},{6,4},{1,3},{3,1},{5,7},{7,5},{8,10},{10,8},{12,... | collective-permute-start | bytes 1572872 | tf_op jit(solution)/shard_map/ppermute | solution.py:108
  20.1 23.8 %collective-permute-start.10 = (f32[512,512]{1,0:T(8,128)S(1)}, f32[512,512]{1,0:T(8,128)S(1)}, u32[]{:S(2)}, u32[]{:S(2)}) collective-permute-start(f32[512,512]{1,0:T(8,128)S(1)} %broadcast_select_fusion), channel_id=1, source_target_pairs={{0,64},{64,0},{128,192},{192,128},{1,65},{65,1},{129,193},{193,129... | collective-permute-start | bytes 3145736 | tf_op jit(solution)/shard_map/ppermute | solution.py:223
  22.3 12.9 %collective-permute-start.5 = (f32[8,32,512]{2,1,0:T(8,128)S(1)}, f32[8,32,512]{2,1,0:T(8,128)S(1)}, u32[]{:S(2)}, u32[]{:S(2)}) collective-permute-start(f32[8,32,512]{2,1,0:T(8,128)S(1)} %collective-permute-done.1.b0), channel_id=1, source_target_pairs={{0,6},{2,4},{4,2},{6,0},{1,7},{3,5},{5,3},{7,1},{8,14},{10,12},{12... | collective-permute-start | bytes 1572872 | tf_op jit(solution)/shard_map/ppermute | solution.py:108
  24.0 11.6 %collective-permute-start.4 = (f32[8,32,512]{2,1,0:T(8,128)S(1)}, f32[8,32,512]{2,1,0:T(8,128)S(1)}, u32[]{:S(2)}, u32[]{:S(2)}) collective-permute-start(f32[8,32,512]{2,1,0:T(8,128)S(1)} %collective-permute-done.1.b0), channel_id=1, source_target_pairs={{0,2},{2,0},{4,6},{6,4},{1,3},{3,1},{5,7},{7,5},{8,10},{10,8},{12,... | collective-permute-start | bytes 1572872 | tf_op jit(solution)/shard_map/ppermute | solution.py:108
  24.0 17.2 %collective-permute-start.6 = (f32[8,16,512]{2,1,0:T(8,128)S(1)}, f32[8,16,512]{2,1,0:T(8,128)S(1)}, u32[]{:S(2)}, u32[]{:S(2)}) collective-permute-start(f32[8,16,512]{2,1,0:T(8,128)S(1)} %slice.140), channel_id=1, source_target_pairs={{0,2},{2,0},{4,6},{6,4},{1,3},{3,1},{5,7},{7,5},{8,10},{10,8},{12,... | collective-permute-start | bytes 786440 | tf_op jit(solution)/shard_map/ppermute | solution.py:108
  25.4 15.8 %collective-permute-start.7 = (f32[8,16,512]{2,1,0:T(8,128)S(1)}, f32[8,16,512]{2,1,0:T(8,128)S(1)}, u32[]{:S(2)}, u32[]{:S(2)}) collective-permute-start(f32[8,16,512]{2,1,0:T(8,128)S(1)} %slice.141), channel_id=1, source_target_pairs={{0,6},{2,4},{4,2},{6,0},{1,7},{3,5},{5,3},{7,1},{8,14},{10,12},{12... | collective-permute-start | bytes 786440 | tf_op jit(solution)/shard_map/ppermute | solution.py:108
  41.2 5.6 %collective-permute-start.12 = (f32[512,512]{1,0:T(8,128)S(1)}, f32[512,512]{1,0:T(8,128)S(1)}, u32[]{:S(2)}, u32[]{:S(2)}) collective-permute-start(f32[512,512]{1,0:T(8,128)S(1)} %copy-done), channel_id=1, source_target_pairs={{0,1},{1,0},{2,3},{3,2},{4,5},{5,4},{6,7},{7,6},{8,9},{9,8},{10,11... | collective-permute-start | bytes 3145736 | tf_op jit(solution)/shard_map/ppermute | solution.py:234
  43.9 8.0 %collective-permute-start.11 = (f32[512,512]{1,0:T(8,128)S(1)}, f32[512,512]{1,0:T(8,128)S(1)}, u32[]{:S(2)}, u32[]{:S(2)}) collective-permute-start(f32[512,512]{1,0:T(8,128)S(1)} %collective-permute-done.10.mine), channel_id=1, source_target_pairs={{0,1},{1,0},{2,3},{3,2},{4,5},{5,4},{6,7},{7,6},{8,9},{9,8},{10,11... | collective-permute-start | bytes 3145736 | tf_op jit(solution)/shard_map/ppermute | solution.py:237
  45.8 9.1 %collective-permute-start.8 = (f32[8,16,512]{2,1,0:T(8,128)S(1)}, f32[8,16,512]{2,1,0:T(8,128)S(1)}, u32[]{:S(2)}, u32[]{:S(2)}) collective-permute-start(f32[8,16,512]{2,1,0:T(8,128)S(1)} %slice.143), channel_id=1, source_target_pairs={{0,6},{2,4},{4,2},{6,0},{1,7},{3,5},{5,3},{7,1},{8,14},{10,12},{12... | collective-permute-start | bytes 786440 | tf_op jit(solution)/shard_map/ppermute | solution.py:108
  46.8 8.2 %collective-permute-start.9 = (f32[8,16,512]{2,1,0:T(8,128)S(1)}, f32[8,16,512]{2,1,0:T(8,128)S(1)}, u32[]{:S(2)}, u32[]{:S(2)}) collective-permute-start(f32[8,16,512]{2,1,0:T(8,128)S(1)} %slice.142), channel_id=1, source_target_pairs={{0,2},{2,0},{4,6},{6,4},{1,3},{3,1},{5,7},{7,5},{8,10},{10,8},{12,... | collective-permute-start | bytes 786440 | tf_op jit(solution)/shard_map/ppermute | solution.py:108
  57.3 8.0 %collective-permute-start.13 = (f32[3,32,256]{2,1,0:T(8,128)S(1)}, f32[3,32,256]{2,1,0:T(8,128)S(1)}, u32[]{:S(2)}, u32[]{:S(2)}) collective-permute-start(f32[3,32,256]{2,1,0:T(8,128)S(1)} %get-tuple-element.154), channel_id=1, source_target_pairs={{0,8},{8,16},{16,24},{24,32},{32,40},{40,48},{48,56},{56,0},{1,9},... | collective-permute-start | bytes 294920 | tf_op jit(solution)/shard_map/ppermute | solution.py:112
  58.5 6.8 %collective-permute-start.14 = (f32[3,32,256]{2,1,0:T(8,128)S(1)}, f32[3,32,256]{2,1,0:T(8,128)S(1)}, u32[]{:S(2)}, u32[]{:S(2)}) collective-permute-start(f32[3,32,256]{2,1,0:T(8,128)S(1)} %get-tuple-element.153), channel_id=1, source_target_pairs={{0,56},{8,0},{16,8},{24,16},{32,24},{40,32},{48,40},{56,48},{1,57}... | collective-permute-start | bytes 294920 | tf_op jit(solution)/shard_map/ppermute | solution.py:112
  62.5 5.6 %collective-permute-start.21 = (f32[3,32,256]{2,1,0:T(8,128)S(1)}, f32[3,32,256]{2,1,0:T(8,128)S(1)}, u32[]{:S(2)}, u32[]{:S(2)}) collective-permute-start(f32[3,32,256]{2,1,0:T(8,128)S(1)} %get-tuple-element.160), channel_id=1, source_target_pairs={{0,8},{8,16},{16,24},{24,32},{32,40},{40,48},{48,56},{56,0},{1,9},... | collective-permute-start | bytes 294920 | tf_op jit(solution)/shard_map/ppermute | solution.py:112
  62.6 5.5 %collective-permute-start.22 = (f32[3,32,256]{2,1,0:T(8,128)S(1)}, f32[3,32,256]{2,1,0:T(8,128)S(1)}, u32[]{:S(2)}, u32[]{:S(2)}) collective-permute-start(f32[3,32,256]{2,1,0:T(8,128)S(1)} %get-tuple-element.159), channel_id=1, source_target_pairs={{0,56},{8,0},{16,8},{24,16},{32,24},{40,32},{48,40},{56,48},{1,57}... | collective-permute-start | bytes 294920 | tf_op jit(solution)/shard_map/ppermute | solution.py:112
  65.4 8.8 %collective-permute-start.15 = (f32[3,32,512]{2,1,0:T(8,128)S(1)}, f32[3,32,512]{2,1,0:T(8,128)S(1)}, u32[]{:S(2)}, u32[]{:S(2)}) collective-permute-start(f32[3,32,512]{2,1,0:T(8,128)S(1)} %pad_maximum_fusion), channel_id=1, source_target_pairs={{0,8},{8,16},{16,24},{24,32},{32,40},{40,48},{48,56},{56,0},{1,9},... | collective-permute-start | bytes 589832 | tf_op jit(solution)/shard_map/ppermute | solution.py:112
  65.5 8.8 %collective-permute-start.16 = (f32[3,32,512]{2,1,0:T(8,128)S(1)}, f32[3,32,512]{2,1,0:T(8,128)S(1)}, u32[]{:S(2)}, u32[]{:S(2)}) collective-permute-start(f32[3,32,512]{2,1,0:T(8,128)S(1)} %pad_maximum_fusion.1), channel_id=1, source_target_pairs={{0,56},{8,0},{16,8},{24,16},{32,24},{40,32},{48,40},{56,48},{1,57}... | collective-permute-start | bytes 589832 | tf_op jit(solution)/shard_map/ppermute | solution.py:112
  68.2 8.8 %collective-permute-start.23 = (f32[3,32,512]{2,1,0:T(8,128)S(1)}, f32[3,32,512]{2,1,0:T(8,128)S(1)}, u32[]{:S(2)}, u32[]{:S(2)}) collective-permute-start(f32[3,32,512]{2,1,0:T(8,128)S(1)} %pad_maximum_fusion.2), channel_id=1, source_target_pairs={{0,8},{8,16},{16,24},{24,32},{32,40},{40,48},{48,56},{56,0},{1,9},... | collective-permute-start | bytes 589832 | tf_op jit(solution)/shard_map/ppermute | solution.py:112
  68.3 8.7 %collective-permute-start.24 = (f32[3,32,512]{2,1,0:T(8,128)S(1)}, f32[3,32,512]{2,1,0:T(8,128)S(1)}, u32[]{:S(2)}, u32[]{:S(2)}) collective-permute-start(f32[3,32,512]{2,1,0:T(8,128)S(1)} %pad_maximum_fusion.3), channel_id=1, source_target_pairs={{0,56},{8,0},{16,8},{24,16},{32,24},{40,32},{48,40},{56,48},{1,57}... | collective-permute-start | bytes 589832 | tf_op jit(solution)/shard_map/ppermute | solution.py:112
  74.3 5.8 %collective-permute-start.17 = (f32[3,32,512]{2,1,0:T(8,128)S(1)}, f32[3,32,512]{2,1,0:T(8,128)S(1)}, u32[]{:S(2)}, u32[]{:S(2)}) collective-permute-start(f32[3,32,512]{2,1,0:T(8,128)S(1)} %get-tuple-element.95), channel_id=1, source_target_pairs={{0,8},{8,16},{16,24},{24,32},{32,40},{40,48},{48,56},{56,0},{1,9},... | collective-permute-start | bytes 589832 | tf_op jit(solution)/shard_map/ppermute | solution.py:112
  74.4 5.7 %collective-permute-start.18 = (f32[3,32,512]{2,1,0:T(8,128)S(1)}, f32[3,32,512]{2,1,0:T(8,128)S(1)}, u32[]{:S(2)}, u32[]{:S(2)}) collective-permute-start(f32[3,32,512]{2,1,0:T(8,128)S(1)} %get-tuple-element.96), channel_id=1, source_target_pairs={{0,56},{8,0},{16,8},{24,16},{32,24},{40,32},{48,40},{56,48},{1,57}... | collective-permute-start | bytes 589832 | tf_op jit(solution)/shard_map/ppermute | solution.py:112
  77.1 7.6 %collective-permute-start.25 = (f32[3,32,512]{2,1,0:T(8,128)S(1)}, f32[3,32,512]{2,1,0:T(8,128)S(1)}, u32[]{:S(2)}, u32[]{:S(2)}) collective-permute-start(f32[3,32,512]{2,1,0:T(8,128)S(1)} %get-tuple-element.110), channel_id=1, source_target_pairs={{0,8},{8,16},{16,24},{24,32},{32,40},{40,48},{48,56},{56,0},{1,9},... | collective-permute-start | bytes 589832 | tf_op jit(solution)/shard_map/ppermute | solution.py:112
  77.7 7.0 %collective-permute-start.26 = (f32[3,32,512]{2,1,0:T(8,128)S(1)}, f32[3,32,512]{2,1,0:T(8,128)S(1)}, u32[]{:S(2)}, u32[]{:S(2)}) collective-permute-start(f32[3,32,512]{2,1,0:T(8,128)S(1)} %get-tuple-element.111), channel_id=1, source_target_pairs={{0,56},{8,0},{16,8},{24,16},{32,24},{40,32},{48,40},{56,48},{1,57}... | collective-permute-start | bytes 589832 | tf_op jit(solution)/shard_map/ppermute | solution.py:112
  80.2 8.7 %collective-permute-start.19 = (f32[3,32,512]{2,1,0:T(8,128)S(1)}, f32[3,32,512]{2,1,0:T(8,128)S(1)}, u32[]{:S(2)}, u32[]{:S(2)}) collective-permute-start(f32[3,32,512]{2,1,0:T(8,128)S(1)} %get-tuple-element.99), channel_id=1, source_target_pairs={{0,8},{8,16},{16,24},{24,32},{32,40},{40,48},{48,56},{56,0},{1,9},... | collective-permute-start | bytes 589832 | tf_op jit(solution)/shard_map/ppermute | solution.py:112
  82.1 6.8 %collective-permute-start.20 = (f32[3,32,512]{2,1,0:T(8,128)S(1)}, f32[3,32,512]{2,1,0:T(8,128)S(1)}, u32[]{:S(2)}, u32[]{:S(2)}) collective-permute-start(f32[3,32,512]{2,1,0:T(8,128)S(1)} %get-tuple-element.100), channel_id=1, source_target_pairs={{0,56},{8,0},{16,8},{24,16},{32,24},{40,32},{48,40},{56,48},{1,57}... | collective-permute-start | bytes 589832 | tf_op jit(solution)/shard_map/ppermute | solution.py:112
  84.7 7.6 %collective-permute-start.27 = (f32[3,32,512]{2,1,0:T(8,128)S(1)}, f32[3,32,512]{2,1,0:T(8,128)S(1)}, u32[]{:S(2)}, u32[]{:S(2)}) collective-permute-start(f32[3,32,512]{2,1,0:T(8,128)S(1)} %get-tuple-element.114), channel_id=1, source_target_pairs={{0,8},{8,16},{16,24},{24,32},{32,40},{40,48},{48,56},{56,0},{1,9},... | collective-permute-start | bytes 589832 | tf_op jit(solution)/shard_map/ppermute | solution.py:112
  85.9 6.4 %collective-permute-start.28 = (f32[3,32,512]{2,1,0:T(8,128)S(1)}, f32[3,32,512]{2,1,0:T(8,128)S(1)}, u32[]{:S(2)}, u32[]{:S(2)}) collective-permute-start(f32[3,32,512]{2,1,0:T(8,128)S(1)} %get-tuple-element.115), channel_id=1, source_target_pairs={{0,56},{8,0},{16,8},{24,16},{32,24},{40,32},{48,40},{56,48},{1,57}... | collective-permute-start | bytes 589832 | tf_op jit(solution)/shard_map/ppermute | solution.py:112
  92.4 5.4 %collective-permute-start.29 = (f32[2,32,512]{2,1,0:T(8,128)S(1)}, f32[2,32,512]{2,1,0:T(8,128)S(1)}, u32[]{:S(2)}, u32[]{:S(2)}) collective-permute-start(f32[2,32,512]{2,1,0:T(8,128)S(1)} %pad_maximum_fusion.4), channel_id=1, source_target_pairs={{0,128},{64,192},{128,0},{192,64},{1,129},{65,193},{129,1},{193,65... | collective-permute-start | bytes 393224 | tf_op jit(solution)/shard_map/ppermute | solution.py:247
  95.2 5.1 %collective-permute-start.31 = (f32[2,32,512]{2,1,0:T(8,128)S(1)}, f32[2,32,512]{2,1,0:T(8,128)S(1)}, u32[]{:S(2)}, u32[]{:S(2)}) collective-permute-start(f32[2,32,512]{2,1,0:T(8,128)S(1)} %pad_maximum_fusion.6), channel_id=1, source_target_pairs={{0,192},{64,128},{128,64},{192,0},{1,193},{65,129},{129,65},{193,1... | collective-permute-start | bytes 393224 | tf_op jit(solution)/shard_map/ppermute | solution.py:249
  100.4 7.8 %collective-permute-start.32 = (f32[64,512]{1,0:T(8,128)S(1)}, f32[64,512]{1,0:T(8,128)S(1)}, u32[]{:S(2)}, u32[]{:S(2)}) collective-permute-start(f32[64,512]{1,0:T(8,128)S(1)} %get-tuple-element.139), channel_id=1, source_target_pairs={{0,1},{1,0},{2,3},{3,2},{4,5},{5,4},{6,7},{7,6},{8,9},{9,8},{10,11... | collective-permute-start | bytes 393224 | tf_op jit(solution)/shard_map/ppermute | solution.py:255
  (3 other events, 42.6 us)
